TPU v7x, 512 devices: a whole 4x4x16 slice. The times are simulated.
512 devices in a mesh: dp: 32 (over x_hi, z), space: 16 (over x_lo, y, core).
Axes of the slice: x: 4 (x_hi: 2, x_lo: 2; x = x_hi * 2 + x_lo), y: 4, z: 16, core: 2. Of those that a mesh axis runs over, the one named last changes fastest.
Arguments:
- volume: bfloat16 [32, 96, 32, 2, 256], P('dp', None, 'space'), may hold values from -6 to 6
- first_weight: bfloat16 [27, 4, 24, 24], replicated, may hold values from -0.25 to 0.25
- second_weight: bfloat16 [27, 96, 192], replicated, may hold values from -0.125 to 0.125
- out_cotangent: bfloat16 [32, 192, 16, 1, 128], P('dp', None, 'space'), may hold values from -6 to 6
Outputs:
- features: bfloat16 [32, 192, 16, 1, 128], P('dp', None, 'space')
- volume_grad: bfloat16 [32, 96, 32, 2, 256], P('dp', None, 'space')
- first_grad: float32 [27, 4, 24, 24], replicated
- second_grad: float32 [27, 96, 192], replicated
All inputs are finite; a program needn't handle non-finite values.
Results may differ from a plain program's by a relative error of at most 0.0049.
Values may be sent and summed in bfloat16 or wider, within the bound.
No kernel may reach another device: no remote copies, remote signals or barrier semaphores. Data moves between devices by JAX's collectives and lax.ppermute only.
A program may use at most 64 MiB of HBM per device.

v0:
```python
import math

import jax
import jax.numpy as jnp
from jax import lax
from jax.sharding import PartitionSpec as P

offsets = [(off_x, off_y, off_z) for off_x in range(3) for off_y in range(3) for off_z in range(3)]
parity_of = {0: (1, -1), 1: (0, 0), 2: (1, 0)}


def padded_2(block, sides, width):
    for axis, dim in sides:
        count = lax.axis_size(axis)
        forward = [(i, i + 1) for i in range(count - 1)]
        backward = [(target, source) for source, target in forward]
        low = lax.ppermute(
            lax.slice_in_dim(block, block.shape[dim] - width, None, axis=dim), axis, forward
        )
        high = lax.ppermute(lax.slice_in_dim(block, 0, width, axis=dim), axis, backward)
        block = jnp.concatenate([low, block, high], axis=dim)
    return block


def shifted_2(array, axis, by):
    size = lax.axis_size(axis)
    pairs = [(i, i + by) for i in range(size) if 0 <= i + by < size]
    return lax.ppermute(array, axis, pairs)


def silu_slope(values):
    sigma = jax.nn.sigmoid(values)
    return sigma * (1.0 + values * (1.0 - sigma))


def edge_mask(length, cells_z, towards, dtype):
    column = lax.iota(jnp.int32, length) % cells_z
    if towards < 0:
        keep = column >= 1
    else:
        keep = column <= cells_z - 2
    return keep.astype(dtype)


def shifted(field, offset_flat, cells_z, towards, reach):
    length = field.shape[-1]
    last = field.ndim - 1
    widths = [(0, 0)] * last + [(reach, reach)]
    padded = jnp.pad(field, widths)
    window = lax.slice_in_dim(padded, reach + offset_flat, reach + offset_flat + length, axis=last)
    if towards != 0:
        window = window * edge_mask(length, cells_z, towards, field.dtype)
    return window


def unsplit(parts, count, channels, half_y, half_z):
    rows = []
    for bit_y in (0, 1):
        rows.append(
            jnp.stack(
                [
                    parts[bit_y, 0].reshape(count, channels, half_y, half_z),
                    parts[bit_y, 1].reshape(count, channels, half_y, half_z),
                ],
                axis=4,
            )
        )
    merged = jnp.stack(rows, axis=3)
    return merged.reshape(count, channels, 4 * half_y * half_z)


def spread_parts(weight, cotangent, tap_count, half_z):
    width_flat = cotangent.shape[-1]
    spreads = jnp.einsum("tco,qon->tqcn", weight, cotangent, preferred_element_type=jnp.float32)
    buckets = {}
    for tap_index in range(tap_count):
        off_x, off_y, off_z = offsets[tap_index]
        bit_y, move_y = parity_of[off_y]
        bit_z, move_z = parity_of[off_z]
        values = spreads[tap_index]
        if move_z < 0:
            values = values * edge_mask(width_flat, half_z, -1, jnp.float32)
        distance = -(move_y * half_z + move_z)
        values = jnp.pad(values, ((0, 0), (0, 0), (0, distance)))[
            :, :, distance : distance + width_flat
        ]
        key = (off_x % 2, off_x // 2, bit_y, bit_z)
        buckets[key] = buckets[key] + values if key in buckets else values
    return buckets


def shards(volume, first_weight, second_weight, out_cotangent):
    channels, planes, cells_y, cells_z = (
        volume.shape[1],
        volume.shape[2],
        volume.shape[3],
        volume.shape[4],
    )
    groups = first_weight.shape[1]
    per_group = channels // groups
    out_channels = second_weight.shape[2]
    half_x, half_y, half_z = (planes // 2, cells_y // 2, cells_z // 2)
    flat_len = cells_y * cells_z
    half_len = half_y * half_z
    cotangent = out_cotangent[0].transpose(1, 0, 2, 3).reshape(half_x, out_channels, half_len)
    flat_in = volume[0].transpose(1, 0, 2, 3).reshape(planes, channels, flat_len)
    extended = padded_2(flat_in, (("space", 0),), 1)
    stacked = jnp.stack(
        [
            shifted(extended, (off_y - 1) * cells_z + (off_z - 1), cells_z, off_z - 1, cells_z + 1)
            for off_y in range(3)
            for off_z in range(3)
        ]
    )
    stacked = stacked.reshape(9, planes + 2, groups, per_group, flat_len)
    kernel = first_weight.reshape(3, 9, groups, per_group, per_group)
    pre = None
    for off_x in range(3):
        term = jnp.einsum(
            "kgio,kqgin->qgon",
            kernel[off_x],
            stacked[:, off_x : off_x + planes],
            preferred_element_type=jnp.float32,
        )
        pre = term if pre is None else pre + term
    pre = pre.reshape(planes, channels, flat_len)
    hidden = jax.nn.silu(pre).astype(jnp.bfloat16)
    below = shifted_2(hidden[planes - 1 : planes], "space", 1)
    joined = jnp.concatenate([below, hidden], axis=0)
    split6 = joined.reshape(planes + 1, channels, half_y, 2, half_z, 2)
    parity = {}
    for bit_y in (0, 1):
        for bit_z in (0, 1):
            parity[bit_y, bit_z] = split6[:, :, :, bit_y, :, bit_z].reshape(
                planes + 1, channels, half_len
            )
    windows = []
    for off_x, off_y, off_z in offsets:
        bit_y, move_y = parity_of[off_y]
        bit_z, move_z = parity_of[off_z]
        window = shifted(parity[bit_y, bit_z], move_y * half_z + move_z, half_z, move_z, half_z + 1)
        windows.append(lax.slice_in_dim(window, off_x, off_x + planes - 1, stride=2, axis=0))
    windows = jnp.stack(windows)
    summed = jnp.einsum("tco,tqcn->qon", second_weight, windows, preferred_element_type=jnp.float32)
    features = (
        summed.astype(jnp.bfloat16)
        .reshape(half_x, out_channels, half_y, half_z)
        .transpose(1, 0, 2, 3)
    )
    second_grad = jnp.einsum(
        "tqcn,qon->tco", windows, cotangent, preferred_element_type=jnp.float32
    )
    buckets = spread_parts(second_weight, cotangent, 27, half_z)
    even_parts = {}
    odd_parts = {}
    for bit_y in (0, 1):
        for bit_z in (0, 1):
            near = jnp.pad(buckets[0, 0, bit_y, bit_z], ((0, 1), (0, 0), (0, 0)))
            far = jnp.pad(buckets[0, 1, bit_y, bit_z], ((1, 0), (0, 0), (0, 0)))
            even_parts[bit_y, bit_z] = near + far
            odd_parts[bit_y, bit_z] = buckets[1, 0, bit_y, bit_z]
    even_full = unsplit(even_parts, half_x + 1, channels, half_y, half_z)
    odd_full = unsplit(odd_parts, half_x, channels, half_y, half_z)
    hidden_grad = jnp.stack([odd_full, even_full[1:]], axis=1).reshape(planes, channels, flat_len)
    returned = shifted_2(even_full[0:1], "space", -1)
    hidden_grad = jnp.concatenate(
        [hidden_grad[: planes - 1], hidden_grad[planes - 1 :] + returned], axis=0
    )
    pre_grad = (hidden_grad * silu_slope(pre)).astype(jnp.bfloat16)
    grad_ext = padded_2(pre_grad, (("space", 0),), 1)
    grad_stack = jnp.stack(
        [
            shifted(grad_ext, (1 - off_y) * cells_z + (1 - off_z), cells_z, 1 - off_z, cells_z + 1)
            for off_y in range(3)
            for off_z in range(3)
        ]
    )
    grad_stack = grad_stack.reshape(9, planes + 2, groups, per_group, flat_len)
    centre = pre_grad.reshape(planes, groups, per_group, flat_len)
    back = None
    tap_grads = []
    for off_x in range(3):
        term = jnp.einsum(
            "kgio,kqgon->qgin",
            kernel[off_x],
            grad_stack[:, 2 - off_x : 2 - off_x + planes],
            preferred_element_type=jnp.float32,
        )
        back = term if back is None else back + term
        tap_grads.append(
            jnp.einsum(
                "kqgin,qgon->kgio",
                stacked[:, off_x : off_x + planes],
                centre,
                preferred_element_type=jnp.float32,
            )
        )
    first_grad = jnp.stack(tap_grads).reshape(first_weight.shape)
    volume_grad = back.reshape(planes, channels, flat_len).astype(jnp.bfloat16)
    volume_grad = volume_grad.reshape(planes, channels, cells_y, cells_z).transpose(1, 0, 2, 3)
    first_grad, second_grad = lax.psum((first_grad, second_grad), ("dp", "space"))
    factor = 1.0 / math.sqrt(
        lax.axis_size("dp") * lax.axis_size("space") * half_x * half_y * half_z
    )
    return (features[None], volume_grad[None], first_grad * factor, second_grad * factor)


def solution(mesh):
    in_specs = (P("dp", None, "space", None, None), P(), P(), P("dp", None, "space", None, None))
    out_specs = (P("dp", None, "space", None, None), P("dp", None, "space", None, None), P(), P())
    return jax.shard_map(shards, mesh=mesh, in_specs=in_specs, out_specs=out_specs, check_vma=False)
```

profile of v0, /device:TPU:1, one launch (start us, length us, event | category | flops | bytes accessed | tf_op | source)
XLA Modules:
  0.0 590.7 jit_solution(12952221345959561960)
XLA Ops:
  9.1 8.8 %collective-permute-start.1 = (bf16[1,96,512]{2,1,0:T(8,128)(2,1)}, bf16[1,96,512]{2,1,0:T(8,128)(2,1)}, u32[]{:S(2)}, u32[]{:S(2)}) collective-permute-start(bf16[1,96,512]{2,1,0:T(8,128)(2,1)} %slice.362), channel_id=1, source_target_pairs={{1,0},{2,1},{3,2},{4,3},{5,4},{6,5},{7,6},{8,7},{9,8},{10,9},{11,1... | collective-permute-start | bytes 294920 | tf_op jit(solution)/shard_map/ppermute | solution.py:20
  18.6 1.9 collective-permute-start
  20.6 1.3 fusion.97
  23.9 3.0 collective-permute-start.3
  36.2 2.4 copy.162
  40.0 1.3 fusion.52
  45.6 1.5 fusion.16
  47.1 1.5 fusion.19
  48.6 1.5 fusion.13
  51.0 2.5 collective-permute-start.2
  54.3 1.9 collective-permute-start.4
  56.2 2.6 collective-permute-start.5
  58.9 1.5 copy.132
  79.1 3.1 fusion.53
  83.2 1.8 fusion.61
  85.8 1.8 constant_dynamic-update-slice_fusion.34
  87.6 1.8 constant_dynamic-update-slice_fusion.33
  89.4 1.8 constant_dynamic-update-slice_fusion.32
  95.1 3.2 fusion.106
  100.6 2.3 fusion.47
  102.9 474.2 %all-reduce.21.cloned.1.call-done = (f32[27,4,24,24]{3,2,1,0:T(8,128)}, f32[27,96,192]{2,1,0:T(8,128)}) async-done(((f32[27,4,24,24]{3,2,1,0:T(8,128)}, f32[27,96,192]{2,1,0:T(8,128)}), (f32[27,4,24,24]{3,2,1,0:T(8,128)}, f32[27,96,192]{2,1,0:T(8,128)})) %all-reduce.21.cloned.1.call-update) | async-done | bytes 2239504 | tf_op jit(solution)/shard_map/psum | solution.py:201
  577.0 1.4 broadcast_multiply_fusion.1
  578.4 1.9 copy.134
  580.4 3.5 broadcast_multiply_fusion
  (145 shorter events, 47.6 us)
Async XLA Ops:
  7.2 13.4 %copy-start = (bf16[27,96,192]{2,1,0:T(8,128)(2,1)S(1)}, bf16[27,96,192]{2,1,0:T(8,128)(2,1)}, u32[]{:S(2)}) copy-start(bf16[27,96,192]{2,1,0:T(8,128)(2,1)} %param.6) | copy-start | bytes 2985988
  7.2 569.8 %all-reduce.21.cloned.1.call-start = ((), (), s32[]{:S(2)}) async-start(), calls=%async_computation | async-start | bytes 7962624 | tf_op jit(solution)/shard_map/psum | solution.py:201
  9.1 30.9 %collective-permute-start.1 = (bf16[1,96,512]{2,1,0:T(8,128)(2,1)}, bf16[1,96,512]{2,1,0:T(8,128)(2,1)}, u32[]{:S(2)}, u32[]{:S(2)}) collective-permute-start(bf16[1,96,512]{2,1,0:T(8,128)(2,1)} %slice.362), channel_id=1, source_target_pairs={{1,0},{2,1},{3,2},{4,3},{5,4},{6,5},{7,6},{8,7},{9,8},{10,9},{11,1... | collective-permute-start | bytes 294920 | tf_op jit(solution)/shard_map/ppermute | solution.py:20
  18.6 21.4 %collective-permute-start = (bf16[1,96,512]{2,1,0:T(8,128)(2,1)}, bf16[1,96,512]{2,1,0:T(8,128)(2,1)}, u32[]{:S(2)}, u32[]{:S(2)}) collective-permute-start(bf16[1,96,512]{2,1,0:T(8,128)(2,1)} %slice.360), channel_id=1, source_target_pairs={{0,1},{1,2},{2,3},{3,4},{4,5},{5,6},{6,7},{7,8},{8,9},{9,10},{10,1... | collective-permute-start | bytes 294920 | tf_op jit(solution)/shard_map/ppermute | solution.py:17
  20.5 6.4 %copy-start.2 = (bf16[1,96,2,2,256]{4,3,2,1,0:T(2,128)(2,1)S(1)}, bf16[1,96,2,2,256]{4,3,2,1,0:T(2,128)(2,1)}, u32[]{:S(2)}) copy-start(bf16[1,96,2,2,256]{4,3,2,1,0:T(2,128)(2,1)} %param.4) | copy-start | bytes 589828
  23.1 11.9 %copy-start.1 = (bf16[27,4,24,24]{0,3,2,1:T(8,128)(2,1)S(1)}, bf16[27,4,24,24]{0,3,2,1:T(8,128)(2,1)}, u32[]{:S(2)}) copy-start(bf16[27,4,24,24]{0,3,2,1:T(8,128)(2,1)} %param.5) | copy-start | bytes 373252
  23.9 20.3 %collective-permute-start.3 = (f32[1,96,512]{2,1,0:T(8,128)}, f32[1,96,512]{2,1,0:T(8,128)}, u32[]{:S(2)}, u32[]{:S(2)}) collective-permute-start(f32[1,96,512]{2,1,0:T(8,128)} %copy.111), channel_id=1, source_target_pairs={{1,0},{2,1},{3,2},{4,3},{5,4},{6,5},{7,6},{8,7},{9,8},{10,9},{11,1... | collective-permute-start | bytes 589832 | tf_op jit(solution)/shard_map/ppermute | solution.py:28
  33.9 6.1 %copy-start.6 = (bf16[2,96,512]{2,1,0:T(8,128)(2,1)S(1)}, bf16[2,96,512]{2,1,0:T(8,128)(2,1)}, u32[]{:S(2)}) copy-start(bf16[2,96,512]{2,1,0:T(8,128)(2,1)} %copy.152) | copy-start | bytes 589828
  40.0 3.4 copy-start.3
  41.3 0.9 copy-start.8
  43.3 0.9 copy-start.7
  43.4 1.8 copy-start.9
  43.4 1.8 copy-start.11
  47.1 3.0 copy-start.5
  51.0 9.4 %collective-permute-start.2 = (bf16[1,96,512]{2,1,0:T(8,128)(2,1)}, bf16[1,96,512]{2,1,0:T(8,128)(2,1)}, u32[]{:S(2)}, u32[]{:S(2)}) collective-permute-start(bf16[1,96,512]{2,1,0:T(8,128)(2,1)} %slice.452), channel_id=1, source_target_pairs={{0,1},{1,2},{2,3},{3,4},{4,5},{5,6},{6,7},{7,8},{8,9},{9,10},{10,1... | collective-permute-start | bytes 294920 | tf_op jit(solution)/shard_map/ppermute | solution.py:28
  54.3 28.0 %collective-permute-start.4 = (bf16[1,96,512]{2,1,0:T(8,128)(2,1)}, bf16[1,96,512]{2,1,0:T(8,128)(2,1)S(1)}, u32[]{:S(2)}, u32[]{:S(2)}) collective-permute-start(bf16[1,96,512]{2,1,0:T(8,128)(2,1)} %get-tuple-element.73), channel_id=1, source_target_pairs={{0,1},{1,2},{2,3},{3,4},{4,5},{5,6},{6,7},{7,8},{8,9},{9,10},{10,1... | collective-permute-start | bytes 294920 | tf_op jit(solution)/shard_map/ppermute | solution.py:17
  56.2 26.1 %collective-permute-start.5 = (bf16[1,96,512]{2,1,0:T(8,128)(2,1)}, bf16[1,96,512]{2,1,0:T(8,128)(2,1)}, u32[]{:S(2)}, u32[]{:S(2)}) collective-permute-start(bf16[1,96,512]{2,1,0:T(8,128)(2,1)} %get-tuple-element.74), channel_id=1, source_target_pairs={{1,0},{2,1},{3,2},{4,3},{5,4},{6,5},{7,6},{8,7},{9,8},{10,9},{11,1... | collective-permute-start | bytes 294920 | tf_op jit(solution)/shard_map/ppermute | solution.py:20
  60.4 18.8 %copy-start.12 = (bf16[1,192,1,1,128]{4,1,3,2,0:T(8,128)(2,1)S(1)}, bf16[1,192,1,1,128]{4,1,3,2,0:T(8,128)(2,1)}, u32[]{:S(2)}) copy-start(bf16[1,192,1,1,128]{4,1,3,2,0:T(8,128)(2,1)} %param.7) | copy-start | bytes 147460
  95.1 3.2 copy-start.10
  98.3 0.9 copy-start.4
Sparse Core Ops, SparseCore 0:
  85.9 491.0 all-reduce.20
where the time goes:
time: 592 us; the launch traced here: 591 us
  waiting for transfers between devices  474 us (80%)
  local copies, waits for them, and re-layouts  53.7 us (9%)
  starting transfers between devices  20.8 us (4%)
  between operations  14.6 us (2%)
  other arithmetic  13.8 us (2%)
  matrix products  13.7 us (2%)
    psum x1, waiting for transfers between devices, shards(): lax.psum((first_grad, second_grad), ('dp', 'space'))  474 us
    unnamed x86, local copies, waits for them, and re-layouts  33.8 us
  transfers between devices with their start and end apart: 7, of which 1 were waited for; matrix products, arithmetic and copies ran while one was open for 10% of the time, Pallas kernels for 0%

commit v1 on v0

v1 whole, which is shorter than its diff:
```python
import math

import jax
import jax.numpy as jnp
import numpy as np
from jax import lax
from jax.experimental import pallas as pl
from jax.experimental.pallas import tpu as pltpu
from jax.sharding import Mesh
from jax.sharding import PartitionSpec as P

SPACE = ("xl", "y", "core")
DP = ("xh", "z")
NEAR = ("xh", "xl", "y", "core")
F32 = jnp.float32
BF16 = jnp.bfloat16

CH = 96
PG = 24
WIN = 9 * CH
LANES = 128
PIECES = 32
S_ROWS = 4096
F_ROWS = 768
S_PIECE = S_ROWS // PIECES
F_PIECE = F_ROWS // PIECES


def dot(a, b):
    return lax.dot_general(a, b, (((1,), (0,)), ((), ())), preferred_element_type=F32)


def dot_nt(a, b):
    return lax.dot_general(a, b, (((1,), (1,)), ((), ())), preferred_element_type=F32)


def dot_tn(a, b):
    return lax.dot_general(a, b, (((0,), (0,)), ((), ())), preferred_element_type=F32)


def later(tile):
    lane = lax.broadcasted_iota(jnp.int32, tile.shape, 1)
    return jnp.where(lane == 0, 0.0, pltpu.roll(tile, 1, 1))


def earlier(tile):
    lane = lax.broadcasted_iota(jnp.int32, tile.shape, 1)
    return jnp.where(lane == LANES - 1, 0.0, pltpu.roll(tile, LANES - 1, 1))


def fill_windows(ref, tiles):
    zero = jnp.zeros((CH, LANES), BF16)
    for b in range(3):
        for c in range(3):
            rows = pl.ds((b * 3 + c) * CH, CH)
            for y in range(2):
                source = y + b - 1
                if source in (0, 1):
                    even, odd, odd_later, even_earlier = tiles[source]
                    pair = ((odd_later, even), (even, odd), (odd, even_earlier))[c]
                else:
                    pair = (zero, zero)
                for parity in range(2):
                    ref[rows, pl.ds((2 * y + parity) * LANES, LANES)] = pair[parity]


def split_matrix():
    z = lax.broadcasted_iota(jnp.int32, (256, LANES), 0)
    k2 = 2 * lax.broadcasted_iota(jnp.int32, (256, LANES), 1)
    return jnp.concatenate(
        [jnp.where(z == k2 + off, 1.0, 0.0).astype(BF16) for off in (0, 1, -1, 2)], axis=1
    )


def merge_matrix():
    lane = lax.broadcasted_iota(jnp.int32, (LANES, 256), 0)
    z = lax.broadcasted_iota(jnp.int32, (LANES, 256), 1)
    return jnp.concatenate(
        [jnp.where(z == 2 * lane + bit, 1.0, 0.0).astype(BF16) for bit in (0, 1)], axis=0
    )


def expand(narrow, fold, mask):
    return (dot(narrow, fold) * mask).astype(BF16)


def forward_kernel(
    inner_ref, low_ref, own_ref, high_ref, fw_ref, fold_ref, mask_ref, cot_ref,
    sg_ref, pre_ref, xc_ref, wn_ref, xs, w1,
):
    inner = inner_ref[0]
    split = split_matrix()
    mask = mask_ref[...].astype(F32)
    for a in range(3):
        w1[pl.ds(a * CH, CH), :] = expand(fw_ref[pl.ds(a * CH, CH), :], fold_ref[...], mask)
    for e in range(6):
        plane_ref = (low_ref, own_ref, high_ref)[e // 2].at[e % 2]
        tiles = []
        for y in range(2):
            parts = dot(plane_ref[:, pl.ds(y * 256, 256)], split).astype(BF16)
            tiles.append([parts[:, q * LANES : (q + 1) * LANES] for q in range(4)])
            if 1 <= e <= 4:
                xc_ref[e - 1, :, pl.ds(y * 256, 256)] = parts[:, :256]
        fill_windows(xs.at[e], tiles)
    for e in range(6):
        first, last = max(0, e - 3), min(2, e)
        terms = dot(w1[pl.ds(first * CH, (last - first + 1) * CH), :], xs[e])
        for a in range(first, last + 1):
            term = terms[(a - first) * CH : (a - first + 1) * CH]
            j = e - a
            if a == 0:
                pre_ref[j] = term
            else:
                pre_ref[j] += term
    zero = jnp.zeros((CH, LANES), BF16)
    for a in range(3):
        for c in range(3):
            wn_ref[pl.ds((9 * a + c) * CH, CH), :] = zero
        for y in range(2):
            value = pre_ref[a, :, pl.ds(y * 256, 256)]
            hidden = value * jax.nn.sigmoid(value)
            if a == 0:
                hidden = hidden * inner
            even, odd = hidden[:, :LANES], hidden[:, LANES:]
            base = (9 * a + 3 * (y + 1)) * CH
            wn_ref[pl.ds(base, CH), :] = later(odd).astype(BF16)
            wn_ref[pl.ds(base + CH, CH), :] = even.astype(BF16)
            wn_ref[pl.ds(base + 2 * CH, CH), :] = odd.astype(BF16)
    cot = cot_ref[...]
    rows = 27 * CH
    half = rows // 2
    sg_ref[pl.ds(0, rows), :] = dot_nt(wn_ref[...], cot[:LANES]).astype(BF16)
    rest = cot[LANES:]
    none = jnp.zeros_like(rest)
    both = jnp.concatenate(
        [jnp.concatenate([rest, none], axis=1), jnp.concatenate([none, rest], axis=1)], axis=0
    )
    pairs = jnp.concatenate([wn_ref[pl.ds(0, half), :], wn_ref[pl.ds(half, half), :]], axis=1)
    sg_ref[pl.ds(rows, half), :] = dot_nt(pairs, both).astype(BF16)
    sg_ref[pl.ds(rows + half, S_ROWS - rows - half), :] = jnp.zeros(
        (S_ROWS - rows - half, LANES), BF16
    )


def backward_kernel(
    inner_ref, pre_ref, xc_ref, wn_ref, w2_ref, below_ref, cot_ref, above_ref, fw_ref, fold_ref,
    flip_ref, mask_ref, feat_ref, vg_ref, fg_ref, gs, w1, acc,
):
    inner = inner_ref[0]
    mask = mask_ref[...].astype(F32)
    for a in range(3):
        w1[pl.ds(a * CH, CH), :] = expand(fw_ref[pl.ds(a * CH, CH), :], fold_ref[...], mask)
    feat_ref[...] = dot_tn(w2_ref[...], wn_ref[...]).astype(BF16)
    cot = cot_ref[...]
    with_above = jnp.concatenate([cot, above_ref[...]], axis=1)
    with_below = jnp.concatenate([cot, below_ref[...]], axis=1)
    spread = [
        dot(w2_ref[pl.ds((9 * a + 3) * CH, 6 * CH), :], with_below if a == 2 else with_above)
        for a in range(3)
    ]
    for j in range(4):
        sources = {0: ((0, 0), (2, 1)), 1: ((1, 0),), 2: ((2, 0), (0, 1)), 3: ((1, 1),)}[j]
        tiles = []
        for y in range(2):
            got = []
            for c in range(3):
                total = None
                for a, part in sources:
                    tile = spread[a][
                        (3 * y + c) * CH : (3 * y + c + 1) * CH, part * LANES : (part + 1) * LANES
                    ]
                    total = tile if total is None else total + tile
                got.append(total)
            even = got[1]
            odd = got[2] + earlier(got[0])
            value = pre_ref[j, :, pl.ds(y * 256, 256)]
            sigma = jax.nn.sigmoid(value)
            slope = sigma * (1.0 + value * (1.0 - sigma))
            if j == 0:
                slope = slope * inner
            even = even * slope[:, :LANES]
            odd = odd * slope[:, LANES:]
            tiles.append(
                [t.astype(BF16) for t in (even, odd, later(odd), earlier(even))]
            )
        fill_windows(gs.at[j], tiles)
    for j in range(4):
        first, last = max(0, j - 1), min(2, j)
        terms = dot(w1[pl.ds(first * CH, (last - first + 1) * CH), :], gs[j])
        for a in range(first, last + 1):
            term = terms[(a - first) * CH : (a - first + 1) * CH]
            out = j - a
            if a == 0:
                acc[out] = term
            else:
                acc[out] += term
    merge = merge_matrix()
    for out in range(2):
        for y in range(2):
            cut = pl.ds(y * 256, 256)
            vg_ref[out, :, cut] = dot(acc[out, :, cut].astype(BF16), merge).astype(BF16)
    taps = None
    for j in (1, 2):
        planes = jnp.concatenate([xc_ref[j - 1], xc_ref[j], xc_ref[j + 1]], axis=0)
        term = dot_nt(planes, gs[j])
        taps = term if taps is None else taps + term
    for a in range(3):
        kept = (taps[a * CH : (a + 1) * CH] * mask).astype(BF16)
        narrow = dot_nt(kept, flip_ref[...]).astype(BF16)
        fg_ref[pl.ds(a * CH, CH), :] = narrow[:, :LANES]
        fg_ref[pl.ds((3 + a) * CH, CH), :] = narrow[:, LANES:]
    fg_ref[pl.ds(6 * CH, F_ROWS - 6 * CH), :] = jnp.zeros((F_ROWS - 6 * CH, LANES), BF16)


def finish_kernel(factor, all_ref, out_ref):
    rows = 27 * CH
    half = rows // 2
    flat = all_ref[:, pl.ds(0, S_PIECE), :].reshape(S_ROWS, LANES).astype(F32) * factor
    out_ref[:, pl.ds(0, LANES)] = flat[:rows]
    rest = flat[rows : rows + half]
    out_ref[pl.ds(0, half), pl.ds(LANES, 64)] = rest[:, :64]
    out_ref[pl.ds(half, half), pl.ds(LANES, 64)] = rest[:, 64:]


def constants():
    narrow = np.arange(9 * PG)
    wide = np.arange(WIN)
    same = (narrow[:, None] % PG) == (wide[None, :] % PG)
    fold = same & ((narrow[:, None] // PG) == (wide[None, :] // CH))
    flip = same & ((8 - narrow[:, None] // PG) == (wide[None, :] // CH))
    flip = np.pad(flip, ((0, 256 - 9 * PG), (0, 0)))
    mask = (np.arange(CH)[:, None] // PG) == ((wide[None, :] % CH) // PG)
    return [jnp.asarray(m.astype(np.float32), BF16) for m in (fold, flip, mask)]


def sum_pieces(parts):
    return jnp.sum(parts.astype(F32), axis=0).astype(BF16)


def to_all(piece, axes, count):
    copies = jnp.broadcast_to(piece[None], (count,) + piece.shape)
    return lax.all_to_all(copies, axes, 0, 0, tiled=True)


def shards(volume, first_weight, second_weight, out_cotangent):
    vmem = pl.BlockSpec(memory_space=pltpu.VMEM)
    smem = pl.BlockSpec(memory_space=pltpu.SMEM)
    params = pltpu.CompilerParams(vmem_limit_bytes=56 * 1024 * 1024)
    count = lax.axis_size(SPACE)
    up = [(i, i + 1) for i in range(count - 1)]
    down = [(i + 1, i) for i in range(count - 1)]
    own = volume[0].transpose(1, 0, 2, 3).reshape(2, CH, 512)
    cot = out_cotangent.reshape(192, LANES)
    low = lax.ppermute(own, SPACE, up)
    high = lax.ppermute(own, SPACE, down)
    below = lax.ppermute(cot, SPACE, up)
    above = lax.ppermute(cot, SPACE, down)
    inner = jnp.where(lax.axis_index(SPACE) > 0, 1.0, 0.0).astype(F32).reshape(1)
    fold, flip, mask = constants()
    forward_weight = (
        first_weight.reshape(3, 9, 4, PG, PG).transpose(0, 2, 4, 1, 3).reshape(3 * CH, 9 * PG)
    )
    backward_weight = (
        first_weight[::-1].reshape(3, 9, 4, PG, PG).transpose(0, 2, 3, 1, 4).reshape(3 * CH, 9 * PG)
    )
    w2 = second_weight.reshape(27 * CH, 192)
    sg, pre, centre, windows = pl.pallas_call(
        forward_kernel,
        out_shape=(
            jax.ShapeDtypeStruct((S_ROWS, LANES), BF16),
            jax.ShapeDtypeStruct((4, CH, 512), F32),
            jax.ShapeDtypeStruct((4, CH, 512), BF16),
            jax.ShapeDtypeStruct((27 * CH, LANES), BF16),
        ),
        in_specs=[smem] + [vmem] * 7,
        out_specs=(vmem,) * 4,
        scratch_shapes=[pltpu.VMEM((6, WIN, 512), BF16), pltpu.VMEM((3 * CH, WIN), BF16)],
        compiler_params=params,
        name="forward",
    )(inner, low, own, high, forward_weight, fold, mask, cot)
    s_parts = lax.all_to_all(sg.reshape(PIECES, S_PIECE, LANES), NEAR, 0, 0, tiled=True)
    feat, vgrad, fg = pl.pallas_call(
        backward_kernel,
        out_shape=(
            jax.ShapeDtypeStruct((192, LANES), BF16),
            jax.ShapeDtypeStruct((2, CH, 512), BF16),
            jax.ShapeDtypeStruct((F_ROWS, LANES), BF16),
        ),
        in_specs=[smem] + [vmem] * 11,
        out_specs=(vmem,) * 3,
        scratch_shapes=[
            pltpu.VMEM((4, WIN, 512), BF16),
            pltpu.VMEM((3 * CH, WIN), BF16),
            pltpu.VMEM((2, CH, 512), F32),
        ],
        compiler_params=params,
        cost_estimate=pl.CostEstimate(flops=2 * 10**9, bytes_accessed=4 * 10**6, transcendentals=200000),
        name="backward",
    )(inner, pre, centre, windows, w2, below, cot, above, backward_weight, fold, flip, mask)
    f_parts = lax.all_to_all(fg.reshape(PIECES, F_PIECE, LANES), NEAR, 0, 0, tiled=True)
    piece = jnp.concatenate([sum_pieces(s_parts), sum_pieces(f_parts)], axis=0)
    piece = sum_pieces(to_all(piece, "z", lax.axis_size("z")))
    every = to_all(piece, NEAR, PIECES)
    factor = 1.0 / math.sqrt(lax.axis_size(DP) * lax.axis_size(SPACE) * LANES)
    second_grad = pl.pallas_call(
        lambda a, b: finish_kernel(factor, a, b),
        out_shape=jax.ShapeDtypeStruct((27 * CH, 192), F32),
        in_specs=[vmem],
        out_specs=vmem,
        compiler_params=params,
        name="finish",
    )(every)
    narrow = every[:, S_PIECE:].reshape(F_ROWS, LANES)[: 6 * CH].astype(F32) * factor
    narrow = jnp.concatenate([narrow[: 3 * CH], narrow[3 * CH :]], axis=1)[:, : 9 * PG]
    first_grad = (
        narrow.reshape(3, 4, PG, 9, PG).transpose(0, 3, 1, 2, 4).reshape(first_weight.shape)
    )
    features = feat.reshape(out_cotangent.shape)
    volume_grad = vgrad.reshape(2, CH, 2, 256).transpose(1, 0, 2, 3)[None]
    return (features, volume_grad, first_grad, second_grad.reshape(second_weight.shape))


def solution(mesh):
    fine = Mesh(mesh.devices.reshape(2, 16, 2, 4, 2), ("xh", "z", "xl", "y", "core"))
    split = P(DP, None, SPACE, None, None)
    return jax.shard_map(
        shards,
        mesh=fine,
        in_specs=(split, P(), P(), split),
        out_specs=(split, split, P(), P()),
        check_vma=False,
    )
```

time: 592 us -> 160 us (0.27)
  waiting for transfers between devices: 474 us -> 35.2 us
  blocking collectives: 0 us -> 64.5 us
  local copies, waits for them, and re-layouts: 53.7 us -> 16.9 us
  Pallas kernels: 0 us -> 15.8 us
  between operations: 14.6 us -> 0.87 us
  matrix products: 13.7 us -> 0 us
  other arithmetic: 13.8 us -> 0.34 us
    psum x1 -> x0, waiting for transfers between devices: 474 us -> none  [shards(): lax.psum((first_grad, second_grad), ('dp', 'space'))]
    all_to_all x0 -> x2, blocking collectives: none -> 64.5 us  [the longest x1 49.3 us: to_all(): return lax.all_to_all(copies, axes, 0, 0, tiled=True)]
    all_to_all x0 -> x2, waiting for transfers between devices: none -> 35.2 us  [the longest x1 18.3 us: to_all(): return lax.all_to_all(copies, axes, 0, 0, tiled=True)]
    unnamed x86 -> x16, local copies, waits for them, and re-layouts: 33.8 us -> 6.72 us
    pallas_call x0 -> x3, Pallas kernels: none -> 15.8 us  [the longest x1 7.17 us: shards(): pl.pallas_call(backward_kernel, out_shape=(jax.ShapeDtypeStruct((192, LAN...]
    dot_general x12 -> x0, matrix products: 13.7 us -> none  [the longest x3 4.47 us: shards(): jnp.einsum('kqgin,qgon->kgio', stacked[:, off_x:off_x + planes], centre,...]
    slice x14 -> x3, local copies, waits for them, and re-layouts: 13.2 us -> 0.28 us  [the longest x2 0.15 us: shards(): narrow[:3 * CH]]
    all_to_all x0 -> x2, starting transfers between devices: none -> 9.57 us  [the longest x1 5.72 us: to_all(): return lax.all_to_all(copies, axes, 0, 0, tiled=True)]
  transfers between devices with their start and end apart: 7 -> 6, of which waited for: 1 -> 2; matrix products, arithmetic and copies ran while one was open for 10% -> 4% of each run, Pallas kernels for 0% -> 3%
where the time goes in v1:
time: 160 us; the launch traced here: 159 us
  blocking collectives  64.5 us (40%)
  waiting for transfers between devices  35.2 us (22%)
  starting transfers between devices  25.8 us (16%)
  local copies, waits for them, and re-layouts  16.9 us (11%)
  Pallas kernels  15.8 us (10%)
    all_to_all x1, blocking collectives, to_all(): return lax.all_to_all(copies, axes, 0, 0, tiled=True)  49.3 us
    all_to_all x1, waiting for transfers between devices, to_all(): return lax.all_to_all(copies, axes, 0, 0, tiled=True)  18.3 us
    all_to_all x1, waiting for transfers between devices, shards(): lax.all_to_all(sg.reshape(PIECES, S_PIECE, LANES), NEAR, 0, 0, tiled=True)  16.9 us
    all_to_all x1, blocking collectives, shards(): lax.all_to_all(fg.reshape(PIECES, F_PIECE, LANES), NEAR, 0, 0, tiled=True)  15.3 us
    ppermute x1, starting transfers between devices, shards(): high = lax.ppermute(own, SPACE, down)  8.79 us
    pallas_call x1, Pallas kernels, shards(): pl.pallas_call(backward_kernel, out_shape=(jax.ShapeDtypeStruct((192, LAN...  7.17 us
    unnamed x16, local copies, waits for them, and re-layouts  6.72 us
    all_to_all x1, starting transfers between devices, to_all(): return lax.all_to_all(copies, axes, 0, 0, tiled=True)  5.72 us
  transfers between devices with their start and end apart: 6, of which 2 were waited for; matrix products, arithmetic and copies ran while one was open for 4% of the time, Pallas kernels for 3%

profile of v1, /device:TPU:1, one launch (start us, length us, event | category | flops | bytes accessed | tf_op | source)
XLA Modules:
  0.0 159.5 jit_solution(8462483242544955297)
XLA Ops:
  0.6 1.1 reshape.77
  1.7 8.8 %collective-permute-start.1 = (bf16[2,96,512]{2,1,0:T(8,128)(2,1)S(1)}, bf16[2,96,512]{2,1,0:T(8,128)(2,1)S(1)}, u32[]{:S(2)}, u32[]{:S(2)}) collective-permute-start(bf16[2,96,512]{2,1,0:T(8,128)(2,1)S(1)} %copy.40.own_ref), channel_id=1, source_target_pairs={{1,0},{2,1},{3,2},{4,3},{5,4},{6,5},{7,6},{8,7},{9,8},{10,9},{11,1... | collective-permute-start | bytes 589832 | tf_op jit(solution)/shard_map/ppermute | solution.py:255
  10.5 1.9 %collective-permute-start = (bf16[2,96,512]{2,1,0:T(8,128)(2,1)S(1)}, bf16[2,96,512]{2,1,0:T(8,128)(2,1)S(1)}, u32[]{:S(2)}, u32[]{:S(2)}) collective-permute-start(bf16[2,96,512]{2,1,0:T(8,128)(2,1)S(1)} %copy.40.own_ref), channel_id=1, source_target_pairs={{0,1},{1,2},{2,3},{3,4},{4,5},{5,6},{6,7},{7,8},{8,9},{9,10},{10,1... | collective-permute-start | bytes 589832 | tf_op jit(solution)/shard_map/ppermute | solution.py:254
  12.5 2.4 %collective-permute-start.3 = (bf16[192,128]{1,0:T(8,128)(2,1)}, bf16[192,128]{1,0:T(8,128)(2,1)S(1)}, u32[]{:S(2)}, u32[]{:S(2)}) collective-permute-start(bf16[192,128]{1,0:T(8,128)(2,1)} %bitcast.43), channel_id=1, source_target_pairs={{1,0},{2,1},{3,2},{4,3},{5,4},{6,5},{7,6},{8,7},{9,8},{10,9},{11,1... | collective-permute-start | bytes 147464 | tf_op jit(solution)/shard_map/ppermute | solution.py:257
  14.9 3.2 %collective-permute-start.2 = (bf16[192,128]{1,0:T(8,128)(2,1)}, bf16[192,128]{1,0:T(8,128)(2,1)S(1)}, u32[]{:S(2)}, u32[]{:S(2)}) collective-permute-start(bf16[192,128]{1,0:T(8,128)(2,1)} %bitcast.44), channel_id=1, source_target_pairs={{0,1},{1,2},{2,3},{3,4},{4,5},{5,6},{6,7},{7,8},{8,9},{9,10},{10,1... | collective-permute-start | bytes 147464 | tf_op jit(solution)/shard_map/ppermute | solution.py:256
  18.0 2.3 %copy.29 = bf16[27,4,24,24]{3,2,1,0:T(8,128)(2,1)S(1)} copy(bf16[27,4,24,24]{0,3,2,1:T(8,128)(2,1)} %param.8) | data formatting | bytes 248832 | tf_op args[1]
  21.0 0.8 copy.31.fw_ref
  21.8 1.3 copy.33
  23.5 0.8 copy.34.fw_ref
  24.3 0.7 copy-done.2
  25.0 5.5 %forward.1 = (bf16[4096,128]{1,0:T(8,128)(2,1)}, f32[4,96,512]{2,1,0:T(8,128)}, bf16[4,96,512]{2,1,0:T(8,128)(2,1)}, bf16[2592,128]{1,0:T(8,128)(2,1)}) custom-call(f32[1]{0:T(128)} %bitcast.inner_ref, bf16[2,96,512]{2,1,0:T(8,128)(2,1)} %copy-done.3, bf16[2,96,512]{2,1,0:T(8,128)(2,1)} %copy-done.1, bf16[2,96,512]{2,1,0:T(8,128)(2,1)} %copy-done.2, ...), custom_call_target="tpu_custom_call" | custom-call | tf_op jit(solution)/shard_map/forward/pallas_call | solution.py:267
  31.2 7.2 %backward.1 = (bf16[192,128]{1,0:T(8,128)(2,1)}, bf16[2,96,512]{2,1,0:T(8,128)(2,1)}, bf16[768,128]{1,0:T(8,128)(2,1)}) custom-call(f32[1]{0:T(128)} %bitcast.inner_ref, f32[4,96,512]{2,1,0:T(8,128)} %get-tuple-element.11.pre_ref, bf16[4,96,512]{2,1,0:T(8,128)(2,1)} %get-tuple-element.12.xc_ref, bf16[2592,128]{1,0:T(8,128)(2,1)} %get-tuple-element.13.wn_ref, ...), custom_call_target="tpu_custom_call" | custom-call | flops 2000000000 | bytes 4000000 | tf_op jit(solution)/shard_map/backward/pallas_call | solution.py:282
  38.3 15.3 %all_to_all.20 = bf16[32,24,128]{2,1,0:T(8,128)(2,1)S(1)} all-to-all(bf16[32,24,128]{2,1,0:T(8,128)(2,1)} %bitcast.42), channel_id=1, replica_groups=mesh['xh'=2,'z'=16,'xl'=2,'y'=4,'core'=2] {'xh','xl','y','core'}, dimensions={0} | all-to-all | bytes 393216 | tf_op jit(solution)/shard_map/all_to_all | solution.py:300
  53.6 3.8 %all-to-all-start = ((bf16[32,128,128]{2,1,0:T(8,128)(2,1)}), bf16[32,128,128]{2,1,0:T(8,128)(2,1)S(1)}, u32[]{:S(2)}, u32[]{:S(2)}) async-start(bf16[32,128,128]{2,1,0:T(8,128)(2,1)} %bitcast.13), calls=%async_computation | async-start | bytes 2097152 | tf_op jit(solution)/shard_map/all_to_all | solution.py:281
  57.5 16.9 %all-to-all-done = bf16[32,128,128]{2,1,0:T(8,128)(2,1)S(1)} async-done(((bf16[32,128,128]{2,1,0:T(8,128)(2,1)}), bf16[32,128,128]{2,1,0:T(8,128)(2,1)S(1)}, u32[]{:S(2)}, u32[]{:S(2)}) %all-to-all-start) | async-done | bytes 1048608 | tf_op jit(solution)/shard_map/all_to_all | solution.py:281
  74.7 49.3 %all_to_all.21 = bf16[16,152,128]{2,1,0:T(8,128)(2,1)S(1)} all-to-all(bf16[16,152,128]{2,1,0:T(8,128)(2,1)S(1)} %broadcast_in_dim.7), channel_id=1, replica_groups=mesh['xh'=2,'z'=16,'xl'=2,'y'=4,'core'=2] {'z'}, dimensions={0} | all-to-all | bytes 1245184 | tf_op jit(solution)/shard_map/all_to_all | solution.py:242
  124.1 1.2 broadcast_in_dim.8
  125.3 5.7 %all-to-all-start.3 = ((bf16[32,152,128]{2,1,0:T(8,128)(2,1)}), bf16[32,152,128]{2,1,0:T(8,128)(2,1)S(1)}, u32[]{:S(2)}, u32[]{:S(2)}) async-start(bf16[32,152,128]{2,1,0:T(8,128)(2,1)} %broadcast_in_dim.8), calls=%async_computation.3 | async-start | bytes 2490368 | tf_op jit(solution)/shard_map/all_to_all | solution.py:242
  131.1 0.8 copy.42
  131.9 18.3 %all-to-all-done.3.a = bf16[32,152,128]{2,1,0:T(8,128)(2,1)S(1)} async-done(((bf16[32,152,128]{2,1,0:T(8,128)(2,1)}), bf16[32,152,128]{2,1,0:T(8,128)(2,1)S(1)}, u32[]{:S(2)}, u32[]{:S(2)}) %all-to-all-start.3) | async-done | bytes 1245216 | tf_op jit(solution)/shard_map/all_to_all | solution.py:242
  150.5 0.7 reshape.74
  151.3 2.0 %copy.38 = f32[3,9,4,24,24]{4,3,2,1,0:T(8,128)} copy(f32[3,9,4,24,24]{3,2,0,4,1:T(4,128)S(1)} %bitcast.34) | data formatting | bytes 497664 | tf_op jit(solution)/shard_map/transpose | solution.py:316
  153.3 3.1 %copy.39 = f32[27,4,24,24]{0,3,2,1:T(8,128)} copy(f32[27,4,24,24]{3,2,1,0:T(8,128)} %bitcast.35) | data formatting | bytes 497664
  156.4 3.1 %finish.1 = f32[2592,192]{1,0:T(8,128)} custom-call(bf16[32,152,128]{2,1,0:T(8,128)(2,1)} %copy-done), custom_call_target="tpu_custom_call" | custom-call | tf_op jit(solution)/shard_map/finish/pallas_call | solution.py:305
  (33 shorter events, 2.5 us)
Async XLA Ops:
  1.7 18.9 %copy-start.1 = (bf16[2,96,512]{2,1,0:T(8,128)(2,1)}, bf16[2,96,512]{2,1,0:T(8,128)(2,1)S(1)}, u32[]{:S(2)}) copy-start(bf16[2,96,512]{2,1,0:T(8,128)(2,1)S(1)} %copy.40.own_ref) | copy-start | bytes 589828
  1.7 22.5 %collective-permute-start.1 = (bf16[2,96,512]{2,1,0:T(8,128)(2,1)S(1)}, bf16[2,96,512]{2,1,0:T(8,128)(2,1)S(1)}, u32[]{:S(2)}, u32[]{:S(2)}) collective-permute-start(bf16[2,96,512]{2,1,0:T(8,128)(2,1)S(1)} %copy.40.own_ref), channel_id=1, source_target_pairs={{1,0},{2,1},{3,2},{4,3},{5,4},{6,5},{7,6},{8,7},{9,8},{10,9},{11,1... | collective-permute-start | bytes 589832 | tf_op jit(solution)/shard_map/ppermute | solution.py:255
  10.5 13.7 %collective-permute-start = (bf16[2,96,512]{2,1,0:T(8,128)(2,1)S(1)}, bf16[2,96,512]{2,1,0:T(8,128)(2,1)S(1)}, u32[]{:S(2)}, u32[]{:S(2)}) collective-permute-start(bf16[2,96,512]{2,1,0:T(8,128)(2,1)S(1)} %copy.40.own_ref), channel_id=1, source_target_pairs={{0,1},{1,2},{2,3},{3,4},{4,5},{5,6},{6,7},{7,8},{8,9},{9,10},{10,1... | collective-permute-start | bytes 589832 | tf_op jit(solution)/shard_map/ppermute | solution.py:254
  12.5 18.1 %collective-permute-start.3 = (bf16[192,128]{1,0:T(8,128)(2,1)}, bf16[192,128]{1,0:T(8,128)(2,1)S(1)}, u32[]{:S(2)}, u32[]{:S(2)}) collective-permute-start(bf16[192,128]{1,0:T(8,128)(2,1)} %bitcast.43), channel_id=1, source_target_pairs={{1,0},{2,1},{3,2},{4,3},{5,4},{6,5},{7,6},{8,7},{9,8},{10,9},{11,1... | collective-permute-start | bytes 147464 | tf_op jit(solution)/shard_map/ppermute | solution.py:257
  14.9 15.7 %collective-permute-start.2 = (bf16[192,128]{1,0:T(8,128)(2,1)}, bf16[192,128]{1,0:T(8,128)(2,1)S(1)}, u32[]{:S(2)}, u32[]{:S(2)}) collective-permute-start(bf16[192,128]{1,0:T(8,128)(2,1)} %bitcast.44), channel_id=1, source_target_pairs={{0,1},{1,2},{2,3},{3,4},{4,5},{5,6},{6,7},{7,8},{8,9},{9,10},{10,1... | collective-permute-start | bytes 147464 | tf_op jit(solution)/shard_map/ppermute | solution.py:256
  24.3 0.7 copy-start.2
  24.3 0.7 copy-start.3
  30.5 0.6 copy-start.5
  30.6 0.6 copy-start.6
  53.6 20.9 %all-to-all-start = ((bf16[32,128,128]{2,1,0:T(8,128)(2,1)}), bf16[32,128,128]{2,1,0:T(8,128)(2,1)S(1)}, u32[]{:S(2)}, u32[]{:S(2)}) async-start(bf16[32,128,128]{2,1,0:T(8,128)(2,1)} %bitcast.13), calls=%async_computation | async-start | bytes 2097152 | tf_op jit(solution)/shard_map/all_to_all | solution.py:281
  125.3 5.7 %copy-start.4 = (bf16[2,96,512]{2,1,0:T(8,128)(2,1)S(1)}, bf16[2,96,512]{2,1,0:T(8,128)(2,1)}, u32[]{:S(2)}) copy-start(bf16[2,96,512]{2,1,0:T(8,128)(2,1)} %get-tuple-element.15) | copy-start | bytes 589828
  125.3 24.9 %all-to-all-start.3 = ((bf16[32,152,128]{2,1,0:T(8,128)(2,1)}), bf16[32,152,128]{2,1,0:T(8,128)(2,1)S(1)}, u32[]{:S(2)}, u32[]{:S(2)}) async-start(bf16[32,152,128]{2,1,0:T(8,128)(2,1)} %broadcast_in_dim.8), calls=%async_computation.3 | async-start | bytes 2490368 | tf_op jit(solution)/shard_map/all_to_all | solution.py:242
  150.2 1.1 copy-start

commit v2 on v1

v2 whole, which is shorter than its diff:
```python
import math

import jax
import jax.numpy as jnp
import numpy as np
from jax import lax
from jax.experimental import pallas as pl
from jax.experimental.pallas import tpu as pltpu
from jax.sharding import Mesh
from jax.sharding import PartitionSpec as P

SPACE = ("xl", "y", "core")
DP = ("xh", "zh", "zl")
NEAR = ("xh", "xl", "y", "core", "zl")
F32 = jnp.float32
BF16 = jnp.bfloat16

CH = 96
PG = 24
WIN = 9 * CH
LANES = 128
PIECES = 64
ROWS = 4608
S_ROWS = 3 * (WIN + WIN // 2)
PIECE = ROWS // PIECES


def dot(a, b):
    return lax.dot_general(a, b, (((1,), (0,)), ((), ())), preferred_element_type=F32)


def dot_nt(a, b):
    return lax.dot_general(a, b, (((1,), (1,)), ((), ())), preferred_element_type=F32)


def dot_tn(a, b):
    return lax.dot_general(a, b, (((0,), (0,)), ((), ())), preferred_element_type=F32)


def later(tile):
    lane = lax.broadcasted_iota(jnp.int32, tile.shape, 1)
    return jnp.where(lane == 0, 0.0, pltpu.roll(tile, 1, 1))


def earlier(tile):
    lane = lax.broadcasted_iota(jnp.int32, tile.shape, 1)
    return jnp.where(lane == LANES - 1, 0.0, pltpu.roll(tile, LANES - 1, 1))


def fill_windows(ref, tiles):
    zero = jnp.zeros((CH, LANES), BF16)
    for b in range(3):
        for c in range(3):
            rows = pl.ds((b * 3 + c) * CH, CH)
            for y in range(2):
                source = y + b - 1
                if source in (0, 1):
                    even, odd, odd_later, even_earlier = tiles[source]
                    pair = ((odd_later, even), (even, odd), (odd, even_earlier))[c]
                else:
                    pair = (zero, zero)
                for parity in range(2):
                    ref[rows, pl.ds((2 * y + parity) * LANES, LANES)] = pair[parity]


def split_matrix():
    z = lax.broadcasted_iota(jnp.int32, (256, LANES), 0)
    k2 = 2 * lax.broadcasted_iota(jnp.int32, (256, LANES), 1)
    return jnp.concatenate(
        [jnp.where(z == k2 + off, 1.0, 0.0).astype(BF16) for off in (0, 1, -1, 2)], axis=1
    )


def merge_matrix():
    lane = lax.broadcasted_iota(jnp.int32, (LANES, 256), 0)
    z = lax.broadcasted_iota(jnp.int32, (LANES, 256), 1)
    return jnp.concatenate(
        [jnp.where(z == 2 * lane + bit, 1.0, 0.0).astype(BF16) for bit in (0, 1)], axis=0
    )


def expand(narrow, fold, mask):
    return (dot(narrow, fold) * mask).astype(BF16)


def main_kernel(
    inner_ref, low_ref, own_ref, high_ref, fw_ref, fold_ref, mask_ref, order_ref, w2_ref,
    comm_ref, wn_ref, g_ref, xs, w1, pre_ref, xc_ref, gs,
):
    inner = inner_ref[0]
    split = split_matrix()
    mask = mask_ref[...].astype(F32)
    for a in range(3):
        w1[pl.ds(a * CH, CH), :] = expand(fw_ref[pl.ds(a * CH, CH), :], fold_ref[...], mask)
    for e in range(6):
        slab = (low_ref, own_ref, high_ref)[e // 2]
        tiles = []
        for y in range(2):
            at = 4 * (e % 2) + 2 * y
            parts = dot(jnp.concatenate([slab[at], slab[at + 1]], axis=1), split).astype(BF16)
            tiles.append([parts[:, q * LANES : (q + 1) * LANES] for q in range(4)])
            if 1 <= e <= 4:
                xc_ref[e - 1, :, pl.ds(y * 256, 256)] = parts[:, :256]
        fill_windows(xs.at[e], tiles)
    for e in range(6):
        first, last = max(0, e - 3), min(2, e)
        terms = dot(w1[pl.ds(first * CH, (last - first + 1) * CH), :], xs[e])
        for a in range(first, last + 1):
            term = terms[(a - first) * CH : (a - first + 1) * CH]
            j = e - a
            if a == 0:
                pre_ref[j] = term
            else:
                pre_ref[j] += term
    zero = jnp.zeros((CH, LANES), BF16)
    for a in range(3):
        for c in range(3):
            wn_ref[pl.ds((9 * a + c) * CH, CH), :] = zero
        for y in range(2):
            value = pre_ref[a, :, pl.ds(y * 256, 256)]
            hidden = value * jax.nn.sigmoid(value)
            if a == 0:
                hidden = hidden * inner
            even, odd = hidden[:, :LANES], hidden[:, LANES:]
            base = (9 * a + 3 * (y + 1)) * CH
            wn_ref[pl.ds(base, CH), :] = later(odd).astype(BF16)
            wn_ref[pl.ds(base + CH, CH), :] = even.astype(BF16)
            wn_ref[pl.ds(base + 2 * CH, CH), :] = odd.astype(BF16)
    cot = jnp.concatenate([own_ref[8], own_ref[9]], axis=0)
    rest = cot[LANES:]
    none = jnp.zeros_like(rest)
    both = jnp.concatenate(
        [jnp.concatenate([rest, none], axis=1), jnp.concatenate([none, rest], axis=1)], axis=0
    )
    half = WIN // 2
    for a in range(3):
        at = a * (WIN + half)
        comm_ref[pl.ds(at, WIN), :] = dot_nt(wn_ref[pl.ds(a * WIN, WIN), :], cot[:LANES]).astype(
            BF16
        )
        pairs = jnp.concatenate(
            [wn_ref[pl.ds(a * WIN, half), :], wn_ref[pl.ds(a * WIN + half, half), :]], axis=1
        )
        comm_ref[pl.ds(at + WIN, half), :] = dot_nt(pairs, both).astype(BF16)
    above = jnp.concatenate([high_ref[8], high_ref[9]], axis=0)
    below = jnp.concatenate([low_ref[8], low_ref[9]], axis=0)
    with_above = jnp.concatenate([cot, above], axis=1)
    with_below = jnp.concatenate([cot, below], axis=1)
    spread = [
        dot(w2_ref[pl.ds((9 * a + 3) * CH, 6 * CH), :], with_below if a == 2 else with_above)
        for a in range(3)
    ]
    for j in range(4):
        sources = {0: ((0, 0), (2, 1)), 1: ((1, 0),), 2: ((2, 0), (0, 1)), 3: ((1, 1),)}[j]
        tiles = []
        for y in range(2):
            got = []
            for c in range(3):
                total = None
                for a, part in sources:
                    tile = spread[a][
                        (3 * y + c) * CH : (3 * y + c + 1) * CH, part * LANES : (part + 1) * LANES
                    ]
                    total = tile if total is None else total + tile
                got.append(total)
            even = got[1]
            odd = got[2] + earlier(got[0])
            value = pre_ref[j, :, pl.ds(y * 256, 256)]
            sigma = jax.nn.sigmoid(value)
            slope = sigma * (1.0 + value * (1.0 - sigma))
            if j == 0:
                slope = slope * inner
            even = even * slope[:, :LANES]
            odd = odd * slope[:, LANES:]
            tiles.append([t.astype(BF16) for t in (even, odd, later(odd), earlier(even))])
            for q in range(4):
                g_ref[j, :, pl.ds((4 * y + q) * LANES, LANES)] = tiles[y][q]
        if j in (1, 2):
            fill_windows(gs.at[j - 1], tiles)
    taps = None
    for j in (1, 2):
        planes = jnp.concatenate([xc_ref[j - 1], xc_ref[j], xc_ref[j + 1]], axis=0)
        term = dot_nt(planes, gs[j - 1])
        taps = term if taps is None else taps + term
    narrow = [
        dot_nt((taps[a * CH : (a + 1) * CH] * mask).astype(BF16), fold_ref[...]).astype(BF16)
        for a in range(3)
    ]
    ordered = dot(jnp.concatenate(narrow, axis=1), order_ref[...]).astype(BF16)
    for k in range(6):
        comm_ref[pl.ds(S_ROWS + k * CH, CH), :] = ordered[:, k * LANES : (k + 1) * LANES]
    left = ROWS - S_ROWS - 6 * CH
    comm_ref[pl.ds(ROWS - left, left), :] = jnp.zeros((left, LANES), BF16)


def tail_kernel(g_ref, wn_ref, w2_ref, fw_ref, fold_ref, mask_ref, feat_ref, vg_ref, gs, w1, acc):
    mask = mask_ref[...].astype(F32)
    for a in range(3):
        w1[pl.ds(a * CH, CH), :] = expand(fw_ref[pl.ds(a * CH, CH), :], fold_ref[...], mask)
    feat_ref[...] = dot_tn(w2_ref[...], wn_ref[...]).astype(BF16)
    for j in range(4):
        tiles = [
            [g_ref[j, :, pl.ds((4 * y + q) * LANES, LANES)] for q in range(4)] for y in range(2)
        ]
        fill_windows(gs.at[j], tiles)
    for j in range(4):
        first, last = max(0, j - 1), min(2, j)
        terms = dot(w1[pl.ds(first * CH, (last - first + 1) * CH), :], gs[j])
        for a in range(first, last + 1):
            term = terms[(a - first) * CH : (a - first + 1) * CH]
            out = j - a
            if a == 0:
                acc[out] = term
            else:
                acc[out] += term
    merge = merge_matrix()
    for out in range(2):
        for y in range(2):
            cut = pl.ds(y * 256, 256)
            vg_ref[out, :, cut] = dot(acc[out, :, cut].astype(BF16), merge).astype(BF16)


def finish_kernel(factor, all_ref, out_ref):
    half = WIN // 2
    out_ref[:, pl.ds(0, LANES)] = all_ref[pl.ds(0, WIN), :].astype(F32) * factor
    rest = all_ref[pl.ds(WIN, half), :].astype(F32) * factor
    out_ref[pl.ds(0, half), pl.ds(LANES, 64)] = rest[:, :64]
    out_ref[pl.ds(half, half), pl.ds(LANES, 64)] = rest[:, 64:]


def constants():
    narrow = np.arange(9 * PG)
    wide = np.arange(WIN)
    fold = ((narrow[:, None] % PG) == (wide[None, :] % PG)) & (
        (narrow[:, None] // PG) == (wide[None, :] // CH)
    )
    fold = np.pad(fold, ((0, 256 - 9 * PG), (0, 0)))
    mask = (np.arange(CH)[:, None] // PG) == ((wide[None, :] % CH) // PG)
    order = np.zeros((3 * 256, 6 * LANES))
    for a in range(3):
        for back in range(9):
            for o in range(PG):
                order[a * 256 + back * PG + o, o * 27 + 9 * a + 8 - back] = 1
    return [jnp.asarray(m.astype(np.float32), BF16) for m in (fold, mask, order)]


def sum_pieces(parts):
    return jnp.sum(parts.astype(F32), axis=0).astype(BF16)


def to_all(piece, axes, count):
    copies = jnp.broadcast_to(piece[None], (count,) + piece.shape)
    return lax.all_to_all(copies, axes, 0, 0, tiled=True)


def shards(volume, first_weight, second_weight, out_cotangent):
    vmem = pl.BlockSpec(memory_space=pltpu.VMEM)
    smem = pl.BlockSpec(memory_space=pltpu.SMEM)
    params = pltpu.CompilerParams(vmem_limit_bytes=56 * 1024 * 1024)
    count = lax.axis_size(SPACE)
    up = [(i, i + 1) for i in range(count - 1)]
    down = [(i + 1, i) for i in range(count - 1)]
    planes = volume.reshape(CH, 2, 2, 2, LANES).transpose(1, 2, 3, 0, 4).reshape(8, CH, LANES)
    own = jnp.concatenate([planes, out_cotangent.reshape(2, CH, LANES)], axis=0)
    low = lax.ppermute(own, SPACE, up)
    high = lax.ppermute(own, SPACE, down)
    inner = jnp.where(lax.axis_index(SPACE) > 0, 1.0, 0.0).astype(F32).reshape(1)
    fold, mask, order = constants()
    wide = ((0, 0), (0, 256 - 9 * PG))
    forward_weight = jnp.pad(
        first_weight.reshape(3, 9, 4, PG, PG).transpose(0, 2, 4, 1, 3).reshape(3 * CH, 9 * PG), wide
    )
    w2 = second_weight.reshape(27 * CH, 192)
    comm, windows, grads = pl.pallas_call(
        main_kernel,
        out_shape=(
            jax.ShapeDtypeStruct((ROWS, LANES), BF16),
            jax.ShapeDtypeStruct((27 * CH, LANES), BF16),
            jax.ShapeDtypeStruct((4, CH, 8 * LANES), BF16),
        ),
        in_specs=[smem] + [vmem] * 8,
        out_specs=(vmem,) * 3,
        scratch_shapes=[
            pltpu.VMEM((6, WIN, 512), BF16),
            pltpu.VMEM((3 * CH, WIN), BF16),
            pltpu.VMEM((4, CH, 512), F32),
            pltpu.VMEM((4, CH, 512), BF16),
            pltpu.VMEM((2, WIN, 512), BF16),
        ],
        compiler_params=params,
        name="main",
    )(inner, low, own, high, forward_weight, fold, mask, order, w2)
    parts = lax.all_to_all(comm.reshape(PIECES, PIECE, LANES), NEAR, 0, 0, tiled=True)
    late_weight = lax.optimization_barrier((first_weight, comm))[0]
    backward_weight = jnp.pad(
        late_weight[::-1].reshape(3, 9, 4, PG, PG).transpose(0, 2, 3, 1, 4).reshape(3 * CH, 9 * PG),
        wide,
    )
    feat, vgrad = pl.pallas_call(
        tail_kernel,
        out_shape=(
            jax.ShapeDtypeStruct((192, LANES), BF16),
            jax.ShapeDtypeStruct((2, CH, 512), BF16),
        ),
        in_specs=[vmem] * 6,
        out_specs=(vmem,) * 2,
        scratch_shapes=[
            pltpu.VMEM((4, WIN, 512), BF16),
            pltpu.VMEM((3 * CH, WIN), BF16),
            pltpu.VMEM((2, CH, 512), F32),
        ],
        compiler_params=params,
        cost_estimate=pl.CostEstimate(flops=10**9, bytes_accessed=4 * 10**6, transcendentals=0),
        name="tail",
    )(grads, windows, w2, backward_weight, fold, mask)
    piece = sum_pieces(to_all(sum_pieces(parts), "zh", lax.axis_size("zh")))
    every = to_all(piece, NEAR, PIECES).reshape(ROWS, LANES)
    factor = 1.0 / math.sqrt(lax.axis_size(DP) * lax.axis_size(SPACE) * LANES)
    block = WIN + WIN // 2
    second_grad = pl.pallas_call(
        lambda a, b: finish_kernel(factor, a, b),
        out_shape=jax.ShapeDtypeStruct((27 * CH, 192), F32),
        grid=(3,),
        in_specs=[pl.BlockSpec((block, LANES), lambda k: (k, 0))],
        out_specs=pl.BlockSpec((WIN, 192), lambda k: (k, 0)),
        compiler_params=params,
        name="finish",
    )(every)
    narrow = every[S_ROWS : S_ROWS + 6 * CH].reshape(6, CH, LANES).transpose(1, 0, 2)
    narrow = narrow.reshape(CH, 6 * LANES)[:, : 27 * PG].astype(F32) * factor
    first_grad = narrow.reshape(4, PG, PG, 27).transpose(3, 0, 1, 2)
    features = feat.reshape(out_cotangent.shape)
    volume_grad = vgrad.reshape(2, CH, 2, 256).transpose(1, 0, 2, 3)[None]
    return (features, volume_grad, first_grad, second_grad.reshape(second_weight.shape))


def solution(mesh):
    fine = Mesh(mesh.devices.reshape(2, 8, 2, 2, 4, 2), ("xh", "zh", "zl", "xl", "y", "core"))
    split = P(DP, None, SPACE, None, None)
    return jax.shard_map(
        shards,
        mesh=fine,
        in_specs=(split, P(), P(), split),
        out_specs=(split, split, P(), P()),
        check_vma=False,
    )
```

time: 160 us -> 115 us (0.72)
  waiting for transfers between devices: 35.2 us -> 8.78 us
  blocking collectives: 64.5 us -> 55.2 us
  starting transfers between devices: 25.8 us -> 18.5 us
  local copies, waits for them, and re-layouts: 16.9 us -> 14.8 us
    all_to_all x1, blocking collectives: 49.3 us -> 27.2 us  [to_all(): return lax.all_to_all(copies, axes, 0, 0, tiled=True)]
    all_to_all x1 -> x0, waiting for transfers between devices: 16.9 us -> none  [shards(): lax.all_to_all(sg.reshape(PIECES, S_PIECE, LANES), NEAR, 0, 0, tiled=True)]
    all_to_all x1, blocking collectives: 15.3 us -> 28 us  [shards(): lax.all_to_all(comm.reshape(PIECES, PIECE, LANES), NEAR, 0, 0, tiled=True)]
    all_to_all x1, waiting for transfers between devices: 18.3 us -> 8.78 us  [to_all(): return lax.all_to_all(copies, axes, 0, 0, tiled=True)]
    ppermute x2 -> x0, starting transfers between devices: 5.57 us -> none  [the longest x1 3.15 us: shards(): below = lax.ppermute(cot, SPACE, up)]
    all_to_all x1 -> x0, starting transfers between devices: 3.85 us -> none  [shards(): lax.all_to_all(sg.reshape(PIECES, S_PIECE, LANES), NEAR, 0, 0, tiled=True)]
    unnamed x16 -> x11, local copies, waits for them, and re-layouts: 6.72 us -> 3.06 us
    ppermute x1, starting transfers between devices: 8.79 us -> 5.5 us  [shards(): high = lax.ppermute(own, SPACE, down)]
  transfers between devices with their start and end apart: 6 -> 3, of which waited for: 2 -> 1; matrix products, arithmetic and copies ran while one was open for 4% -> 7% of each run, Pallas kernels for 3% -> 4%
where the time goes in v2:
time: 115 us
  blocking collectives  55.2 us (48%)
  starting transfers between devices  18.5 us (16%)
  Pallas kernels  15.7 us (14%)
  local copies, waits for them, and re-layouts  14.8 us (13%)
  waiting for transfers between devices  8.78 us (8%)
    all_to_all x1, blocking collectives, shards(): lax.all_to_all(comm.reshape(PIECES, PIECE, LANES), NEAR, 0, 0, tiled=True)  28 us
    all_to_all x1, blocking collectives, to_all(): return lax.all_to_all(copies, axes, 0, 0, tiled=True)  27.2 us
    all_to_all x1, waiting for transfers between devices, to_all(): return lax.all_to_all(copies, axes, 0, 0, tiled=True)  8.78 us
    all_to_all x1, starting transfers between devices, to_all(): return lax.all_to_all(copies, axes, 0, 0, tiled=True)  8.39 us
    pallas_call x1, Pallas kernels, shards(): pl.pallas_call(main_kernel, out_shape=(jax.ShapeDtypeStruct((ROWS, LANES)...  8.1 us
    ppermute x1, starting transfers between devices, shards(): high = lax.ppermute(own, SPACE, down)  5.5 us
    ppermute x1, starting transfers between devices, shards(): low = lax.ppermute(own, SPACE, up)  4.59 us
    pallas_call x1, Pallas kernels, shards(): pl.pallas_call(tail_kernel, out_shape=(jax.ShapeDtypeStruct((192, LANES),...  4.26 us
  transfers between devices with their start and end apart: 3, of which 1 were waited for; matrix products, arithmetic and copies ran while one was open for 7% of the time, Pallas kernels for 4%

profile of v2, /device:TPU:1, one launch (start us, length us, event | category | flops | bytes accessed | tf_op | source)
XLA Modules:
  0.0 114.8 jit_solution(10807814454032989667)
XLA Ops:
  0.6 1.1 reshape.64
  1.8 0.8 pad_maximum_fusion.own_ref
  2.6 4.6 %collective-permute-start = (bf16[10,96,128]{2,1,0:T(8,128)(2,1)S(1)}, bf16[10,96,128]{2,1,0:T(8,128)(2,1)S(1)}, u32[]{:S(2)}, u32[]{:S(2)}) collective-permute-start(bf16[10,96,128]{2,1,0:T(8,128)(2,1)S(1)} %pad_maximum_fusion.own_ref), channel_id=1, source_target_pairs={{0,1},{1,2},{2,3},{3,4},{4,5},{5,6},{6,7},{7,8},{8,9},{9,10},{10,1... | collective-permute-start | bytes 737288 | tf_op jit(solution)/shard_map/ppermute | solution.py:265
  7.2 5.5 %collective-permute-start.1 = (bf16[10,96,128]{2,1,0:T(8,128)(2,1)S(1)}, bf16[10,96,128]{2,1,0:T(8,128)(2,1)S(1)}, u32[]{:S(2)}, u32[]{:S(2)}) collective-permute-start(bf16[10,96,128]{2,1,0:T(8,128)(2,1)S(1)} %pad_maximum_fusion.own_ref), channel_id=1, source_target_pairs={{1,0},{2,1},{3,2},{4,3},{5,4},{6,5},{7,6},{8,7},{9,8},{10,9},{11,1... | collective-permute-start | bytes 737288 | tf_op jit(solution)/shard_map/ppermute | solution.py:266
  12.8 1.2 %copy.34 = bf16[27,4,24,24]{3,2,1,0:T(8,128)(2,1)S(1)} copy(bf16[27,4,24,24]{0,3,2,1:T(8,128)(2,1)S(1)} %copy-done.1) | data formatting | bytes 248832 | tf_op args[1]
  14.8 0.7 pad.7.fw_ref
  15.5 0.7 copy-done.3
  16.3 8.1 %main.1 = (bf16[4608,128]{1,0:T(8,128)(2,1)}, bf16[2592,128]{1,0:T(8,128)(2,1)}, bf16[4,96,1024]{2,1,0:T(8,128)(2,1)}) custom-call(f32[1]{0:T(128)} %bitcast.inner_ref, bf16[10,96,128]{2,1,0:T(8,128)(2,1)} %copy-done.3, bf16[10,96,128]{2,1,0:T(8,128)(2,1)} %copy-done.2, bf16[10,96,128]{2,1,0:T(8,128)(2,1)} %copy-done.4, bf16[288,256]{1,0:T(8,128)(2,1)} %pad.7.fw_ref, ...), custom_call_target="tpu_custom_call" | custom-call | tf_op jit(solution)/shard_map/main/pallas_call | solution.py:274
  24.4 28.0 %all_to_all.15 = bf16[64,72,128]{2,1,0:T(8,128)(2,1)S(1)} all-to-all(bf16[64,72,128]{2,1,0:T(8,128)(2,1)} %bitcast.39), channel_id=1, replica_groups=mesh['xh'=2,'zh'=8,'zl'=2,'xl'=2,'y'=4,'core'=2] {'xh','xl','y','core','..., dimensions={0} | all-to-all | bytes 2359296 | tf_op jit(solution)/shard_map/all_to_all | solution.py:293
  52.6 27.2 %all_to_all.16 = bf16[8,72,128]{2,1,0:T(8,128)(2,1)S(1)} all-to-all(bf16[8,72,128]{2,1,0:T(8,128)(2,1)S(1)} %broadcast_in_dim.7), channel_id=1, replica_groups=mesh['xh'=2,'zh'=8,'zl'=2,'xl'=2,'y'=4,'core'=2] {'zh'}, dimensions={0} | all-to-all | bytes 294912 | tf_op jit(solution)/shard_map/all_to_all | solution.py:253
  79.8 1.2 %broadcast_in_dim.8 = bf16[64,72,128]{2,1,0:T(8,128)(2,1)} broadcast(bf16[72,128]{1,0:T(8,128)(2,1)S(1)} %reduce_sum.25), dimensions={1,2} | broadcast | bytes 1198080 | tf_op jit(solution)/shard_map/broadcast_in_dim | solution.py:252
  81.0 8.4 %all-to-all-start.2 = ((bf16[64,72,128]{2,1,0:T(8,128)(2,1)}), bf16[64,72,128]{2,1,0:T(8,128)(2,1)S(1)}, u32[]{:S(2)}, u32[]{:S(2)}) async-start(bf16[64,72,128]{2,1,0:T(8,128)(2,1)} %broadcast_in_dim.8), calls=%async_computation.2 | async-start | bytes 2359296 | tf_op jit(solution)/shard_map/all_to_all | solution.py:253
  89.3 1.2 %copy.37 = bf16[27,4,24,24]{3,2,1,0:T(8,128)(2,1)S(1)} copy(bf16[27,4,24,24]{0,3,2,1:T(8,128)(2,1)S(1)} %copy-done.1) | data formatting | bytes 248832 | tf_op jit(solution)/shard_map/optimization_barrier | solution.py:294
  90.7 1.3 %copy.38 = bf16[3,4,24,9,24]{2,1,0,4,3:T(4,128)(2,1)S(1)} copy(bf16[3,4,24,9,24]{4,2,1,3,0:T(8,128)(2,1)S(1)} %bitcast.35) | data formatting | bytes 248832 | tf_op jit(solution)/shard_map/transpose | solution.py:296
  92.0 0.4 reshape.71
  92.5 0.7 pad.8.fw_ref
  93.2 4.3 %tail.1 = (bf16[192,128]{1,0:T(8,128)(2,1)}, bf16[2,96,512]{2,1,0:T(8,128)(2,1)}) custom-call(bf16[4,96,1024]{2,1,0:T(8,128)(2,1)} %get-tuple-element.10.g_ref, bf16[2592,128]{1,0:T(8,128)(2,1)} %get-tuple-element.11.wn_ref, bf16[2592,192]{1,0:T(8,128)(2,1)} %bitcast.38, bf16[288,256]{1,0:T(8,128)(2,1)} %pad.8.fw_ref, ...), custom_call_target="tpu_custom_call" | custom-call | flops 1000000000 | bytes 4000000 | tf_op jit(solution)/shard_map/tail/pallas_call | solution.py:299
  97.4 1.0 reshape.73
  98.4 0.8 copy.45
  99.2 8.8 %all-to-all-done.2 = bf16[64,72,128]{2,1,0:T(8,128)(2,1)S(1)} async-done(((bf16[64,72,128]{2,1,0:T(8,128)(2,1)}), bf16[64,72,128]{2,1,0:T(8,128)(2,1)S(1)}, u32[]{:S(2)}, u32[]{:S(2)}) %all-to-all-start.2) | async-done | bytes 1179680 | tf_op jit(solution)/shard_map/all_to_all | solution.py:253
  108.0 1.0 copy-done
  109.0 3.4 %finish.1 = f32[2592,192]{1,0:T(8,128)} custom-call(bf16[4608,128]{1,0:T(8,128)(2,1)} %bitcast.33), custom_call_target="tpu_custom_call" | custom-call | tf_op jit(solution)/shard_map/finish/pallas_call | solution.py:320
  112.4 0.9 slice.9
  113.4 1.5 %reshape.77 = f32[4,24,24,27]{3,2,1,0:T(8,128)} reshape(f32[96,648]{1,0:T(8,128)S(1)} %convert_multiply_fusion) | data formatting | bytes 497664 | tf_op jit(solution)/shard_map/reshape | solution.py:331
  (21 shorter events, 1.4 us)
Async XLA Ops:
  0.6 12.1 %copy-start.1 = (bf16[27,4,24,24]{0,3,2,1:T(8,128)(2,1)S(1)}, bf16[27,4,24,24]{0,3,2,1:T(8,128)(2,1)}, u32[]{:S(2)}) copy-start(bf16[27,4,24,24]{0,3,2,1:T(8,128)(2,1)} %param.8) | copy-start | bytes 373252
  2.6 11.6 %copy-start.2 = (bf16[10,96,128]{2,1,0:T(8,128)(2,1)}, bf16[10,96,128]{2,1,0:T(8,128)(2,1)S(1)}, u32[]{:S(2)}) copy-start(bf16[10,96,128]{2,1,0:T(8,128)(2,1)S(1)} %pad_maximum_fusion.own_ref) | copy-start | bytes 737284
  2.6 12.8 %collective-permute-start = (bf16[10,96,128]{2,1,0:T(8,128)(2,1)S(1)}, bf16[10,96,128]{2,1,0:T(8,128)(2,1)S(1)}, u32[]{:S(2)}, u32[]{:S(2)}) collective-permute-start(bf16[10,96,128]{2,1,0:T(8,128)(2,1)S(1)} %pad_maximum_fusion.own_ref), channel_id=1, source_target_pairs={{0,1},{1,2},{2,3},{3,4},{4,5},{5,6},{6,7},{7,8},{8,9},{9,10},{10,1... | collective-permute-start | bytes 737288 | tf_op jit(solution)/shard_map/ppermute | solution.py:265
  7.2 8.2 %collective-permute-start.1 = (bf16[10,96,128]{2,1,0:T(8,128)(2,1)S(1)}, bf16[10,96,128]{2,1,0:T(8,128)(2,1)S(1)}, u32[]{:S(2)}, u32[]{:S(2)}) collective-permute-start(bf16[10,96,128]{2,1,0:T(8,128)(2,1)S(1)} %pad_maximum_fusion.own_ref), channel_id=1, source_target_pairs={{1,0},{2,1},{3,2},{4,3},{5,4},{6,5},{7,6},{8,7},{9,8},{10,9},{11,1... | collective-permute-start | bytes 737288 | tf_op jit(solution)/shard_map/ppermute | solution.py:266
  15.5 0.7 copy-start.3
  15.5 0.8 copy-start.4
  81.0 27.0 %all-to-all-start.2 = ((bf16[64,72,128]{2,1,0:T(8,128)(2,1)}), bf16[64,72,128]{2,1,0:T(8,128)(2,1)S(1)}, u32[]{:S(2)}, u32[]{:S(2)}) async-start(bf16[64,72,128]{2,1,0:T(8,128)(2,1)} %broadcast_in_dim.8), calls=%async_computation.2 | async-start | bytes 2359296 | tf_op jit(solution)/shard_map/all_to_all | solution.py:253
  108.0 1.0 copy-start

commit v3 on v2

--- a/solution.py
+++ b/solution.py
@@ -1,3 +1,4 @@
+import functools
 import math
 
 import jax
@@ -11,7 +12,7 @@
 
 SPACE = ("xl", "y", "core")
 DP = ("xh", "zh", "zl")
-NEAR = ("xh", "xl", "y", "core", "zl")
+NEAR = ("xh", "xl", "y", "zl")
 F32 = jnp.float32
 BF16 = jnp.bfloat16
 
@@ -19,10 +20,13 @@
 PG = 24
 WIN = 9 * CH
 LANES = 128
-PIECES = 64
-ROWS = 4608
-S_ROWS = 3 * (WIN + WIN // 2)
-PIECE = ROWS // PIECES
+HALF = 27 * CH // 2
+LEFT, RIGHT = 656, HALF - 656
+S_ROWS = HALF + LEFT
+F_ROWS = 3 * CH
+PIECES = 32
+PIECE = 72
+ROWS = PIECES * PIECE
 
 
 def dot(a, b):
@@ -80,20 +84,28 @@
 
 
 def expand(narrow, fold, mask):
-    return (dot(narrow, fold) * mask).astype(BF16)
+    return (dot(narrow, fold[: 9 * PG]) * mask).astype(BF16)
 
 
 def main_kernel(
-    inner_ref, low_ref, own_ref, high_ref, fw_ref, fold_ref, mask_ref, order_ref, w2_ref,
-    comm_ref, wn_ref, g_ref, xs, w1, pre_ref, xc_ref, gs,
+    inner_ref, core_ref, low_hbm, own_ref, high_hbm, fw_ref, fold_ref, mask_ref, order_ref, w2_ref,
+    mine_ref, other_ref, wn_ref, g_ref, xs, w1, pre_ref, xc_ref, gs, low_ref, high_ref, fg, sems,
 ):
     inner = inner_ref[0]
+    core = core_ref[0]
+    fetch_low = pltpu.make_async_copy(low_hbm, low_ref, sems.at[0])
+    fetch_high = pltpu.make_async_copy(high_hbm, high_ref, sems.at[1])
+    fetch_low.start()
+    fetch_high.start()
     split = split_matrix()
     mask = mask_ref[...].astype(F32)
     for a in range(3):
         w1[pl.ds(a * CH, CH), :] = expand(fw_ref[pl.ds(a * CH, CH), :], fold_ref[...], mask)
-    for e in range(6):
+    for e in (2, 3, 0, 1, 4, 5):
         slab = (low_ref, own_ref, high_ref)[e // 2]
+        if e == 0:
+            fetch_low.wait()
+            fetch_high.wait()
         tiles = []
         for y in range(2):
             at = 4 * (e % 2) + 2 * y
@@ -132,16 +144,14 @@
     both = jnp.concatenate(
         [jnp.concatenate([rest, none], axis=1), jnp.concatenate([none, rest], axis=1)], axis=0
     )
-    half = WIN // 2
-    for a in range(3):
-        at = a * (WIN + half)
-        comm_ref[pl.ds(at, WIN), :] = dot_nt(wn_ref[pl.ds(a * WIN, WIN), :], cot[:LANES]).astype(
-            BF16
-        )
-        pairs = jnp.concatenate(
-            [wn_ref[pl.ds(a * WIN, half), :], wn_ref[pl.ds(a * WIN + half, half), :]], axis=1
-        )
-        comm_ref[pl.ds(at + WIN, half), :] = dot_nt(pairs, both).astype(BF16)
+    for out_ref, half in ((mine_ref, core), (other_ref, 1 - core)):
+        base = pl.multiple_of(half * HALF, 16)
+        out_ref[pl.ds(0, HALF), :] = dot_nt(wn_ref[pl.ds(base, HALF), :], cot[:LANES]).astype(BF16)
+        left = wn_ref[pl.ds(base, LEFT), :]
+        right = wn_ref[pl.ds(base + LEFT, RIGHT), :]
+        right = jnp.concatenate([right, jnp.zeros((LEFT - RIGHT, LANES), BF16)], axis=0)
+        pairs = jnp.concatenate([left, right], axis=1)
+        out_ref[pl.ds(HALF, LEFT), :] = dot_nt(pairs, both).astype(BF16)
     above = jnp.concatenate([high_ref[8], high_ref[9]], axis=0)
     below = jnp.concatenate([low_ref[8], low_ref[9]], axis=0)
     with_above = jnp.concatenate([cot, above], axis=1)
@@ -188,12 +198,18 @@
     ]
     ordered = dot(jnp.concatenate(narrow, axis=1), order_ref[...]).astype(BF16)
     for k in range(6):
-        comm_ref[pl.ds(S_ROWS + k * CH, CH), :] = ordered[:, k * LANES : (k + 1) * LANES]
-    left = ROWS - S_ROWS - 6 * CH
-    comm_ref[pl.ds(ROWS - left, left), :] = jnp.zeros((left, LANES), BF16)
-
-
-def tail_kernel(g_ref, wn_ref, w2_ref, fw_ref, fold_ref, mask_ref, feat_ref, vg_ref, gs, w1, acc):
+        fg[pl.ds(k * CH, CH), :] = ordered[:, k * LANES : (k + 1) * LANES]
+    for out_ref, half in ((mine_ref, core), (other_ref, 1 - core)):
+        base = pl.multiple_of(half * F_ROWS, 16)
+        out_ref[pl.ds(S_ROWS, F_ROWS), :] = fg[pl.ds(base, F_ROWS), :]
+        left = ROWS - S_ROWS - F_ROWS
+        out_ref[pl.ds(ROWS - left, left), :] = jnp.zeros((left, LANES), BF16)
+
+
+def tail_kernel(
+    after_ref, g_ref, wn_ref, w2_ref, fw_ref, fold_ref, mask_ref, feat_ref, vg_ref, done_ref, gs, w1, acc,
+):
+    done_ref[...] = jnp.zeros((1, LANES), F32)
     mask = mask_ref[...].astype(F32)
     for a in range(3):
         w1[pl.ds(a * CH, CH), :] = expand(fw_ref[pl.ds(a * CH, CH), :], fold_ref[...], mask)
@@ -220,12 +236,29 @@
             vg_ref[out, :, cut] = dot(acc[out, :, cut].astype(BF16), merge).astype(BF16)
 
 
-def finish_kernel(factor, all_ref, out_ref):
-    half = WIN // 2
-    out_ref[:, pl.ds(0, LANES)] = all_ref[pl.ds(0, WIN), :].astype(F32) * factor
-    rest = all_ref[pl.ds(WIN, half), :].astype(F32) * factor
-    out_ref[pl.ds(0, half), pl.ds(LANES, 64)] = rest[:, :64]
-    out_ref[pl.ds(half, half), pl.ds(LANES, 64)] = rest[:, 64:]
+def finish_kernel(factor, half_ref, all_ref, *refs):
+    out_ref = refs[-1]
+    out_ref[:, pl.ds(0, LANES)] = all_ref[pl.ds(0, HALF), :].astype(F32) * factor
+    rest = all_ref[pl.ds(HALF, LEFT), :].astype(F32) * factor
+    out_ref[pl.ds(0, LEFT), pl.ds(LANES, 64)] = rest[:, :64]
+    out_ref[pl.ds(LEFT, RIGHT), pl.ds(LANES, 64)] = rest[:RIGHT, 64:]
+
+
+def finish(factor, half, rows, params, before=None):
+    return pl.pallas_call(
+        functools.partial(finish_kernel, factor),
+        out_shape=jax.ShapeDtypeStruct((27 * CH, 192), F32),
+        grid_spec=pltpu.PrefetchScalarGridSpec(
+            num_scalar_prefetch=1,
+            grid=(1,),
+            in_specs=[pl.BlockSpec((ROWS, LANES), lambda k, half: (0, 0))]
+            + ([] if before is None else [pl.BlockSpec(memory_space=pl.ANY)]),
+            out_specs=pl.BlockSpec((HALF, 192), lambda k, half: (half[0], 0)),
+        ),
+        input_output_aliases={} if before is None else {2: 0},
+        compiler_params=params,
+        name="finish",
+    )(half, rows, *([] if before is None else [before]))
 
 
 def constants():
@@ -256,6 +289,7 @@
 def shards(volume, first_weight, second_weight, out_cotangent):
     vmem = pl.BlockSpec(memory_space=pltpu.VMEM)
     smem = pl.BlockSpec(memory_space=pltpu.SMEM)
+    anywhere = pl.BlockSpec(memory_space=pl.ANY)
     params = pltpu.CompilerParams(vmem_limit_bytes=56 * 1024 * 1024)
     count = lax.axis_size(SPACE)
     up = [(i, i + 1) for i in range(count - 1)]
@@ -264,46 +298,54 @@
     own = jnp.concatenate([planes, out_cotangent.reshape(2, CH, LANES)], axis=0)
     low = lax.ppermute(own, SPACE, up)
     high = lax.ppermute(own, SPACE, down)
+    core = lax.axis_index("core").astype(jnp.int32).reshape(1)
     inner = jnp.where(lax.axis_index(SPACE) > 0, 1.0, 0.0).astype(F32).reshape(1)
     fold, mask, order = constants()
-    wide = ((0, 0), (0, 256 - 9 * PG))
-    forward_weight = jnp.pad(
-        first_weight.reshape(3, 9, 4, PG, PG).transpose(0, 2, 4, 1, 3).reshape(3 * CH, 9 * PG), wide
+    forward_weight = (
+        first_weight.reshape(3, 9, 4, PG, PG).transpose(0, 2, 4, 1, 3).reshape(3 * CH, 9 * PG)
     )
     w2 = second_weight.reshape(27 * CH, 192)
-    comm, windows, grads = pl.pallas_call(
+    mine, other, windows, grads = pl.pallas_call(
         main_kernel,
         out_shape=(
+            jax.ShapeDtypeStruct((ROWS, LANES), BF16),
             jax.ShapeDtypeStruct((ROWS, LANES), BF16),
             jax.ShapeDtypeStruct((27 * CH, LANES), BF16),
             jax.ShapeDtypeStruct((4, CH, 8 * LANES), BF16),
         ),
-        in_specs=[smem] + [vmem] * 8,
-        out_specs=(vmem,) * 3,
+        in_specs=[smem, smem, anywhere, vmem, anywhere] + [vmem] * 5,
+        out_specs=(vmem,) * 4,
         scratch_shapes=[
             pltpu.VMEM((6, WIN, 512), BF16),
             pltpu.VMEM((3 * CH, WIN), BF16),
             pltpu.VMEM((4, CH, 512), F32),
             pltpu.VMEM((4, CH, 512), BF16),
             pltpu.VMEM((2, WIN, 512), BF16),
+            pltpu.VMEM((10, CH, LANES), BF16),
+            pltpu.VMEM((10, CH, LANES), BF16),
+            pltpu.VMEM((6 * CH, LANES), BF16),
+            pltpu.SemaphoreType.DMA((2,)),
         ],
         compiler_params=params,
         name="main",
-    )(inner, low, own, high, forward_weight, fold, mask, order, w2)
-    parts = lax.all_to_all(comm.reshape(PIECES, PIECE, LANES), NEAR, 0, 0, tiled=True)
-    late_weight = lax.optimization_barrier((first_weight, comm))[0]
-    backward_weight = jnp.pad(
-        late_weight[::-1].reshape(3, 9, 4, PG, PG).transpose(0, 2, 3, 1, 4).reshape(3 * CH, 9 * PG),
-        wide,
-    )
-    feat, vgrad = pl.pallas_call(
+    )(inner, core, low, own, high, forward_weight, fold, mask, order, w2)
+    swap = [(0, 1), (1, 0)]
+    got = lax.ppermute(other, "core", swap)
+    chip = (mine.astype(F32) + got.astype(F32)).astype(BF16)
+    parts = lax.all_to_all(chip.reshape(PIECES, PIECE, LANES), NEAR, 0, 0, tiled=True)
+    late_weight = lax.optimization_barrier((first_weight, windows))[0]
+    backward_weight = (
+        late_weight[::-1].reshape(3, 9, 4, PG, PG).transpose(0, 2, 3, 1, 4).reshape(3 * CH, 9 * PG)
+    )
+    feat, vgrad, done = pl.pallas_call(
         tail_kernel,
         out_shape=(
             jax.ShapeDtypeStruct((192, LANES), BF16),
             jax.ShapeDtypeStruct((2, CH, 512), BF16),
+            jax.ShapeDtypeStruct((1, LANES), F32),
         ),
-        in_specs=[vmem] * 6,
-        out_specs=(vmem,) * 2,
+        in_specs=[anywhere] + [vmem] * 6,
+        out_specs=(vmem,) * 3,
         scratch_shapes=[
             pltpu.VMEM((4, WIN, 512), BF16),
             pltpu.VMEM((3 * CH, WIN), BF16),
@@ -312,21 +354,17 @@
         compiler_params=params,
         cost_estimate=pl.CostEstimate(flops=10**9, bytes_accessed=4 * 10**6, transcendentals=0),
         name="tail",
-    )(grads, windows, w2, backward_weight, fold, mask)
-    piece = sum_pieces(to_all(sum_pieces(parts), "zh", lax.axis_size("zh")))
-    every = to_all(piece, NEAR, PIECES).reshape(ROWS, LANES)
+    )(chip, grads, windows, w2, backward_weight, fold, mask)
+    piece = (jnp.sum(parts.astype(F32), axis=0) + done).astype(BF16)
+    piece = sum_pieces(to_all(piece, "zh", lax.axis_size("zh")))
+    own_half = to_all(piece, NEAR, PIECES).reshape(ROWS, LANES)
+    other_half = lax.ppermute(own_half, "core", swap)
     factor = 1.0 / math.sqrt(lax.axis_size(DP) * lax.axis_size(SPACE) * LANES)
-    block = WIN + WIN // 2
-    second_grad = pl.pallas_call(
-        lambda a, b: finish_kernel(factor, a, b),
-        out_shape=jax.ShapeDtypeStruct((27 * CH, 192), F32),
-        grid=(3,),
-        in_specs=[pl.BlockSpec((block, LANES), lambda k: (k, 0))],
-        out_specs=pl.BlockSpec((WIN, 192), lambda k: (k, 0)),
-        compiler_params=params,
-        name="finish",
-    )(every)
-    narrow = every[S_ROWS : S_ROWS + 6 * CH].reshape(6, CH, LANES).transpose(1, 0, 2)
+    second_grad = finish(factor, core, own_half, params)
+    second_grad = finish(factor, 1 - core, other_half, params, second_grad)
+    cut = slice(S_ROWS, S_ROWS + F_ROWS)
+    halves = [jnp.where(core == h, own_half[cut], other_half[cut]) for h in (0, 1)]
+    narrow = jnp.concatenate([t.reshape(3, CH, LANES) for t in halves]).transpose(1, 0, 2)
     narrow = narrow.reshape(CH, 6 * LANES)[:, : 27 * PG].astype(F32) * factor
     first_grad = narrow.reshape(4, PG, PG, 27).transpose(3, 0, 1, 2)
     features = feat.reshape(out_cotangent.shape)

time: 115 us -> 110 us (0.957)
  blocking collectives: 55.2 us -> 41.5 us
  starting transfers between devices: 18.5 us -> 27.2 us
  local copies, waits for them, and re-layouts: 14.8 us -> 10.9 us
  other arithmetic: 1.07 us -> 4.74 us
  waiting for transfers between devices: 8.78 us -> 6.58 us
  Pallas kernels: 15.7 us -> 17.7 us
    all_to_all x1 -> x0, blocking collectives: 28 us -> none  [shards(): lax.all_to_all(comm.reshape(PIECES, PIECE, LANES), NEAR, 0, 0, tiled=True)]
    all_to_all x1 -> x2, blocking collectives: 27.2 us -> 41.5 us  [to_all(): return lax.all_to_all(copies, axes, 0, 0, tiled=True)]
    ppermute x0 -> x2, starting transfers between devices: none -> 8.31 us  [the longest x1 6.39 us: shards(): other_half = lax.ppermute(own_half, 'core', swap)]
    all_to_all x1, waiting for transfers between devices: 8.78 us -> 4.39 us  [shards(): lax.all_to_all(chip.reshape(PIECES, PIECE, LANES), NEAR, 0, 0, tiled=True)]
    convert_element_type x0 -> x2, other arithmetic: none -> 2.72 us  [the longest x1 2.04 us: shards(): chip = (mine.astype(F32) + got.astype(F32)).astype(BF16)]
    ppermute x0 -> x2, waiting for transfers between devices: none -> 2.18 us  [the longest x1 2.18 us: shards(): got = lax.ppermute(other, 'core', swap)]
    pad x2 -> x0, local copies, waits for them, and re-layouts: 1.36 us -> none  [the longest x1 0.68 us: shards(): jnp.pad(first_weight.reshape(3, 9, 4, PG, PG).transpose(0, 2, 4, 1, 3).re...]
    pallas_call x1 -> x2, Pallas kernels: 3.37 us -> 4.59 us  [finish(): pl.pallas_call(functools.partial(finish_kernel, factor), out_shape=jax.Sh...]
  transfers between devices with their start and end apart: 3 -> 5, of which waited for: 1 -> 2; matrix products, arithmetic and copies ran while one was open for 7% -> 7% of each run, Pallas kernels for 4% -> 6%
where the time goes in v3:
time: 110 us
  blocking collectives  41.5 us (38%)
  starting transfers between devices  27.2 us (25%)
  Pallas kernels  17.7 us (16%)
  local copies, waits for them, and re-layouts  10.9 us (10%)
  waiting for transfers between devices  6.58 us (6%)
  other arithmetic  4.74 us (4%)
    all_to_all x2, blocking collectives, to_all(): return lax.all_to_all(copies, axes, 0, 0, tiled=True)  41.5 us
    pallas_call x1, Pallas kernels, shards(): pl.pallas_call(main_kernel, out_shape=(jax.ShapeDtypeStruct((ROWS, LANES)...  8.99 us
    all_to_all x1, starting transfers between devices, shards(): lax.all_to_all(chip.reshape(PIECES, PIECE, LANES), NEAR, 0, 0, tiled=True)  8.85 us
    ppermute x1, starting transfers between devices, shards(): other_half = lax.ppermute(own_half, 'core', swap)  6.39 us
    ppermute x1, starting transfers between devices, shards(): high = lax.ppermute(own, SPACE, down)  5.5 us
    ppermute x1, starting transfers between devices, shards(): low = lax.ppermute(own, SPACE, up)  4.59 us
    pallas_call x2, Pallas kernels, finish(): pl.pallas_call(functools.partial(finish_kernel, factor), out_shape=jax.Sh...  4.59 us
    all_to_all x1, waiting for transfers between devices, shards(): lax.all_to_all(chip.reshape(PIECES, PIECE, LANES), NEAR, 0, 0, tiled=True)  4.39 us
  transfers between devices with their start and end apart: 5, of which 2 were waited for; matrix products, arithmetic and copies ran while one was open for 7% of the time, Pallas kernels for 6%

profile of v3, /device:TPU:1, one launch (start us, length us, event | category | flops | bytes accessed | tf_op | source)
XLA Modules:
  0.0 109.6 jit_solution(11456252770098747268)
XLA Ops:
  0.6 1.1 %reshape.90 = bf16[96,2,2,2,128]{4,3,2,1,0:T(2,128)(2,1)S(1)} reshape(bf16[1,96,2,2,256]{4,3,2,1,0:T(2,128)(2,1)} %param.7) | data formatting | bytes 393216 | tf_op jit(solution)/shard_map/reshape | solution.py:297
  1.8 0.8 pad_maximum_fusion.own_ref
  2.6 4.6 %collective-permute-start = (bf16[10,96,128]{2,1,0:T(8,128)(2,1)S(1)}, bf16[10,96,128]{2,1,0:T(8,128)(2,1)S(1)}, u32[]{:S(2)}, u32[]{:S(2)}) collective-permute-start(bf16[10,96,128]{2,1,0:T(8,128)(2,1)S(1)} %pad_maximum_fusion.own_ref), channel_id=1, source_target_pairs={{0,1},{1,2},{2,3},{3,4},{4,5},{5,6},{6,7},{7,8},{8,9},{9,10},{10,1... | collective-permute-start | bytes 737288 | tf_op jit(solution)/shard_map/ppermute | solution.py:299
  7.2 5.5 %collective-permute-start.1 = (bf16[10,96,128]{2,1,0:T(8,128)(2,1)S(1)}, bf16[10,96,128]{2,1,0:T(8,128)(2,1)S(1)}, u32[]{:S(2)}, u32[]{:S(2)}) collective-permute-start(bf16[10,96,128]{2,1,0:T(8,128)(2,1)S(1)} %pad_maximum_fusion.own_ref), channel_id=1, source_target_pairs={{1,0},{2,1},{3,2},{4,3},{5,4},{6,5},{7,6},{8,7},{9,8},{10,9},{11,1... | collective-permute-start | bytes 737288 | tf_op jit(solution)/shard_map/ppermute | solution.py:300
  12.8 1.2 %copy.27 = bf16[27,4,24,24]{3,2,1,0:T(8,128)(2,1)S(1)} copy(bf16[27,4,24,24]{0,3,2,1:T(8,128)(2,1)S(1)} %copy-done.1) | data formatting | bytes 248832 | tf_op args[1]
  14.6 0.8 copy.29.fw_ref
  16.2 9.0 %main.1 = (bf16[2304,128]{1,0:T(8,128)(2,1)}, bf16[2304,128]{1,0:T(8,128)(2,1)}, bf16[2592,128]{1,0:T(8,128)(2,1)}, bf16[4,96,1024]{2,1,0:T(8,128)(2,1)}) custom-call(f32[1]{0:T(128)} %bitcast.inner_ref, s32[1]{0:T(128)} %bitcast.1.core_ref.half_ref, bf16[10,96,128]{2,1,0:T(8,128)(2,1)} %copy-done.4, bf16[10,96,128]{2,1,0:T(8,128)(2,1)} %copy-done.2, ...), custom_call_target="tpu_custom_call" | custom-call | tf_op jit(solution)/shard_map/main/pallas_call | solution.py:308
  25.2 1.9 %collective-permute-start.2 = (bf16[2304,128]{1,0:T(8,128)(2,1)}, bf16[2304,128]{1,0:T(8,128)(2,1)S(1)}, u32[]{:S(2)}, u32[]{:S(2)}) collective-permute-start(bf16[2304,128]{1,0:T(8,128)(2,1)} %get-tuple-element.13), channel_id=1, source_target_pairs={{0,1},{1,0},{2,3},{3,2},{4,5},{5,4},{6,7},{7,6},{8,9},{9,8},{10,11... | collective-permute-start | bytes 1769480 | tf_op jit(solution)/shard_map/ppermute | solution.py:333
  27.1 2.2 %collective-permute-done.2 = bf16[2304,128]{1,0:T(8,128)(2,1)S(1)} collective-permute-done((bf16[2304,128]{1,0:T(8,128)(2,1)}, bf16[2304,128]{1,0:T(8,128)(2,1)S(1)}, u32[]{:S(2)}, u32[]{:S(2)}) %collective-permute-start.2) | collective-permute-done | bytes 589856 | tf_op jit(solution)/shard_map/ppermute | solution.py:333
  29.3 2.0 %add_convert_fusion.after_ref = bf16[2304,128]{1,0:T(8,128)(2,1)} fusion(bf16[2304,128]{1,0:T(8,128)(2,1)S(1)} %collective-permute-done.2, bf16[2304,128]{1,0:T(8,128)(2,1)} %get-tuple-element.12), kind=kLoop, calls=%fused_computation.1 | loop fusion | flops 1179648 | bytes 1769472 | tf_op jit(solution)/shard_map/convert_element_type | solution.py:334
  31.4 8.8 %all-to-all-start = ((bf16[32,72,128]{2,1,0:T(8,128)(2,1)}), bf16[32,72,128]{2,1,0:T(8,128)(2,1)S(1)}, u32[]{:S(2)}, u32[]{:S(2)}) async-start(bf16[32,72,128]{2,1,0:T(8,128)(2,1)} %bitcast.14), calls=%async_computation | async-start | bytes 1179648 | tf_op jit(solution)/shard_map/all_to_all | solution.py:335
  40.2 1.2 %copy.30 = bf16[27,4,24,24]{3,2,1,0:T(8,128)(2,1)S(1)} copy(bf16[27,4,24,24]{0,3,2,1:T(8,128)(2,1)S(1)} %copy-done.1) | data formatting | bytes 248832 | tf_op jit(solution)/shard_map/optimization_barrier | solution.py:336
  41.5 1.3 %copy.31 = bf16[3,4,24,9,24]{2,1,0,4,3:T(4,128)(2,1)S(1)} copy(bf16[3,4,24,9,24]{4,2,1,3,0:T(8,128)(2,1)S(1)} %bitcast.44) | data formatting | bytes 248832 | tf_op jit(solution)/shard_map/transpose | solution.py:338
  43.2 0.8 copy.32.fw_ref
  44.0 4.1 %tail.1 = (bf16[192,128]{1,0:T(8,128)(2,1)}, bf16[2,96,512]{2,1,0:T(8,128)(2,1)}, f32[1,128]{1,0:T(1,128)}) custom-call(bf16[2304,128]{1,0:T(8,128)(2,1)} %add_convert_fusion.after_ref, bf16[4,96,1024]{2,1,0:T(8,128)(2,1)} %get-tuple-element.14.g_ref, bf16[2592,128]{1,0:T(8,128)(2,1)} %get-tuple-element.15.wn_ref, bf16[2592,192]{1,0:T(8,128)(2,1)} %bitcast.39, ...), custom_call_target="tpu_custom_call" | custom-call | flops 1000000000 | bytes 4000000 | tf_op jit(solution)/shard_map/tail/pallas_call | solution.py:340
  48.1 4.4 %all-to-all-done = bf16[32,72,128]{2,1,0:T(8,128)(2,1)S(1)} async-done(((bf16[32,72,128]{2,1,0:T(8,128)(2,1)}), bf16[32,72,128]{2,1,0:T(8,128)(2,1)S(1)}, u32[]{:S(2)}, u32[]{:S(2)}) %all-to-all-start) | async-done | bytes 589856 | tf_op jit(solution)/shard_map/all_to_all | solution.py:335
  53.3 27.3 %all_to_all.15 = bf16[8,72,128]{2,1,0:T(8,128)(2,1)S(1)} all-to-all(bf16[8,72,128]{2,1,0:T(8,128)(2,1)S(1)} %broadcast_in_dim.30), channel_id=1, replica_groups=mesh['xh'=2,'zh'=8,'zl'=2,'xl'=2,'y'=4,'core'=2] {'zh'}, dimensions={0} | all-to-all | bytes 294912 | tf_op jit(solution)/shard_map/all_to_all | solution.py:286
  80.7 14.2 %all_to_all.16 = bf16[32,72,128]{2,1,0:T(8,128)(2,1)S(1)} all-to-all(bf16[32,72,128]{2,1,0:T(8,128)(2,1)S(1)} %broadcast_in_dim.31), channel_id=1, replica_groups=mesh['xh'=2,'zh'=8,'zl'=2,'xl'=2,'y'=4,'core'=2] {'xh','xl','y','zl'}, dimensions={0} | all-to-all | bytes 1179648 | tf_op jit(solution)/shard_map/all_to_all | solution.py:286
  95.0 6.4 %collective-permute-start.3 = (bf16[2304,128]{1,0:T(8,128)(2,1)S(1)}, bf16[2304,128]{1,0:T(8,128)(2,1)S(1)}, u32[]{:S(2)}, u32[]{:S(2)}) collective-permute-start(bf16[2304,128]{1,0:T(8,128)(2,1)S(1)} %bitcast.40), channel_id=1, source_target_pairs={{0,1},{1,0},{2,3},{3,2},{4,5},{5,4},{6,7},{7,6},{8,9},{9,8},{10,11... | collective-permute-start | bytes 1769480 | tf_op jit(solution)/shard_map/ppermute | solution.py:361
  101.4 0.8 copy.39
  102.3 2.3 %finish.2.refs_0_ = f32[2592,192]{1,0:T(8,128)} custom-call(s32[1]{0:T(128)} %bitcast.1.core_ref.half_ref, bf16[2304,128]{1,0:T(8,128)(2,1)} %bitcast.41), custom_call_target="tpu_custom_call" | custom-call | tf_op jit(solution)/shard_map/finish/pallas_call | solution.py:248
  104.6 0.9 broadcast_select_fusion.1
  105.8 1.5 %reshape.105 = f32[4,24,24,27]{3,2,1,0:T(8,128)} reshape(f32[96,648]{1,0:T(8,128)S(1)} %convert_multiply_fusion) | data formatting | bytes 497664 | tf_op jit(solution)/shard_map/reshape | solution.py:369
  107.3 2.3 %finish.3 = f32[2592,192]{1,0:T(8,128)} custom-call(s32[1]{0:T(128)S(6)} %sub.3.half_ref, bf16[2304,128]{1,0:T(8,128)(2,1)} %copy-done.3, f32[2592,192]{1,0:T(8,128)} %finish.2.refs_0_), custom_call_target="tpu_custom_call", output_to_operand_aliasing={{}: (2, {})} | custom-call | tf_op jit(solution)/shard_map/finish/pallas_call | solution.py:248
  (33 shorter events, 3.1 us)
Async XLA Ops:
  0.6 12.1 %copy-start.1 = (bf16[27,4,24,24]{0,3,2,1:T(8,128)(2,1)S(1)}, bf16[27,4,24,24]{0,3,2,1:T(8,128)(2,1)}, u32[]{:S(2)}) copy-start(bf16[27,4,24,24]{0,3,2,1:T(8,128)(2,1)} %param.8) | copy-start | bytes 373252
  2.6 11.6 %copy-start.2 = (bf16[10,96,128]{2,1,0:T(8,128)(2,1)}, bf16[10,96,128]{2,1,0:T(8,128)(2,1)S(1)}, u32[]{:S(2)}) copy-start(bf16[10,96,128]{2,1,0:T(8,128)(2,1)S(1)} %pad_maximum_fusion.own_ref) | copy-start | bytes 737284
  2.6 12.8 %collective-permute-start = (bf16[10,96,128]{2,1,0:T(8,128)(2,1)S(1)}, bf16[10,96,128]{2,1,0:T(8,128)(2,1)S(1)}, u32[]{:S(2)}, u32[]{:S(2)}) collective-permute-start(bf16[10,96,128]{2,1,0:T(8,128)(2,1)S(1)} %pad_maximum_fusion.own_ref), channel_id=1, source_target_pairs={{0,1},{1,2},{2,3},{3,4},{4,5},{5,6},{6,7},{7,8},{8,9},{9,10},{10,1... | collective-permute-start | bytes 737288 | tf_op jit(solution)/shard_map/ppermute | solution.py:299
  7.2 8.2 %collective-permute-start.1 = (bf16[10,96,128]{2,1,0:T(8,128)(2,1)S(1)}, bf16[10,96,128]{2,1,0:T(8,128)(2,1)S(1)}, u32[]{:S(2)}, u32[]{:S(2)}) collective-permute-start(bf16[10,96,128]{2,1,0:T(8,128)(2,1)S(1)} %pad_maximum_fusion.own_ref), channel_id=1, source_target_pairs={{1,0},{2,1},{3,2},{4,3},{5,4},{6,5},{7,6},{8,7},{9,8},{10,9},{11,1... | collective-permute-start | bytes 737288 | tf_op jit(solution)/shard_map/ppermute | solution.py:300
  15.4 0.7 copy-start.4
  15.4 0.8 copy-start.5
  25.2 4.1 %collective-permute-start.2 = (bf16[2304,128]{1,0:T(8,128)(2,1)}, bf16[2304,128]{1,0:T(8,128)(2,1)S(1)}, u32[]{:S(2)}, u32[]{:S(2)}) collective-permute-start(bf16[2304,128]{1,0:T(8,128)(2,1)} %get-tuple-element.13), channel_id=1, source_target_pairs={{0,1},{1,0},{2,3},{3,2},{4,5},{5,4},{6,7},{7,6},{8,9},{9,8},{10,11... | collective-permute-start | bytes 1769480 | tf_op jit(solution)/shard_map/ppermute | solution.py:333
  31.4 21.2 %all-to-all-start = ((bf16[32,72,128]{2,1,0:T(8,128)(2,1)}), bf16[32,72,128]{2,1,0:T(8,128)(2,1)S(1)}, u32[]{:S(2)}, u32[]{:S(2)}) async-start(bf16[32,72,128]{2,1,0:T(8,128)(2,1)} %bitcast.14), calls=%async_computation | async-start | bytes 1179648 | tf_op jit(solution)/shard_map/all_to_all | solution.py:335
  53.3 48.1 %copy-start.6 = (bf16[2,96,512]{2,1,0:T(8,128)(2,1)S(1)}, bf16[2,96,512]{2,1,0:T(8,128)(2,1)}, u32[]{:S(2)}) copy-start(bf16[2,96,512]{2,1,0:T(8,128)(2,1)} %get-tuple-element.18) | copy-start | bytes 589828
  95.0 7.3 %copy-start = (bf16[32,72,128]{2,1,0:T(8,128)(2,1)}, bf16[32,72,128]{2,1,0:T(8,128)(2,1)S(1)}, u32[]{:S(2)}) copy-start(bf16[32,72,128]{2,1,0:T(8,128)(2,1)S(1)} %all_to_all.16) | copy-start | bytes 1769476
  95.0 9.6 %collective-permute-start.3 = (bf16[2304,128]{1,0:T(8,128)(2,1)S(1)}, bf16[2304,128]{1,0:T(8,128)(2,1)S(1)}, u32[]{:S(2)}, u32[]{:S(2)}) collective-permute-start(bf16[2304,128]{1,0:T(8,128)(2,1)S(1)} %bitcast.40), channel_id=1, source_target_pairs={{0,1},{1,0},{2,3},{3,2},{4,5},{5,4},{6,7},{7,6},{8,9},{9,8},{10,11... | collective-permute-start | bytes 1769480 | tf_op jit(solution)/shard_map/ppermute | solution.py:361
  104.6 2.7 %copy-start.3 = (bf16[2304,128]{1,0:T(8,128)(2,1)}, bf16[2304,128]{1,0:T(8,128)(2,1)S(1)}, u32[]{:S(2)}) copy-start(bf16[2304,128]{1,0:T(8,128)(2,1)S(1)} %collective-permute-done.3.all_ref) | copy-start | bytes 1769476

commit v4 on v3

v4 whole, which is shorter than its diff:
```python
import functools
import math

import jax
import jax.numpy as jnp
from jax import lax
from jax.experimental import pallas as pl
from jax.experimental.pallas import tpu as pltpu
from jax.sharding import Mesh
from jax.sharding import PartitionSpec as P

SPACE = ("xl", "y", "core")
DP = ("xh", "zh", "zl")
NEAR = ("xh", "xl", "y", "zl")
F32 = jnp.float32
BF16 = jnp.bfloat16

CH = 96
PG = 24
TAPS = 27
WIN = 9 * CH
LANES = 128
HALF = TAPS * CH // 2
PART = HALF // 3
LEFT, RIGHT = 224, PART - 224
F_PART = CH // 2
CHUNK = PART + LEFT + 2 * F_PART
PIECES = 32
PIECE = 72
ROWS = PIECES * PIECE


def dot(a, b):
    return lax.dot_general(a, b, (((1,), (0,)), ((), ())), preferred_element_type=F32)


def dot_nt(a, b):
    return lax.dot_general(a, b, (((1,), (1,)), ((), ())), preferred_element_type=F32)


def dot_tn(a, b):
    return lax.dot_general(a, b, (((0,), (0,)), ((), ())), preferred_element_type=F32)


def later(tile):
    lane = lax.broadcasted_iota(jnp.int32, tile.shape, 1)
    return jnp.where(lane == 0, 0.0, pltpu.roll(tile, 1, 1))


def earlier(tile):
    lane = lax.broadcasted_iota(jnp.int32, tile.shape, 1)
    return jnp.where(lane == LANES - 1, 0.0, pltpu.roll(tile, LANES - 1, 1))


def fill_windows(ref, tiles):
    zero = jnp.zeros((CH, LANES), BF16)
    for b in range(3):
        for c in range(3):
            rows = pl.ds((b * 3 + c) * CH, CH)
            for y in range(2):
                source = y + b - 1
                if source in (0, 1):
                    even, odd, odd_later, even_earlier = tiles[source]
                    pair = ((odd_later, even), (even, odd), (odd, even_earlier))[c]
                else:
                    pair = (zero, zero)
                for parity in range(2):
                    ref[rows, pl.ds((2 * y + parity) * LANES, LANES)] = pair[parity]


def ones_where(condition):
    return jnp.where(condition, 1.0, 0.0).astype(BF16)


def split_matrix():
    z = lax.broadcasted_iota(jnp.int32, (256, LANES), 0)
    k2 = 2 * lax.broadcasted_iota(jnp.int32, (256, LANES), 1)
    return jnp.concatenate([ones_where(z == k2 + off) for off in (0, 1, -1, 2)], axis=1)


def merge_matrix():
    lane = lax.broadcasted_iota(jnp.int32, (LANES, 256), 0)
    z = lax.broadcasted_iota(jnp.int32, (LANES, 256), 1)
    return jnp.concatenate([ones_where(z == 2 * lane + bit) for bit in (0, 1)], axis=0)


def quotient(value, divisor, bits):
    return (value * (2**bits // divisor + 1)) >> bits


def fold_matrix(rows):
    row = lax.broadcasted_iota(jnp.int32, (rows, WIN), 0)
    column = lax.broadcasted_iota(jnp.int32, (1, WIN), 1)
    target = quotient(column, CH, 16) * PG + column - PG * quotient(column, PG, 16)
    return ones_where(row == target)


def group_mask():
    row = lax.broadcasted_iota(jnp.int32, (CH, WIN), 0)
    column = lax.broadcasted_iota(jnp.int32, (1, WIN), 1)
    offset = row - PG * quotient(column - CH * quotient(column, CH, 16), PG, 16)
    return (offset >= 0) & (offset < PG)


def order_matrix():
    row = lax.broadcasted_iota(jnp.int32, (3 * 256, 6 * LANES), 0)
    column = lax.broadcasted_iota(jnp.int32, (1, 6 * LANES), 1)
    channel = quotient(column, TAPS, 16)
    tap = column - TAPS * channel
    plane = quotient(tap, 9, 16)
    target = plane * 256 + (8 - tap + 9 * plane) * PG + channel
    return ones_where((row == target) & (column < PG * TAPS))


def expand(narrow, fold, mask):
    return jnp.where(mask, dot(narrow, fold), 0.0).astype(BF16)


def main_kernel(
    stage, inner_ref, core_ref, low_hbm, own_hbm, high_hbm, fw_ref, w2_hbm,
    mine_hbm, other_hbm, wn_hbm, g_hbm,
    low_ref, own_ref, high_ref, w2_ref, mine_ref, other_ref, wn_ref, g_ref,
    xs, w1, pre_ref, xc_ref, gs, order_ref, fg, sems,
):
    inner = inner_ref[0]
    core = core_ref[0]
    fetches = [
        pltpu.make_async_copy(source, target, sems.at[i])
        for i, (source, target) in enumerate(
            ((own_hbm, own_ref), (low_hbm, low_ref), (high_hbm, high_ref), (w2_hbm, w2_ref))
        )
    ]
    for fetch in fetches:
        fetch.start()
    split = split_matrix()
    mask = group_mask()
    fold = fold_matrix(9 * PG)
    for a in range(3):
        w1[pl.ds(a * CH, CH), :] = expand(fw_ref[pl.ds(a * CH, CH), :], fold, mask)
    fetches[0].wait()
    for e in (2, 3, 0, 1, 4, 5):
        slab = (low_ref, own_ref, high_ref)[e // 2]
        if e == 0:
            fetches[1].wait()
            fetches[2].wait()
        tiles = []
        for y in range(2):
            at = 4 * (e % 2) + 2 * y
            parts = dot(jnp.concatenate([slab[at], slab[at + 1]], axis=1), split).astype(BF16)
            tiles.append([parts[:, q * LANES : (q + 1) * LANES] for q in range(4)])
            if 1 <= e <= 4:
                xc_ref[e - 1, :, pl.ds(y * 256, 256)] = parts[:, :256]
        fill_windows(xs.at[e], tiles)
    for e in range(6):
        first, last = max(0, e - 3), min(2, e)
        terms = dot(w1[pl.ds(first * CH, (last - first + 1) * CH), :], xs[e])
        for a in range(first, last + 1):
            term = terms[(a - first) * CH : (a - first + 1) * CH]
            j = e - a
            if a == 0:
                pre_ref[j] = term
            else:
                pre_ref[j] += term
    zero = jnp.zeros((CH, LANES), BF16)
    for a in range(3):
        for c in range(3):
            wn_ref[pl.ds((9 * a + c) * CH, CH), :] = zero
        for y in range(2):
            value = pre_ref[a, :, pl.ds(y * 256, 256)]
            hidden = value * jax.nn.sigmoid(value)
            if a == 0:
                hidden = hidden * inner
            even, odd = hidden[:, :LANES], hidden[:, LANES:]
            base = (9 * a + 3 * (y + 1)) * CH
            wn_ref[pl.ds(base, CH), :] = later(odd).astype(BF16)
            wn_ref[pl.ds(base + CH, CH), :] = even.astype(BF16)
            wn_ref[pl.ds(base + 2 * CH, CH), :] = odd.astype(BF16)
    send_wn = pltpu.make_async_copy(wn_ref, wn_hbm, sems.at[0])
    send_wn.start()
    cot = jnp.concatenate([own_ref[8], own_ref[9]], axis=0)
    rest = cot[LANES:]
    none = jnp.zeros_like(rest)
    both = jnp.concatenate(
        [jnp.concatenate([rest, none], axis=1), jnp.concatenate([none, rest], axis=1)], axis=0
    )
    fill = jnp.zeros((LEFT - RIGHT, LANES), BF16)
    for out_ref, half in ((other_ref, 1 - core), (mine_ref, core)):
        for k in range(3):
            base = pl.multiple_of(half * HALF + k * PART, 16)
            wide = dot_nt(wn_ref[pl.ds(base, PART), :], cot[:LANES])
            out_ref[pl.ds(k * CHUNK, PART), :] = wide.astype(BF16)
            left = wn_ref[pl.ds(base, LEFT), :]
            right = jnp.concatenate([wn_ref[pl.ds(base + LEFT, RIGHT), :], fill], axis=0)
            pairs = jnp.concatenate([left, right], axis=1)
            out_ref[pl.ds(k * CHUNK + PART, LEFT), :] = dot_nt(pairs, both).astype(BF16)
    above = jnp.concatenate([high_ref[8], high_ref[9]], axis=0)
    below = jnp.concatenate([low_ref[8], low_ref[9]], axis=0)
    with_above = jnp.concatenate([cot, above], axis=1)
    with_below = jnp.concatenate([cot, below], axis=1)
    order_ref[...] = order_matrix()
    fetches[3].wait()
    spread = [
        dot(w2_ref[pl.ds((9 * a + 3) * CH, 6 * CH), :], with_below if a == 2 else with_above)
        for a in range(3)
    ]
    for j in range(4):
        sources = {0: ((0, 0), (2, 1)), 1: ((1, 0),), 2: ((2, 0), (0, 1)), 3: ((1, 1),)}[j]
        tiles = []
        for y in range(2):
            got = []
            for c in range(3):
                total = None
                for a, part in sources:
                    tile = spread[a][
                        (3 * y + c) * CH : (3 * y + c + 1) * CH, part * LANES : (part + 1) * LANES
                    ]
                    total = tile if total is None else total + tile
                got.append(total)
            even = got[1]
            odd = got[2] + earlier(got[0])
            value = pre_ref[j, :, pl.ds(y * 256, 256)]
            sigma = jax.nn.sigmoid(value)
            slope = sigma * (1.0 + value * (1.0 - sigma))
            if j == 0:
                slope = slope * inner
            even = even * slope[:, :LANES]
            odd = odd * slope[:, LANES:]
            tiles.append([t.astype(BF16) for t in (even, odd, later(odd), earlier(even))])
            for q in range(4):
                g_ref[j, :, pl.ds((4 * y + q) * LANES, LANES)] = tiles[y][q]
        if j in (1, 2):
            fill_windows(gs.at[j - 1], tiles)
    send_g = pltpu.make_async_copy(g_ref, g_hbm, sems.at[1])
    send_g.start()
    taps = None
    for j in (1, 2):
        planes = jnp.concatenate([xc_ref[j - 1], xc_ref[j], xc_ref[j + 1]], axis=0)
        term = dot_nt(planes, gs[j - 1])
        taps = term if taps is None else taps + term
    fold = fold_matrix(256)
    kept = [jnp.where(mask, taps[a * CH : (a + 1) * CH], 0.0).astype(BF16) for a in range(3)]
    narrow = dot_nt(jnp.concatenate(kept, axis=0), fold).astype(BF16)
    ordered = dot(
        jnp.concatenate([narrow[a * CH : (a + 1) * CH] for a in range(3)], axis=1), order_ref[...]
    )
    fg[...] = ordered.astype(BF16)
    for out_ref, half in ((other_ref, 1 - core), (mine_ref, core)):
        base = pl.multiple_of(half * F_PART, 16)
        for k in range(6):
            at = (k // 2) * CHUNK + PART + LEFT + (k % 2) * F_PART
            out_ref[pl.ds(at, F_PART), :] = fg[pl.ds(base, F_PART), pl.ds(k * LANES, LANES)]
        out_ref[pl.ds(3 * CHUNK, ROWS - 3 * CHUNK), :] = jnp.zeros((ROWS - 3 * CHUNK, LANES), BF16)
    send_other = pltpu.make_async_copy(other_ref, other_hbm, sems.at[2])
    send_mine = pltpu.make_async_copy(mine_ref, mine_hbm, sems.at[3])
    send_other.start()
    send_mine.start()
    send_wn.wait()
    send_g.wait()
    send_other.wait()
    send_mine.wait()


def tail_kernel(
    after_hbm, g_hbm, wn_hbm, w2_hbm, fw_ref, feat_ref, vg_ref, done_ref,
    g_ref, wn_ref, w2_ref, gs, w1, acc, sems,
):
    fetches = [
        pltpu.make_async_copy(source, target, sems.at[i])
        for i, (source, target) in enumerate(
            ((g_hbm, g_ref), (wn_hbm, wn_ref), (w2_hbm, w2_ref))
        )
    ]
    for fetch in fetches:
        fetch.start()
    done_ref[...] = jnp.zeros((1, LANES), F32)
    mask = group_mask()
    fold = fold_matrix(9 * PG)
    for a in range(3):
        w1[pl.ds(a * CH, CH), :] = expand(fw_ref[pl.ds(a * CH, CH), :], fold, mask)
    fetches[0].wait()
    for j in range(4):
        tiles = [
            [g_ref[j, :, pl.ds((4 * y + q) * LANES, LANES)] for q in range(4)] for y in range(2)
        ]
        fill_windows(gs.at[j], tiles)
    for j in range(4):
        first, last = max(0, j - 1), min(2, j)
        terms = dot(w1[pl.ds(first * CH, (last - first + 1) * CH), :], gs[j])
        for a in range(first, last + 1):
            term = terms[(a - first) * CH : (a - first + 1) * CH]
            out = j - a
            if a == 0:
                acc[out] = term
            else:
                acc[out] += term
    merge = merge_matrix()
    for out in range(2):
        for y in range(2):
            cut = pl.ds(y * 256, 256)
            vg_ref[out, :, cut] = dot(acc[out, :, cut].astype(BF16), merge).astype(BF16)
    fetches[1].wait()
    fetches[2].wait()
    feat_ref[...] = dot_tn(w2_ref[...], wn_ref[...]).astype(BF16)


def add_kernel(mine_hbm, got_hbm, out_hbm, mine_ref, got_ref, sems):
    fetches = [
        pltpu.make_async_copy(mine_hbm, mine_ref, sems.at[0]),
        pltpu.make_async_copy(got_hbm, got_ref, sems.at[1]),
    ]
    for fetch in fetches:
        fetch.start()
    for fetch in fetches:
        fetch.wait()
    got_ref[...] = (mine_ref[...].astype(F32) + got_ref[...].astype(F32)).astype(BF16)
    send = pltpu.make_async_copy(got_ref, out_hbm, sems.at[0])
    send.start()
    send.wait()


def finish_kernel(factor, half_ref, rows_hbm, *refs):
    strided_hbm, grouped_hbm, rows_ref, strided_ref, grouped_ref, fetch_sems, send_sems = refs[-7:]
    half = half_ref[0]
    fetches = [
        pltpu.make_async_copy(
            rows_hbm.at[pl.ds(k * CHUNK, CHUNK)], rows_ref.at[pl.ds(k * CHUNK, CHUNK)], fetch_sems.at[k]
        )
        for k in range(3)
    ]
    for fetch in fetches:
        fetch.start()
    sends = []
    for k in range(3):
        fetches[k].wait()
        at = k * CHUNK
        here = pl.ds(k * PART, PART)
        strided_ref[here, pl.ds(0, LANES)] = rows_ref[pl.ds(at, PART), :].astype(F32) * factor
        rest = rows_ref[pl.ds(at + PART, LEFT), :].astype(F32) * factor
        strided_ref[pl.ds(k * PART, LEFT), pl.ds(LANES, 64)] = rest[:, :64]
        strided_ref[pl.ds(k * PART + LEFT, RIGHT), pl.ds(LANES, 64)] = rest[:RIGHT, 64:]
        there = pl.ds(pl.multiple_of(half * HALF + k * PART, 8), PART)
        sends.append(
            pltpu.make_async_copy(strided_ref.at[here], strided_hbm.at[there], send_sems.at[k])
        )
        sends[-1].start()
        for i in range(2):
            tile = rows_ref[pl.ds(at + PART + LEFT + i * F_PART, F_PART), :]
            grouped_ref[:, pl.ds((2 * k + i) * LANES, LANES)] = tile.astype(F32) * factor
    there = pl.ds(pl.multiple_of(half * F_PART, 8), F_PART)
    sends.append(pltpu.make_async_copy(grouped_ref, grouped_hbm.at[there], send_sems.at[3]))
    sends[-1].start()
    for send in sends:
        send.wait()


VMEM = pl.BlockSpec(memory_space=pltpu.VMEM)
SMEM = pl.BlockSpec(memory_space=pltpu.SMEM)
ANY = pl.BlockSpec(memory_space=pl.ANY)
MIB = 1024 * 1024


def main_call(inner, core, low, own, high, weight, w2, stage=9):
    return pl.pallas_call(
        functools.partial(main_kernel, stage),
        out_shape=(
            jax.ShapeDtypeStruct((ROWS, LANES), BF16),
            jax.ShapeDtypeStruct((ROWS, LANES), BF16),
            jax.ShapeDtypeStruct((TAPS * CH, LANES), BF16),
            jax.ShapeDtypeStruct((4, CH, 8 * LANES), BF16),
        ),
        in_specs=[SMEM, SMEM, ANY, ANY, ANY, VMEM, ANY],
        out_specs=(ANY,) * 4,
        scratch_shapes=[
            pltpu.VMEM((10, CH, LANES), BF16),
            pltpu.VMEM((10, CH, LANES), BF16),
            pltpu.VMEM((10, CH, LANES), BF16),
            pltpu.VMEM((TAPS * CH, 192), BF16),
            pltpu.VMEM((ROWS, LANES), BF16),
            pltpu.VMEM((ROWS, LANES), BF16),
            pltpu.VMEM((TAPS * CH, LANES), BF16),
            pltpu.VMEM((4, CH, 8 * LANES), BF16),
            pltpu.VMEM((6, WIN, 512), BF16),
            pltpu.VMEM((3 * CH, WIN), BF16),
            pltpu.VMEM((4, CH, 512), F32),
            pltpu.VMEM((4, CH, 512), BF16),
            pltpu.VMEM((2, WIN, 512), BF16),
            pltpu.VMEM((768, 768), BF16),
            pltpu.VMEM((CH, 6 * LANES), BF16),
            pltpu.SemaphoreType.DMA((4,)),
        ],
        compiler_params=pltpu.CompilerParams(vmem_limit_bytes=40 * MIB),
        name="main",
    )(inner, core, low, own, high, weight, w2)


def tail_call(chip, grads, windows, w2, weight):
    return pl.pallas_call(
        tail_kernel,
        out_shape=(
            jax.ShapeDtypeStruct((192, LANES), BF16),
            jax.ShapeDtypeStruct((2, CH, 512), BF16),
            jax.ShapeDtypeStruct((1, LANES), F32),
        ),
        in_specs=[ANY, ANY, ANY, ANY, VMEM],
        out_specs=(VMEM,) * 3,
        scratch_shapes=[
            pltpu.VMEM((4, CH, 8 * LANES), BF16),
            pltpu.VMEM((TAPS * CH, LANES), BF16),
            pltpu.VMEM((TAPS * CH, 192), BF16),
            pltpu.VMEM((4, WIN, 512), BF16),
            pltpu.VMEM((3 * CH, WIN), BF16),
            pltpu.VMEM((2, CH, 512), F32),
            pltpu.SemaphoreType.DMA((3,)),
        ],
        compiler_params=pltpu.CompilerParams(vmem_limit_bytes=40 * MIB),
        cost_estimate=pl.CostEstimate(flops=10**9, bytes_accessed=4 * 10**6, transcendentals=0),
        name="tail",
    )(chip, grads, windows, w2, weight)


def add_call(mine, got):
    return pl.pallas_call(
        add_kernel,
        out_shape=jax.ShapeDtypeStruct((ROWS, LANES), BF16),
        in_specs=[ANY, ANY],
        out_specs=ANY,
        scratch_shapes=[
            pltpu.VMEM((ROWS, LANES), BF16),
            pltpu.VMEM((ROWS, LANES), BF16),
            pltpu.SemaphoreType.DMA((2,)),
        ],
        compiler_params=pltpu.CompilerParams(vmem_limit_bytes=16 * MIB),
        name="add",
    )(mine, got)


def finish_call(factor, half, rows, before=()):
    return pl.pallas_call(
        functools.partial(finish_kernel, factor),
        out_shape=(
            jax.ShapeDtypeStruct((TAPS * CH, 192), F32),
            jax.ShapeDtypeStruct((CH, 6 * LANES), F32),
        ),
        in_specs=[SMEM, ANY] + [ANY] * len(before),
        out_specs=(ANY, ANY),
        scratch_shapes=[
            pltpu.VMEM((ROWS, LANES), BF16),
            pltpu.VMEM((HALF, 192), F32),
            pltpu.VMEM((F_PART, 6 * LANES), F32),
            pltpu.SemaphoreType.DMA((3,)),
            pltpu.SemaphoreType.DMA((4,)),
        ],
        input_output_aliases={2 + i: i for i in range(len(before))},
        compiler_params=pltpu.CompilerParams(vmem_limit_bytes=16 * MIB),
        name="finish",
    )(half, rows, *before)


def sum_pieces(parts):
    return jnp.sum(parts.astype(F32), axis=0).astype(BF16)


def to_all(piece, axes, count):
    copies = jnp.broadcast_to(piece[None], (count,) + piece.shape)
    return lax.all_to_all(copies, axes, 0, 0, tiled=True)


def shards(volume, first_weight, second_weight, out_cotangent):
    count = lax.axis_size(SPACE)
    up = [(i, i + 1) for i in range(count - 1)]
    down = [(i + 1, i) for i in range(count - 1)]
    planes = volume.reshape(CH, 2, 2, 2, LANES).transpose(1, 2, 3, 0, 4).reshape(8, CH, LANES)
    own = jnp.concatenate([planes, out_cotangent.reshape(2, CH, LANES)], axis=0)
    low = lax.ppermute(own, SPACE, up)
    high = lax.ppermute(own, SPACE, down)
    core = lax.axis_index("core").astype(jnp.int32).reshape(1)
    inner = jnp.where(lax.axis_index(SPACE) > 0, 1.0, 0.0).astype(F32).reshape(1)
    blocks = first_weight.reshape(3, 9, 4, PG, PG)
    forward_weight = blocks.transpose(0, 2, 4, 1, 3).reshape(3 * CH, 9 * PG)
    backward_weight = blocks[::-1, ::-1].transpose(0, 2, 3, 1, 4).reshape(3 * CH, 9 * PG)
    w2 = second_weight.reshape(TAPS * CH, 192)
    mine, other, windows, grads = main_call(inner, core, low, own, high, forward_weight, w2)
    swap = [(0, 1), (1, 0)]
    chip = add_call(mine, lax.ppermute(other, "core", swap))
    parts = lax.all_to_all(chip.reshape(PIECES, PIECE, LANES), NEAR, 0, 0, tiled=True)
    feat, vgrad, done = tail_call(chip, grads, windows, w2, backward_weight)
    piece = (jnp.sum(parts.astype(F32), axis=0) + done).astype(BF16)
    piece = sum_pieces(to_all(piece, "zh", lax.axis_size("zh")))
    own_half = to_all(piece, NEAR, PIECES).reshape(ROWS, LANES)
    other_half = lax.ppermute(own_half, "core", swap)
    factor = 1.0 / math.sqrt(lax.axis_size(DP) * lax.axis_size(SPACE) * LANES)
    halves = finish_call(factor, core, own_half)
    second_grad, narrow = finish_call(factor, 1 - core, other_half, halves)
    first_grad = narrow[:, : TAPS * PG].reshape(4, PG, PG, TAPS).transpose(3, 0, 1, 2)
    features = feat.reshape(out_cotangent.shape)
    volume_grad = vgrad.reshape(2, CH, 2, 256).transpose(1, 0, 2, 3)[None]
    return (features, volume_grad, first_grad, second_grad.reshape(second_weight.shape))


def solution(mesh):
    fine = Mesh(mesh.devices.reshape(2, 8, 2, 2, 4, 2), ("xh", "zh", "zl", "xl", "y", "core"))
    split = P(DP, None, SPACE, None, None)
    return jax.shard_map(
        shards,
        mesh=fine,
        in_specs=(split, P(), P(), split),
        out_specs=(split, split, P(), P()),
        check_vma=False,
    )
```

time: 110 us -> 104 us (0.945)
  other arithmetic: 4.74 us -> 2.02 us
  Pallas kernels: 17.7 us -> 16.1 us
  starting transfers between devices: 27.2 us -> 26 us
    ppermute x1, starting transfers between devices: 5.5 us -> 8.79 us  [shards(): high = lax.ppermute(own, SPACE, down)]
    ppermute x1, starting transfers between devices: 4.59 us -> 1.92 us  [shards(): low = lax.ppermute(own, SPACE, up)]
    all_to_all x1, starting transfers between devices: 8.85 us -> 6.5 us  [shards(): lax.all_to_all(chip.reshape(PIECES, PIECE, LANES), NEAR, 0, 0, tiled=True)]
    convert_element_type x1 -> x0, other arithmetic: 2.04 us -> none  [shards(): chip = (mine.astype(F32) + got.astype(F32)).astype(BF16)]
    pallas_call x4 -> x5, Pallas kernels: 17.7 us -> 16.1 us  [the longest x1 7.81 us: main_call(): pl.pallas_call(functools.partial(main_kernel, stage), out_shape=(jax.Shap...]
    all_to_all x1, waiting for transfers between devices: 4.39 us -> 5.79 us  [shards(): lax.all_to_all(chip.reshape(PIECES, PIECE, LANES), NEAR, 0, 0, tiled=True)]
    optimization_barrier x1 -> x0, local copies, waits for them, and re-layouts: 1.22 us -> none  [shards(): late_weight = lax.optimization_barrier((first_weight, windows))[0]]
    unnamed x16 -> x13, local copies, waits for them, and re-layouts: 2.05 us -> 2.34 us
  transfers between devices with their start and end apart: 5 -> 5, of which waited for: 2 -> 2; matrix products, arithmetic and copies ran while one was open for 7% -> 6% of each run, Pallas kernels for 6% -> 5%
where the time goes in v4:
time: 104 us
  blocking collectives  41 us (39%)
  starting transfers between devices  26 us (25%)
  Pallas kernels  16.1 us (15%)
  local copies, waits for them, and re-layouts  10.1 us (10%)
  waiting for transfers between devices  7.41 us (7%)
  other arithmetic  2.02 us (2%)
    all_to_all x2, blocking collectives, to_all(): return lax.all_to_all(copies, axes, 0, 0, tiled=True)  41 us
    ppermute x1, starting transfers between devices, shards(): high = lax.ppermute(own, SPACE, down)  8.79 us
    pallas_call x1, Pallas kernels, main_call(): pl.pallas_call(functools.partial(main_kernel, stage), out_shape=(jax.Shap...  7.81 us
    all_to_all x1, starting transfers between devices, shards(): lax.all_to_all(chip.reshape(PIECES, PIECE, LANES), NEAR, 0, 0, tiled=True)  6.5 us
    ppermute x1, starting transfers between devices, shards(): other_half = lax.ppermute(own_half, 'core', swap)  6.36 us
    all_to_all x1, waiting for transfers between devices, shards(): lax.all_to_all(chip.reshape(PIECES, PIECE, LANES), NEAR, 0, 0, tiled=True)  5.79 us
    pallas_call x2, Pallas kernels, finish_call(): pl.pallas_call(functools.partial(finish_kernel, factor), out_shape=(jax.S...  3.89 us
    pallas_call x1, Pallas kernels, tail_call(): pl.pallas_call(tail_kernel, out_shape=(jax.ShapeDtypeStruct((192, LANES),...  3.25 us
  transfers between devices with their start and end apart: 5, of which 2 were waited for; matrix products, arithmetic and copies ran while one was open for 6% of the time, Pallas kernels for 5%

profile of v4, /device:TPU:1, one launch (start us, length us, event | category | flops | bytes accessed | tf_op | source)
XLA Modules:
  0.0 103.6 jit_solution(6214839340059759564)
XLA Ops:
  0.6 1.1 %reshape.76 = bf16[96,2,2,2,128]{4,3,2,1,0:T(2,128)(2,1)S(1)} reshape(bf16[1,96,2,2,256]{4,3,2,1,0:T(2,128)(2,1)} %param.4) | data formatting | bytes 393216 | tf_op jit(solution)/shard_map/reshape | solution.py:472
  1.8 0.8 pad_maximum_fusion.own_hbm
  2.6 8.8 %collective-permute-start.1 = (bf16[10,96,128]{2,1,0:T(8,128)(2,1)S(1)}, bf16[10,96,128]{2,1,0:T(8,128)(2,1)S(1)}, u32[]{:S(2)}, u32[]{:S(2)}) collective-permute-start(bf16[10,96,128]{2,1,0:T(8,128)(2,1)S(1)} %pad_maximum_fusion.own_hbm), channel_id=1, source_target_pairs={{1,0},{2,1},{3,2},{4,3},{5,4},{6,5},{7,6},{8,7},{9,8},{10,9},{11,1... | collective-permute-start | bytes 737288 | tf_op jit(solution)/shard_map/ppermute | solution.py:475
  11.4 1.9 %collective-permute-start = (bf16[10,96,128]{2,1,0:T(8,128)(2,1)S(1)}, bf16[10,96,128]{2,1,0:T(8,128)(2,1)S(1)}, u32[]{:S(2)}, u32[]{:S(2)}) collective-permute-start(bf16[10,96,128]{2,1,0:T(8,128)(2,1)S(1)} %pad_maximum_fusion.own_hbm), channel_id=1, source_target_pairs={{0,1},{1,2},{2,3},{3,4},{4,5},{5,6},{6,7},{7,8},{8,9},{9,10},{10,1... | collective-permute-start | bytes 737288 | tf_op jit(solution)/shard_map/ppermute | solution.py:474
  13.4 1.2 %copy.22 = bf16[27,4,24,24]{3,2,1,0:T(8,128)(2,1)S(1)} copy(bf16[27,4,24,24]{0,3,2,1:T(8,128)(2,1)S(1)} %copy-done.5) | data formatting | bytes 248832 | tf_op args[1]
  14.9 1.0 reshape.80
  15.9 1.0 copy.24.fw_ref
  17.0 7.8 %main.1 = (bf16[2304,128]{1,0:T(8,128)(2,1)S(1)}, bf16[2304,128]{1,0:T(8,128)(2,1)S(1)}, bf16[2592,128]{1,0:T(8,128)(2,1)S(1)}, bf16[4,96,1024]{2,1,0:T(8,128)(2,1)S(1)}) custom-call(f32[1]{0:T(128)} %bitcast.inner_ref, s32[1]{0:T(128)} %bitcast.1.core_ref.half_ref, bf16[10,96,128]{2,1,0:T(8,128)(2,1)S(1)} %collective-permute-done.low_hbm, ...), custom_call_target="tpu_custom_call" | custom-call | tf_op jit(solution)/shard_map/main/pallas_call | solution.py:363
  24.8 2.4 %collective-permute-start.2 = (bf16[2304,128]{1,0:T(8,128)(2,1)S(1)}, bf16[2304,128]{1,0:T(8,128)(2,1)S(1)}, u32[]{:S(2)}, u32[]{:S(2)}) collective-permute-start(bf16[2304,128]{1,0:T(8,128)(2,1)S(1)} %get-tuple-element.16), channel_id=1, source_target_pairs={{0,1},{1,0},{2,3},{3,2},{4,5},{5,4},{6,7},{7,6},{8,9},{9,8},{10,11... | collective-permute-start | bytes 1769480 | tf_op jit(solution)/shard_map/ppermute | solution.py:484
  27.3 1.6 %collective-permute-done.2.got_hbm = bf16[2304,128]{1,0:T(8,128)(2,1)S(1)} collective-permute-done((bf16[2304,128]{1,0:T(8,128)(2,1)S(1)}, bf16[2304,128]{1,0:T(8,128)(2,1)S(1)}, u32[]{:S(2)}, u32[]{:S(2)}) %collective-permute-start.2) | collective-permute-done | bytes 589856 | tf_op jit(solution)/shard_map/ppermute | solution.py:484
  28.9 1.2 %add.25.after_hbm = bf16[2304,128]{1,0:T(8,128)(2,1)} custom-call(bf16[2304,128]{1,0:T(8,128)(2,1)S(1)} %get-tuple-element.15.mine_hbm, bf16[2304,128]{1,0:T(8,128)(2,1)S(1)} %collective-permute-done.2.got_hbm), custom_call_target="tpu_custom_call" | custom-call | tf_op jit(solution)/shard_map/add/pallas_call | solution.py:422
  30.1 6.5 %all-to-all-start = ((bf16[32,72,128]{2,1,0:T(8,128)(2,1)}), bf16[32,72,128]{2,1,0:T(8,128)(2,1)}, u32[]{:S(2)}, u32[]{:S(2)}) async-start(bf16[32,72,128]{2,1,0:T(8,128)(2,1)} %bitcast.12), calls=%async_computation | async-start | bytes 1179648 | tf_op jit(solution)/shard_map/all_to_all | solution.py:485
  36.7 1.3 %copy.25 = bf16[3,4,24,9,24]{2,1,0,4,3:T(4,128)(2,1)S(1)} copy(bf16[3,4,24,9,24]{4,2,1,3,0:T(8,128)(2,1)S(1)} %reverse_bitcast_fusion) | data formatting | bytes 248832 | tf_op jit(solution)/shard_map/transpose | solution.py:480
  38.5 1.1 %copy-done.2 = bf16[2592,128]{1,0:T(8,128)(2,1)S(1)} copy-done((bf16[2592,128]{1,0:T(8,128)(2,1)S(1)}, bf16[2592,128]{1,0:T(8,128)(2,1)}, u32[]{:S(2)}) %copy-start.2) | copy-done | bytes 663576
  39.6 3.2 %tail.1 = (bf16[192,128]{1,0:T(8,128)(2,1)}, bf16[2,96,512]{2,1,0:T(8,128)(2,1)S(1)}, f32[1,128]{1,0:T(1,128)S(1)}) custom-call(bf16[2304,128]{1,0:T(8,128)(2,1)} %add.25.after_hbm, bf16[4,96,1024]{2,1,0:T(8,128)(2,1)S(1)} %get-tuple-element.17.g_hbm, bf16[2592,128]{1,0:T(8,128)(2,1)S(1)} %copy-done.2, bf16[2592,192]{1,0:T(8,128)(2,1)S(1)} %bitcast.31, ...), custom_call_target="tpu_custom_call" | custom-call | flops 1000000000 | bytes 4000000 | tf_op jit(solution)/shard_map/tail/pallas_call | solution.py:397
  42.9 5.8 %all-to-all-done = bf16[32,72,128]{2,1,0:T(8,128)(2,1)} async-done(((bf16[32,72,128]{2,1,0:T(8,128)(2,1)}), bf16[32,72,128]{2,1,0:T(8,128)(2,1)}, u32[]{:S(2)}, u32[]{:S(2)}) %all-to-all-start) | async-done | bytes 589856 | tf_op jit(solution)/shard_map/all_to_all | solution.py:485
  48.6 1.2 %convert_reduce_fusion = f32[72,128]{1,0:T(8,128)S(1)} fusion(bf16[32,72,128]{2,1,0:T(8,128)(2,1)} %all-to-all-done), kind=kLoop, calls=%fused_computation | loop fusion | flops 580608 | bytes 626688 | tf_op jit(solution)/shard_map/reduce_sum | solution.py:487
  49.8 27.7 %all_to_all.15 = bf16[8,72,128]{2,1,0:T(8,128)(2,1)S(1)} all-to-all(bf16[8,72,128]{2,1,0:T(8,128)(2,1)S(1)} %broadcast_in_dim.7), channel_id=1, replica_groups=mesh['xh'=2,'zh'=8,'zl'=2,'xl'=2,'y'=4,'core'=2] {'zh'}, dimensions={0} | all-to-all | bytes 294912 | tf_op jit(solution)/shard_map/all_to_all | solution.py:465
  77.7 13.4 %all_to_all.16 = bf16[32,72,128]{2,1,0:T(8,128)(2,1)S(1)} all-to-all(bf16[32,72,128]{2,1,0:T(8,128)(2,1)S(1)} %broadcast_in_dim.8), channel_id=1, replica_groups=mesh['xh'=2,'zh'=8,'zl'=2,'xl'=2,'y'=4,'core'=2] {'xh','xl','y','zl'}, dimensions={0} | all-to-all | bytes 1179648 | tf_op jit(solution)/shard_map/all_to_all | solution.py:465
  91.0 6.4 %collective-permute-start.3 = (bf16[2304,128]{1,0:T(8,128)(2,1)S(1)}, bf16[2304,128]{1,0:T(8,128)(2,1)S(1)}, u32[]{:S(2)}, u32[]{:S(2)}) collective-permute-start(bf16[2304,128]{1,0:T(8,128)(2,1)S(1)} %bitcast.28), channel_id=1, source_target_pairs={{0,1},{1,0},{2,3},{3,2},{4,5},{5,4},{6,7},{7,6},{8,9},{9,8},{10,11... | collective-permute-start | bytes 1769480 | tf_op jit(solution)/shard_map/ppermute | solution.py:490
  97.4 0.8 copy.29
  98.2 1.9 %finish.2 = (f32[2592,192]{1,0:T(8,128)}, f32[96,768]{1,0:T(8,128)S(1)}) custom-call(s32[1]{0:T(128)} %bitcast.1.core_ref.half_ref, bf16[2304,128]{1,0:T(8,128)(2,1)S(1)} %bitcast.29), custom_call_target="tpu_custom_call" | custom-call | tf_op jit(solution)/shard_map/finish/pallas_call | solution.py:438
  100.2 2.0 %finish.3 = (f32[2592,192]{1,0:T(8,128)}, f32[96,768]{1,0:T(8,128)S(1)}) custom-call(s32[1]{0:T(128)S(6)} %sub.3.half_ref, bf16[2304,128]{1,0:T(8,128)(2,1)S(1)} %collective-permute-done.3.rows_hbm, f32[2592,192]{1,0:T(8,128)} %get-tuple-element.22.refs_0_, f32[96,768]{1,0:T(8,128)S(1)} %get-tuple-element.23.refs_1_), custom_call_target="tpu_custom_call", output_to_operand_aliasing={{0}: (2, {}), {1}: (3, {})} | custom-call | tf_op jit(solution)/shard_map/finish/pallas_call | solution.py:438
  102.2 1.5 %reshape.87 = f32[4,24,24,27]{3,2,1,0:T(8,128)} reshape(f32[96,648]{1,0:T(8,128)S(1)} %bitcast.32) | data formatting | bytes 497664 | tf_op jit(solution)/shard_map/reshape | solution.py:494
  (24 shorter events, 1.1 us)
Async XLA Ops:
  0.6 12.7 %copy-start.5 = (bf16[27,4,24,24]{0,3,2,1:T(8,128)(2,1)S(1)}, bf16[27,4,24,24]{0,3,2,1:T(8,128)(2,1)}, u32[]{:S(2)}) copy-start(bf16[27,4,24,24]{0,3,2,1:T(8,128)(2,1)} %param.5) | copy-start | bytes 373252
  2.6 14.3 %collective-permute-start.1 = (bf16[10,96,128]{2,1,0:T(8,128)(2,1)S(1)}, bf16[10,96,128]{2,1,0:T(8,128)(2,1)S(1)}, u32[]{:S(2)}, u32[]{:S(2)}) collective-permute-start(bf16[10,96,128]{2,1,0:T(8,128)(2,1)S(1)} %pad_maximum_fusion.own_hbm), channel_id=1, source_target_pairs={{1,0},{2,1},{3,2},{4,3},{5,4},{6,5},{7,6},{8,7},{9,8},{10,9},{11,1... | collective-permute-start | bytes 737288 | tf_op jit(solution)/shard_map/ppermute | solution.py:475
  11.4 5.6 %collective-permute-start = (bf16[10,96,128]{2,1,0:T(8,128)(2,1)S(1)}, bf16[10,96,128]{2,1,0:T(8,128)(2,1)S(1)}, u32[]{:S(2)}, u32[]{:S(2)}) collective-permute-start(bf16[10,96,128]{2,1,0:T(8,128)(2,1)S(1)} %pad_maximum_fusion.own_hbm), channel_id=1, source_target_pairs={{0,1},{1,2},{2,3},{3,4},{4,5},{5,6},{6,7},{7,8},{8,9},{9,10},{10,1... | collective-permute-start | bytes 737288 | tf_op jit(solution)/shard_map/ppermute | solution.py:474
  14.6 2.4 %copy-start.3 = (bf16[27,4,24,24]{3,2,1,0:T(8,128)(2,1)}, bf16[27,4,24,24]{3,2,1,0:T(8,128)(2,1)S(1)}, u32[]{:S(2)}) copy-start(bf16[27,4,24,24]{3,2,1,0:T(8,128)(2,1)S(1)} %copy.22) | copy-start | bytes 373252
  14.6 2.4 %copy-start = (bf16[27,96,192]{2,1,0:T(8,128)(2,1)S(1)}, bf16[27,96,192]{2,1,0:T(8,128)(2,1)}, u32[]{:S(2)}) copy-start(bf16[27,96,192]{2,1,0:T(8,128)(2,1)} %param.6) | copy-start | bytes 2985988
  24.8 5.3 %copy-start.1 = (bf16[2592,128]{1,0:T(8,128)(2,1)}, bf16[2592,128]{1,0:T(8,128)(2,1)S(1)}, u32[]{:S(2)}) copy-start(bf16[2592,128]{1,0:T(8,128)(2,1)S(1)} %get-tuple-element.18.wn_hbm) | copy-start | bytes 1990660
  24.8 4.0 %collective-permute-start.2 = (bf16[2304,128]{1,0:T(8,128)(2,1)S(1)}, bf16[2304,128]{1,0:T(8,128)(2,1)S(1)}, u32[]{:S(2)}, u32[]{:S(2)}) collective-permute-start(bf16[2304,128]{1,0:T(8,128)(2,1)S(1)} %get-tuple-element.16), channel_id=1, source_target_pairs={{0,1},{1,0},{2,3},{3,2},{4,5},{5,4},{6,7},{7,6},{8,9},{9,8},{10,11... | collective-permute-start | bytes 1769480 | tf_op jit(solution)/shard_map/ppermute | solution.py:484
  28.9 7.7 %copy-start.4 = (bf16[27,4,24,24]{3,2,1,0:T(8,128)(2,1)S(1)}, bf16[27,4,24,24]{3,2,1,0:T(8,128)(2,1)}, u32[]{:S(2)}) copy-start(bf16[27,4,24,24]{3,2,1,0:T(8,128)(2,1)} %copy-done.3) | copy-start | bytes 373252
  30.1 18.6 %all-to-all-start = ((bf16[32,72,128]{2,1,0:T(8,128)(2,1)}), bf16[32,72,128]{2,1,0:T(8,128)(2,1)}, u32[]{:S(2)}, u32[]{:S(2)}) async-start(bf16[32,72,128]{2,1,0:T(8,128)(2,1)} %bitcast.12), calls=%async_computation | async-start | bytes 1179648 | tf_op jit(solution)/shard_map/all_to_all | solution.py:485
  38.5 1.1 %copy-start.2 = (bf16[2592,128]{1,0:T(8,128)(2,1)S(1)}, bf16[2592,128]{1,0:T(8,128)(2,1)}, u32[]{:S(2)}) copy-start(bf16[2592,128]{1,0:T(8,128)(2,1)} %copy-done.1) | copy-start | bytes 1990660
  91.0 9.2 %collective-permute-start.3 = (bf16[2304,128]{1,0:T(8,128)(2,1)S(1)}, bf16[2304,128]{1,0:T(8,128)(2,1)S(1)}, u32[]{:S(2)}, u32[]{:S(2)}) collective-permute-start(bf16[2304,128]{1,0:T(8,128)(2,1)S(1)} %bitcast.28), channel_id=1, source_target_pairs={{0,1},{1,0},{2,3},{3,2},{4,5},{5,4},{6,7},{7,6},{8,9},{9,8},{10,11... | collective-permute-start | bytes 1769480 | tf_op jit(solution)/shard_map/ppermute | solution.py:490

commit v5 on v4

--- a/solution.py
+++ b/solution.py
@@ -116,19 +116,24 @@
     return jnp.where(mask, dot(narrow, fold), 0.0).astype(BF16)
 
 
+def cotangent_of(slab):
+    return jnp.concatenate([slab[4, :, :LANES], slab[4, :, LANES:]], axis=0)
+
+
 def main_kernel(
-    stage, inner_ref, core_ref, low_hbm, own_hbm, high_hbm, fw_ref, w2_hbm,
+    inner_ref, core_ref, far_hbm, own_hbm, twin_hbm, fw_ref, w2_hbm,
     mine_hbm, other_hbm, wn_hbm, g_hbm,
-    low_ref, own_ref, high_ref, w2_ref, mine_ref, other_ref, wn_ref, g_ref,
+    beside, own_ref, w2_ref, mine_ref, other_ref, wn_ref, g_ref,
     xs, w1, pre_ref, xc_ref, gs, order_ref, fg, sems,
 ):
     inner = inner_ref[0]
     core = core_ref[0]
+    low_ref, high_ref = beside.at[0], beside.at[1]
     fetches = [
-        pltpu.make_async_copy(source, target, sems.at[i])
-        for i, (source, target) in enumerate(
-            ((own_hbm, own_ref), (low_hbm, low_ref), (high_hbm, high_ref), (w2_hbm, w2_ref))
-        )
+        pltpu.make_async_copy(own_hbm, own_ref, sems.at[0]),
+        pltpu.make_async_copy(far_hbm, beside.at[core], sems.at[1]),
+        pltpu.make_async_copy(twin_hbm, beside.at[1 - core], sems.at[2]),
+        pltpu.make_async_copy(w2_hbm, w2_ref, sems.at[3]),
     ]
     for fetch in fetches:
         fetch.start()
@@ -145,8 +150,7 @@
             fetches[2].wait()
         tiles = []
         for y in range(2):
-            at = 4 * (e % 2) + 2 * y
-            parts = dot(jnp.concatenate([slab[at], slab[at + 1]], axis=1), split).astype(BF16)
+            parts = dot(slab[2 * (e % 2) + y], split).astype(BF16)
             tiles.append([parts[:, q * LANES : (q + 1) * LANES] for q in range(4)])
             if 1 <= e <= 4:
                 xc_ref[e - 1, :, pl.ds(y * 256, 256)] = parts[:, :256]
@@ -177,7 +181,7 @@
             wn_ref[pl.ds(base + 2 * CH, CH), :] = odd.astype(BF16)
     send_wn = pltpu.make_async_copy(wn_ref, wn_hbm, sems.at[0])
     send_wn.start()
-    cot = jnp.concatenate([own_ref[8], own_ref[9]], axis=0)
+    cot = cotangent_of(own_ref)
     rest = cot[LANES:]
     none = jnp.zeros_like(rest)
     both = jnp.concatenate(
@@ -193,10 +197,8 @@
             right = jnp.concatenate([wn_ref[pl.ds(base + LEFT, RIGHT), :], fill], axis=0)
             pairs = jnp.concatenate([left, right], axis=1)
             out_ref[pl.ds(k * CHUNK + PART, LEFT), :] = dot_nt(pairs, both).astype(BF16)
-    above = jnp.concatenate([high_ref[8], high_ref[9]], axis=0)
-    below = jnp.concatenate([low_ref[8], low_ref[9]], axis=0)
-    with_above = jnp.concatenate([cot, above], axis=1)
-    with_below = jnp.concatenate([cot, below], axis=1)
+    with_above = jnp.concatenate([cot, cotangent_of(high_ref)], axis=1)
+    with_below = jnp.concatenate([cot, cotangent_of(low_ref)], axis=1)
     order_ref[...] = order_matrix()
     fetches[3].wait()
     spread = [
@@ -261,7 +263,7 @@
 
 
 def tail_kernel(
-    after_hbm, g_hbm, wn_hbm, w2_hbm, fw_ref, feat_ref, vg_ref, done_ref,
+    after_hbm, g_hbm, wn_hbm, w2_hbm, fw_ref, feat_ref, vg_ref,
     g_ref, wn_ref, w2_ref, gs, w1, acc, sems,
 ):
     fetches = [
@@ -272,7 +274,6 @@
     ]
     for fetch in fetches:
         fetch.start()
-    done_ref[...] = jnp.zeros((1, LANES), F32)
     mask = group_mask()
     fold = fold_matrix(9 * PG)
     for a in range(3):
@@ -359,9 +360,9 @@
 MIB = 1024 * 1024
 
 
-def main_call(inner, core, low, own, high, weight, w2, stage=9):
+def main_call(inner, core, far, own, twin, weight, w2):
     return pl.pallas_call(
-        functools.partial(main_kernel, stage),
+        main_kernel,
         out_shape=(
             jax.ShapeDtypeStruct((ROWS, LANES), BF16),
             jax.ShapeDtypeStruct((ROWS, LANES), BF16),
@@ -371,9 +372,8 @@
         in_specs=[SMEM, SMEM, ANY, ANY, ANY, VMEM, ANY],
         out_specs=(ANY,) * 4,
         scratch_shapes=[
-            pltpu.VMEM((10, CH, LANES), BF16),
-            pltpu.VMEM((10, CH, LANES), BF16),
-            pltpu.VMEM((10, CH, LANES), BF16),
+            pltpu.VMEM((2, 5, CH, 256), BF16),
+            pltpu.VMEM((5, CH, 256), BF16),
             pltpu.VMEM((TAPS * CH, 192), BF16),
             pltpu.VMEM((ROWS, LANES), BF16),
             pltpu.VMEM((ROWS, LANES), BF16),
@@ -390,19 +390,18 @@
         ],
         compiler_params=pltpu.CompilerParams(vmem_limit_bytes=40 * MIB),
         name="main",
-    )(inner, core, low, own, high, weight, w2)
-
-
-def tail_call(chip, grads, windows, w2, weight):
+    )(inner, core, far, own, twin, weight, w2)
+
+
+def tail_call(after, grads, windows, w2, weight):
     return pl.pallas_call(
         tail_kernel,
         out_shape=(
             jax.ShapeDtypeStruct((192, LANES), BF16),
             jax.ShapeDtypeStruct((2, CH, 512), BF16),
-            jax.ShapeDtypeStruct((1, LANES), F32),
         ),
         in_specs=[ANY, ANY, ANY, ANY, VMEM],
-        out_specs=(VMEM,) * 3,
+        out_specs=(VMEM,) * 2,
         scratch_shapes=[
             pltpu.VMEM((4, CH, 8 * LANES), BF16),
             pltpu.VMEM((TAPS * CH, LANES), BF16),
@@ -415,7 +414,7 @@
         compiler_params=pltpu.CompilerParams(vmem_limit_bytes=40 * MIB),
         cost_estimate=pl.CostEstimate(flops=10**9, bytes_accessed=4 * 10**6, transcendentals=0),
         name="tail",
-    )(chip, grads, windows, w2, weight)
+    )(after, grads, windows, w2, weight)
 
 
 def add_call(mine, got):
@@ -456,6 +455,23 @@
     )(half, rows, *before)
 
 
+def sum_kernel(parts_ref, after_hbm, out_ref):
+    total = parts_ref[0].astype(F32)
+    for k in range(1, parts_ref.shape[0]):
+        total = total + parts_ref[k].astype(F32)
+    out_ref[...] = total.astype(BF16)
+
+
+def sum_call(parts, after):
+    return pl.pallas_call(
+        sum_kernel,
+        out_shape=jax.ShapeDtypeStruct(parts.shape[1:], BF16),
+        in_specs=[VMEM, ANY],
+        out_specs=VMEM,
+        name="sum",
+    )(parts, after)
+
+
 def sum_pieces(parts):
     return jnp.sum(parts.astype(F32), axis=0).astype(BF16)
 
@@ -467,34 +483,37 @@
 
 def shards(volume, first_weight, second_weight, out_cotangent):
     count = lax.axis_size(SPACE)
-    up = [(i, i + 1) for i in range(count - 1)]
-    down = [(i + 1, i) for i in range(count - 1)]
-    planes = volume.reshape(CH, 2, 2, 2, LANES).transpose(1, 2, 3, 0, 4).reshape(8, CH, LANES)
-    own = jnp.concatenate([planes, out_cotangent.reshape(2, CH, LANES)], axis=0)
-    low = lax.ppermute(own, SPACE, up)
-    high = lax.ppermute(own, SPACE, down)
+    planes = volume[0].transpose(1, 2, 0, 3).reshape(4, CH, 256)
+    cotangent = out_cotangent.reshape(2, CH, LANES).transpose(1, 0, 2).reshape(1, CH, 256)
+    own = jnp.concatenate([planes, cotangent], axis=0)
+    far = lax.ppermute(
+        own,
+        SPACE,
+        [(i, i + 1) for i in range(1, count - 1, 2)] + [(i, i - 1) for i in range(2, count, 2)],
+    )
+    swap = [(0, 1), (1, 0)]
+    twin = lax.ppermute(own, "core", swap)
     core = lax.axis_index("core").astype(jnp.int32).reshape(1)
     inner = jnp.where(lax.axis_index(SPACE) > 0, 1.0, 0.0).astype(F32).reshape(1)
     blocks = first_weight.reshape(3, 9, 4, PG, PG)
     forward_weight = blocks.transpose(0, 2, 4, 1, 3).reshape(3 * CH, 9 * PG)
     backward_weight = blocks[::-1, ::-1].transpose(0, 2, 3, 1, 4).reshape(3 * CH, 9 * PG)
     w2 = second_weight.reshape(TAPS * CH, 192)
-    mine, other, windows, grads = main_call(inner, core, low, own, high, forward_weight, w2)
-    swap = [(0, 1), (1, 0)]
+    mine, other, windows, grads = main_call(inner, core, far, own, twin, forward_weight, w2)
     chip = add_call(mine, lax.ppermute(other, "core", swap))
     parts = lax.all_to_all(chip.reshape(PIECES, PIECE, LANES), NEAR, 0, 0, tiled=True)
-    feat, vgrad, done = tail_call(chip, grads, windows, w2, backward_weight)
-    piece = (jnp.sum(parts.astype(F32), axis=0) + done).astype(BF16)
-    piece = sum_pieces(to_all(piece, "zh", lax.axis_size("zh")))
+    piece = sum_pieces(parts)
+    feat, vgrad = tail_call(piece, grads, windows, w2, backward_weight)
+    features = feat.reshape(out_cotangent.shape)
+    volume_grad = vgrad.reshape(2, CH, 2, 256).transpose(1, 0, 2, 3)
+    piece = sum_call(to_all(piece, "zh", lax.axis_size("zh")), volume_grad)
     own_half = to_all(piece, NEAR, PIECES).reshape(ROWS, LANES)
     other_half = lax.ppermute(own_half, "core", swap)
     factor = 1.0 / math.sqrt(lax.axis_size(DP) * lax.axis_size(SPACE) * LANES)
     halves = finish_call(factor, core, own_half)
     second_grad, narrow = finish_call(factor, 1 - core, other_half, halves)
     first_grad = narrow[:, : TAPS * PG].reshape(4, PG, PG, TAPS).transpose(3, 0, 1, 2)
-    features = feat.reshape(out_cotangent.shape)
-    volume_grad = vgrad.reshape(2, CH, 2, 256).transpose(1, 0, 2, 3)[None]
-    return (features, volume_grad, first_grad, second_grad.reshape(second_weight.shape))
+    return (features, volume_grad[None], first_grad, second_grad.reshape(second_weight.shape))
 
 
 def solution(mesh):

time: 104 us -> 105 us (level)
  blocking collectives: 41 us -> 30.9 us
  starting transfers between devices: 26 us -> 33.1 us
  local copies, waits for them, and re-layouts: 10.1 us -> 13.3 us
  waiting for transfers between devices: 7.41 us -> 9.39 us
  other arithmetic: 2.02 us -> 0.12 us
    all_to_all x2 -> x1, blocking collectives: 41 us -> 13.8 us  [to_all(): return lax.all_to_all(copies, axes, 0, 0, tiled=True)]
    all_to_all x0 -> x1, blocking collectives: none -> 17.1 us  [shards(): lax.all_to_all(chip.reshape(PIECES, PIECE, LANES), NEAR, 0, 0, tiled=True)]
    all_to_all x1, starting transfers between devices: 6.5 us -> 13.9 us  [to_all(): return lax.all_to_all(copies, axes, 0, 0, tiled=True)]
    pallas_call x1 -> x2, Pallas kernels: 7.81 us -> 9.34 us  [the longest x1 7.8 us: main_call(): pl.pallas_call(main_kernel, out_shape=(jax.ShapeDtypeStruct((ROWS, LANES)...]
    broadcast_in_dim x2, local copies, waits for them, and re-layouts: 0.1 us -> 1.48 us  [to_all(): copies = jnp.broadcast_to(piece[None], (count,) + piece.shape)]
    reduce_sum x1 -> x0, other arithmetic: 1.16 us -> none  [shards(): piece = (jnp.sum(parts.astype(F32), axis=0) + done).astype(BF16)]
    unnamed x13 -> x11, local copies, waits for them, and re-layouts: 2.34 us -> 3.37 us
  transfers between devices with their start and end apart: 5 -> 5, of which waited for: 2 -> 3; matrix products, arithmetic and copies ran while one was open for 6% -> 7% of each run, Pallas kernels for 5% -> 5%
where the time goes in v5:
time: 105 us
  starting transfers between devices  33.1 us (32%)
  blocking collectives  30.9 us (29%)
  Pallas kernels  17 us (16%)
  local copies, waits for them, and re-layouts  13.3 us (13%)
  waiting for transfers between devices  9.39 us (9%)
    all_to_all x1, blocking collectives, shards(): lax.all_to_all(chip.reshape(PIECES, PIECE, LANES), NEAR, 0, 0, tiled=True)  17.1 us
    all_to_all x1, starting transfers between devices, to_all(): return lax.all_to_all(copies, axes, 0, 0, tiled=True)  13.9 us
    all_to_all x1, blocking collectives, to_all(): return lax.all_to_all(copies, axes, 0, 0, tiled=True)  13.8 us
    ppermute x1, starting transfers between devices, shards(): twin = lax.ppermute(own, 'core', swap)  8.79 us
    pallas_call x1, Pallas kernels, main_call(): pl.pallas_call(main_kernel, out_shape=(jax.ShapeDtypeStruct((ROWS, LANES)...  7.8 us
    ppermute x1, starting transfers between devices, shards(): other_half = lax.ppermute(own_half, 'core', swap)  6.47 us
    all_to_all x1, waiting for transfers between devices, to_all(): return lax.all_to_all(copies, axes, 0, 0, tiled=True)  6.46 us
    pallas_call x2, Pallas kernels, finish_call(): pl.pallas_call(functools.partial(finish_kernel, factor), out_shape=(jax.S...  3.92 us
  transfers between devices with their start and end apart: 5, of which 3 were waited for; matrix products, arithmetic and copies ran while one was open for 7% of the time, Pallas kernels for 5%

profile of v5, /device:TPU:1, one launch (start us, length us, event | category | flops | bytes accessed | tf_op | source)
XLA Modules:
  0.0 104.7 jit_solution(12193114162845280512)
XLA Ops:
  0.6 0.9 copy.28
  1.6 1.0 copy.15
  2.6 8.8 %collective-permute-start.1 = (bf16[5,96,256]{2,1,0:T(8,128)(2,1)S(1)}, bf16[5,96,256]{2,1,0:T(8,128)(2,1)S(1)}, u32[]{:S(2)}, u32[]{:S(2)}) collective-permute-start(bf16[5,96,256]{2,1,0:T(8,128)(2,1)S(1)} %pad_maximum_fusion.own_hbm), channel_id=1, source_target_pairs={{0,1},{1,0},{2,3},{3,2},{4,5},{5,4},{6,7},{7,6},{8,9},{9,8},{10,11... | collective-permute-start | bytes 737288 | tf_op jit(solution)/shard_map/ppermute | solution.py:495
  11.4 1.9 %collective-permute-start = (bf16[5,96,256]{2,1,0:T(8,128)(2,1)S(1)}, bf16[5,96,256]{2,1,0:T(8,128)(2,1)S(1)}, u32[]{:S(2)}, u32[]{:S(2)}) collective-permute-start(bf16[5,96,256]{2,1,0:T(8,128)(2,1)S(1)} %pad_maximum_fusion.own_hbm), channel_id=1, source_target_pairs={{1,2},{3,4},{5,6},{7,8},{9,10},{11,12},{13,14},{2,1},{4,3},{6,5},{... | collective-permute-start | bytes 737288 | tf_op jit(solution)/shard_map/ppermute | solution.py:489
  13.3 2.3 %copy.17 = bf16[27,4,24,24]{3,2,1,0:T(8,128)(2,1)S(1)} copy(bf16[27,4,24,24]{0,3,2,1:T(8,128)(2,1)} %param.5) | data formatting | bytes 248832 | tf_op args[1]
  15.9 1.0 reshape.61
  16.9 1.0 copy.19.fw_ref
  18.0 1.0 collective-permute-done.far_hbm
  18.9 7.8 %main.1 = (bf16[2304,128]{1,0:T(8,128)(2,1)S(1)}, bf16[2304,128]{1,0:T(8,128)(2,1)S(1)}, bf16[2592,128]{1,0:T(8,128)(2,1)S(1)}, bf16[4,96,1024]{2,1,0:T(8,128)(2,1)S(1)}) custom-call(f32[1]{0:T(128)} %bitcast.inner_ref, s32[1]{0:T(128)} %bitcast.1.core_ref.half_ref, bf16[5,96,256]{2,1,0:T(8,128)(2,1)S(1)} %collective-permute-done.far_hbm, ...), custom_call_target="tpu_custom_call" | custom-call | tf_op jit(solution)/shard_map/main/pallas_call | solution.py:364
  26.8 2.1 %collective-permute-start.2 = (bf16[2304,128]{1,0:T(8,128)(2,1)S(1)}, bf16[2304,128]{1,0:T(8,128)(2,1)S(1)}, u32[]{:S(2)}, u32[]{:S(2)}) collective-permute-start(bf16[2304,128]{1,0:T(8,128)(2,1)S(1)} %get-tuple-element.15), channel_id=1, source_target_pairs={{0,1},{1,0},{2,3},{3,2},{4,5},{5,4},{6,7},{7,6},{8,9},{9,8},{10,11... | collective-permute-start | bytes 1769480 | tf_op jit(solution)/shard_map/ppermute | solution.py:503
  28.8 2.0 %collective-permute-done.2.got_hbm = bf16[2304,128]{1,0:T(8,128)(2,1)S(1)} collective-permute-done((bf16[2304,128]{1,0:T(8,128)(2,1)S(1)}, bf16[2304,128]{1,0:T(8,128)(2,1)S(1)}, u32[]{:S(2)}, u32[]{:S(2)}) %collective-permute-start.2) | collective-permute-done | bytes 589856 | tf_op jit(solution)/shard_map/ppermute | solution.py:503
  31.3 17.1 %all_to_all.15 = bf16[32,72,128]{2,1,0:T(8,128)(2,1)S(1)} all-to-all(bf16[32,72,128]{2,1,0:T(8,128)(2,1)S(1)} %bitcast.32), channel_id=1, replica_groups=mesh['xh'=2,'zh'=8,'zl'=2,'xl'=2,'y'=4,'core'=2] {'xh','xl','y','zl'}, dimensions={0} | all-to-all | bytes 1179648 | tf_op jit(solution)/shard_map/all_to_all | solution.py:504
  49.2 13.9 %all-to-all-start.1 = ((bf16[8,72,128]{2,1,0:T(8,128)(2,1)}), bf16[8,72,128]{2,1,0:T(8,128)(2,1)}, u32[]{:S(2)}, u32[]{:S(2)}) async-start(bf16[8,72,128]{2,1,0:T(8,128)(2,1)} %broadcast_in_dim.7), calls=%async_computation.1 | async-start | bytes 294912 | tf_op jit(solution)/shard_map/all_to_all | solution.py:481
  63.2 1.3 %copy.20 = bf16[3,4,24,9,24]{2,1,0,4,3:T(4,128)(2,1)S(1)} copy(bf16[3,4,24,9,24]{4,2,1,3,0:T(8,128)(2,1)S(1)} %reverse_bitcast_fusion) | data formatting | bytes 248832 | tf_op jit(solution)/shard_map/transpose | solution.py:500
  65.0 1.1 %copy-done.2 = bf16[2592,128]{1,0:T(8,128)(2,1)S(1)} copy-done((bf16[2592,128]{1,0:T(8,128)(2,1)S(1)}, bf16[2592,128]{1,0:T(8,128)(2,1)}, u32[]{:S(2)}) %copy-start.2) | copy-done | bytes 663576
  66.1 3.2 %tail.1 = (bf16[192,128]{1,0:T(8,128)(2,1)}, bf16[2,96,512]{2,1,0:T(8,128)(2,1)S(1)}) custom-call(bf16[72,128]{1,0:T(8,128)(2,1)S(1)} %reduce_sum.12.after_hbm, bf16[4,96,1024]{2,1,0:T(8,128)(2,1)S(1)} %get-tuple-element.16.g_hbm, bf16[2592,128]{1,0:T(8,128)(2,1)S(1)} %copy-done.2, bf16[2592,192]{1,0:T(8,128)(2,1)S(1)} %bitcast.36, ...), custom_call_target="tpu_custom_call" | custom-call | flops 1000000000 | bytes 4000000 | tf_op jit(solution)/shard_map/tail/pallas_call | solution.py:397
  69.4 0.8 copy.27
  70.2 6.5 %all-to-all-done.1.parts_ref = bf16[8,72,128]{2,1,0:T(8,128)(2,1)} async-done(((bf16[8,72,128]{2,1,0:T(8,128)(2,1)}), bf16[8,72,128]{2,1,0:T(8,128)(2,1)}, u32[]{:S(2)}, u32[]{:S(2)}) %all-to-all-start.1) | async-done | bytes 147488 | tf_op jit(solution)/shard_map/all_to_all | solution.py:481
  76.6 1.5 %sum.1 = bf16[72,128]{1,0:T(8,128)(2,1)} custom-call(bf16[8,72,128]{2,1,0:T(8,128)(2,1)} %all-to-all-done.1.parts_ref, bf16[96,2,2,256]{3,2,1,0:T(2,128)(2,1)} %bitcast.42), custom_call_target="tpu_custom_call" | custom-call | tf_op jit(solution)/shard_map/sum/pallas_call | solution.py:466
  79.0 13.8 %all_to_all.16 = bf16[32,72,128]{2,1,0:T(8,128)(2,1)S(1)} all-to-all(bf16[32,72,128]{2,1,0:T(8,128)(2,1)S(1)} %broadcast_in_dim.8), channel_id=1, replica_groups=mesh['xh'=2,'zh'=8,'zl'=2,'xl'=2,'y'=4,'core'=2] {'xh','xl','y','zl'}, dimensions={0} | all-to-all | bytes 1179648 | tf_op jit(solution)/shard_map/all_to_all | solution.py:481
  92.8 6.5 %collective-permute-start.3 = (bf16[2304,128]{1,0:T(8,128)(2,1)S(1)}, bf16[2304,128]{1,0:T(8,128)(2,1)S(1)}, u32[]{:S(2)}, u32[]{:S(2)}) collective-permute-start(bf16[2304,128]{1,0:T(8,128)(2,1)S(1)} %bitcast.33), channel_id=1, source_target_pairs={{0,1},{1,0},{2,3},{3,2},{4,5},{5,4},{6,7},{7,6},{8,9},{9,8},{10,11... | collective-permute-start | bytes 1769480 | tf_op jit(solution)/shard_map/ppermute | solution.py:511
  99.3 2.0 %finish.2 = (f32[2592,192]{1,0:T(8,128)}, f32[96,768]{1,0:T(8,128)S(1)}) custom-call(s32[1]{0:T(128)} %bitcast.1.core_ref.half_ref, bf16[2304,128]{1,0:T(8,128)(2,1)S(1)} %bitcast.34), custom_call_target="tpu_custom_call" | custom-call | tf_op jit(solution)/shard_map/finish/pallas_call | solution.py:437
  101.3 2.0 %finish.3 = (f32[2592,192]{1,0:T(8,128)}, f32[96,768]{1,0:T(8,128)S(1)}) custom-call(s32[1]{0:T(128)S(6)} %sub.3.half_ref, bf16[2304,128]{1,0:T(8,128)(2,1)S(1)} %collective-permute-done.3.rows_hbm, f32[2592,192]{1,0:T(8,128)} %get-tuple-element.20.refs_0_, f32[96,768]{1,0:T(8,128)S(1)} %get-tuple-element.21.refs_1_), custom_call_target="tpu_custom_call", output_to_operand_aliasing={{0}: (2, {}), {1}: (3, {})} | custom-call | tf_op jit(solution)/shard_map/finish/pallas_call | solution.py:437
  103.2 1.5 %reshape.68 = f32[4,24,24,27]{3,2,1,0:T(8,128)} reshape(f32[96,648]{1,0:T(8,128)S(1)} %bitcast.37) | data formatting | bytes 497664 | tf_op jit(solution)/shard_map/reshape | solution.py:515
  (22 shorter events, 3.0 us)
Async XLA Ops:
  0.6 18.3 %copy-start = (bf16[27,96,192]{2,1,0:T(8,128)(2,1)S(1)}, bf16[27,96,192]{2,1,0:T(8,128)(2,1)}, u32[]{:S(2)}) copy-start(bf16[27,96,192]{2,1,0:T(8,128)(2,1)} %param.6) | copy-start | bytes 2985988
  2.6 15.3 %collective-permute-start.1 = (bf16[5,96,256]{2,1,0:T(8,128)(2,1)S(1)}, bf16[5,96,256]{2,1,0:T(8,128)(2,1)S(1)}, u32[]{:S(2)}, u32[]{:S(2)}) collective-permute-start(bf16[5,96,256]{2,1,0:T(8,128)(2,1)S(1)} %pad_maximum_fusion.own_hbm), channel_id=1, source_target_pairs={{0,1},{1,0},{2,3},{3,2},{4,5},{5,4},{6,7},{7,6},{8,9},{9,8},{10,11... | collective-permute-start | bytes 737288 | tf_op jit(solution)/shard_map/ppermute | solution.py:495
  11.4 7.5 %collective-permute-start = (bf16[5,96,256]{2,1,0:T(8,128)(2,1)S(1)}, bf16[5,96,256]{2,1,0:T(8,128)(2,1)S(1)}, u32[]{:S(2)}, u32[]{:S(2)}) collective-permute-start(bf16[5,96,256]{2,1,0:T(8,128)(2,1)S(1)} %pad_maximum_fusion.own_hbm), channel_id=1, source_target_pairs={{1,2},{3,4},{5,6},{7,8},{9,10},{11,12},{13,14},{2,1},{4,3},{6,5},{... | collective-permute-start | bytes 737288 | tf_op jit(solution)/shard_map/ppermute | solution.py:489
  15.6 3.3 %copy-start.3 = (bf16[27,4,24,24]{3,2,1,0:T(8,128)(2,1)}, bf16[27,4,24,24]{3,2,1,0:T(8,128)(2,1)S(1)}, u32[]{:S(2)}) copy-start(bf16[27,4,24,24]{3,2,1,0:T(8,128)(2,1)S(1)} %copy.17) | copy-start | bytes 373252
  26.7 4.6 %copy-start.1 = (bf16[2592,128]{1,0:T(8,128)(2,1)}, bf16[2592,128]{1,0:T(8,128)(2,1)S(1)}, u32[]{:S(2)}) copy-start(bf16[2592,128]{1,0:T(8,128)(2,1)S(1)} %get-tuple-element.17.wn_hbm) | copy-start | bytes 1990660
  26.8 36.3 %copy-start.4 = (bf16[27,4,24,24]{3,2,1,0:T(8,128)(2,1)S(1)}, bf16[27,4,24,24]{3,2,1,0:T(8,128)(2,1)}, u32[]{:S(2)}) copy-start(bf16[27,4,24,24]{3,2,1,0:T(8,128)(2,1)} %copy-done.3) | copy-start | bytes 373252
  26.8 4.0 %collective-permute-start.2 = (bf16[2304,128]{1,0:T(8,128)(2,1)S(1)}, bf16[2304,128]{1,0:T(8,128)(2,1)S(1)}, u32[]{:S(2)}, u32[]{:S(2)}) collective-permute-start(bf16[2304,128]{1,0:T(8,128)(2,1)S(1)} %get-tuple-element.15), channel_id=1, source_target_pairs={{0,1},{1,0},{2,3},{3,2},{4,5},{5,4},{6,7},{7,6},{8,9},{9,8},{10,11... | collective-permute-start | bytes 1769480 | tf_op jit(solution)/shard_map/ppermute | solution.py:503
  49.2 27.5 %all-to-all-start.1 = ((bf16[8,72,128]{2,1,0:T(8,128)(2,1)}), bf16[8,72,128]{2,1,0:T(8,128)(2,1)}, u32[]{:S(2)}, u32[]{:S(2)}) async-start(bf16[8,72,128]{2,1,0:T(8,128)(2,1)} %broadcast_in_dim.7), calls=%async_computation.1 | async-start | bytes 294912 | tf_op jit(solution)/shard_map/all_to_all | solution.py:481
  65.0 1.1 %copy-start.2 = (bf16[2592,128]{1,0:T(8,128)(2,1)S(1)}, bf16[2592,128]{1,0:T(8,128)(2,1)}, u32[]{:S(2)}) copy-start(bf16[2592,128]{1,0:T(8,128)(2,1)} %copy-done.1) | copy-start | bytes 1990660
  92.8 8.4 %collective-permute-start.3 = (bf16[2304,128]{1,0:T(8,128)(2,1)S(1)}, bf16[2304,128]{1,0:T(8,128)(2,1)S(1)}, u32[]{:S(2)}, u32[]{:S(2)}) collective-permute-start(bf16[2304,128]{1,0:T(8,128)(2,1)S(1)} %bitcast.33), channel_id=1, source_target_pairs={{0,1},{1,0},{2,3},{3,2},{4,5},{5,4},{6,7},{7,6},{8,9},{9,8},{10,11... | collective-permute-start | bytes 1769480 | tf_op jit(solution)/shard_map/ppermute | solution.py:511

commit v6 on v5

--- a/solution.py
+++ b/solution.py
@@ -116,12 +116,29 @@
     return jnp.where(mask, dot(narrow, fold), 0.0).astype(BF16)
 
 
+def prepare_kernel(fw_ref, w1_hbm, w1, sem):
+    row = lax.broadcasted_iota(jnp.int32, (3 * 256, PG * TAPS), 0)
+    column = lax.broadcasted_iota(jnp.int32, (1, PG * TAPS), 1)
+    channel = quotient(column, TAPS, 16)
+    tap = column - TAPS * channel
+    plane = quotient(tap, 9, 16)
+    order = ones_where(row == plane * 256 + (tap - 9 * plane) * PG + channel)
+    narrow = dot_nt(fw_ref[...], order).astype(BF16)
+    mask = group_mask()
+    fold = fold_matrix(256)
+    for a in range(3):
+        w1[pl.ds(a * CH, CH), :] = expand(narrow[:, a * 256 : (a + 1) * 256], fold, mask)
+    send = pltpu.make_async_copy(w1, w1_hbm, sem)
+    send.start()
+    send.wait()
+
+
 def cotangent_of(slab):
     return jnp.concatenate([slab[4, :, :LANES], slab[4, :, LANES:]], axis=0)
 
 
 def main_kernel(
-    inner_ref, core_ref, far_hbm, own_hbm, twin_hbm, fw_ref, w2_hbm,
+    inner_ref, core_ref, far_hbm, own_hbm, twin_hbm, w1_hbm, w2_hbm,
     mine_hbm, other_hbm, wn_hbm, g_hbm,
     beside, own_ref, w2_ref, mine_ref, other_ref, wn_ref, g_ref,
     xs, w1, pre_ref, xc_ref, gs, order_ref, fg, sems,
@@ -133,15 +150,13 @@
         pltpu.make_async_copy(own_hbm, own_ref, sems.at[0]),
         pltpu.make_async_copy(far_hbm, beside.at[core], sems.at[1]),
         pltpu.make_async_copy(twin_hbm, beside.at[1 - core], sems.at[2]),
-        pltpu.make_async_copy(w2_hbm, w2_ref, sems.at[3]),
+        pltpu.make_async_copy(w1_hbm, w1, sems.at[3]),
+        pltpu.make_async_copy(w2_hbm, w2_ref, sems.at[4]),
     ]
     for fetch in fetches:
         fetch.start()
     split = split_matrix()
     mask = group_mask()
-    fold = fold_matrix(9 * PG)
-    for a in range(3):
-        w1[pl.ds(a * CH, CH), :] = expand(fw_ref[pl.ds(a * CH, CH), :], fold, mask)
     fetches[0].wait()
     for e in (2, 3, 0, 1, 4, 5):
         slab = (low_ref, own_ref, high_ref)[e // 2]
@@ -155,6 +170,7 @@
             if 1 <= e <= 4:
                 xc_ref[e - 1, :, pl.ds(y * 256, 256)] = parts[:, :256]
         fill_windows(xs.at[e], tiles)
+    fetches[3].wait()
     for e in range(6):
         first, last = max(0, e - 3), min(2, e)
         terms = dot(w1[pl.ds(first * CH, (last - first + 1) * CH), :], xs[e])
@@ -200,7 +216,7 @@
     with_above = jnp.concatenate([cot, cotangent_of(high_ref)], axis=1)
     with_below = jnp.concatenate([cot, cotangent_of(low_ref)], axis=1)
     order_ref[...] = order_matrix()
-    fetches[3].wait()
+    fetches[4].wait()
     spread = [
         dot(w2_ref[pl.ds((9 * a + 3) * CH, 6 * CH), :], with_below if a == 2 else with_above)
         for a in range(3)
@@ -360,6 +376,18 @@
 MIB = 1024 * 1024
 
 
+def prepare_call(weight):
+    return pl.pallas_call(
+        prepare_kernel,
+        out_shape=jax.ShapeDtypeStruct((3 * CH, WIN), BF16),
+        in_specs=[VMEM],
+        out_specs=ANY,
+        scratch_shapes=[pltpu.VMEM((3 * CH, WIN), BF16), pltpu.SemaphoreType.DMA],
+        compiler_params=pltpu.CompilerParams(vmem_limit_bytes=16 * MIB),
+        name="prepare",
+    )(weight)
+
+
 def main_call(inner, core, far, own, twin, weight, w2):
     return pl.pallas_call(
         main_kernel,
@@ -369,7 +397,7 @@
             jax.ShapeDtypeStruct((TAPS * CH, LANES), BF16),
             jax.ShapeDtypeStruct((4, CH, 8 * LANES), BF16),
         ),
-        in_specs=[SMEM, SMEM, ANY, ANY, ANY, VMEM, ANY],
+        in_specs=[SMEM, SMEM] + [ANY] * 5,
         out_specs=(ANY,) * 4,
         scratch_shapes=[
             pltpu.VMEM((2, 5, CH, 256), BF16),
@@ -386,7 +414,7 @@
             pltpu.VMEM((2, WIN, 512), BF16),
             pltpu.VMEM((768, 768), BF16),
             pltpu.VMEM((CH, 6 * LANES), BF16),
-            pltpu.SemaphoreType.DMA((4,)),
+            pltpu.SemaphoreType.DMA((5,)),
         ],
         compiler_params=pltpu.CompilerParams(vmem_limit_bytes=40 * MIB),
         name="main",
@@ -455,21 +483,18 @@
     )(half, rows, *before)
 
 
-def sum_kernel(parts_ref, after_hbm, out_ref):
-    total = parts_ref[0].astype(F32)
-    for k in range(1, parts_ref.shape[0]):
-        total = total + parts_ref[k].astype(F32)
-    out_ref[...] = total.astype(BF16)
-
-
-def sum_call(parts, after):
+def zero_kernel(after_hbm, out_ref):
+    out_ref[0] = 0.0
+
+
+def zero_call(after):
     return pl.pallas_call(
-        sum_kernel,
-        out_shape=jax.ShapeDtypeStruct(parts.shape[1:], BF16),
-        in_specs=[VMEM, ANY],
-        out_specs=VMEM,
-        name="sum",
-    )(parts, after)
+        zero_kernel,
+        out_shape=jax.ShapeDtypeStruct((1,), F32),
+        in_specs=[ANY],
+        out_specs=SMEM,
+        name="zero",
+    )(after)
 
 
 def sum_pieces(parts):
@@ -486,17 +511,17 @@
     planes = volume[0].transpose(1, 2, 0, 3).reshape(4, CH, 256)
     cotangent = out_cotangent.reshape(2, CH, LANES).transpose(1, 0, 2).reshape(1, CH, 256)
     own = jnp.concatenate([planes, cotangent], axis=0)
+    swap = [(0, 1), (1, 0)]
+    twin = lax.ppermute(own, "core", swap)
     far = lax.ppermute(
         own,
         SPACE,
         [(i, i + 1) for i in range(1, count - 1, 2)] + [(i, i - 1) for i in range(2, count, 2)],
     )
-    swap = [(0, 1), (1, 0)]
-    twin = lax.ppermute(own, "core", swap)
     core = lax.axis_index("core").astype(jnp.int32).reshape(1)
     inner = jnp.where(lax.axis_index(SPACE) > 0, 1.0, 0.0).astype(F32).reshape(1)
     blocks = first_weight.reshape(3, 9, 4, PG, PG)
-    forward_weight = blocks.transpose(0, 2, 4, 1, 3).reshape(3 * CH, 9 * PG)
+    forward_weight = prepare_call(first_weight.transpose(1, 3, 2, 0).reshape(CH, PG * TAPS))
     backward_weight = blocks[::-1, ::-1].transpose(0, 2, 3, 1, 4).reshape(3 * CH, 9 * PG)
     w2 = second_weight.reshape(TAPS * CH, 192)
     mine, other, windows, grads = main_call(inner, core, far, own, twin, forward_weight, w2)
@@ -506,7 +531,8 @@
     feat, vgrad = tail_call(piece, grads, windows, w2, backward_weight)
     features = feat.reshape(out_cotangent.shape)
     volume_grad = vgrad.reshape(2, CH, 2, 256).transpose(1, 0, 2, 3)
-    piece = sum_call(to_all(piece, "zh", lax.axis_size("zh")), volume_grad)
+    parts = to_all(piece, "zh", lax.axis_size("zh"))
+    piece = lax.reduce(parts.astype(F32), zero_call(volume_grad)[0], lax.add, (0,)).astype(BF16)
     own_half = to_all(piece, NEAR, PIECES).reshape(ROWS, LANES)
     other_half = lax.ppermute(own_half, "core", swap)
     factor = 1.0 / math.sqrt(lax.axis_size(DP) * lax.axis_size(SPACE) * LANES)

time: 105 us -> 104 us (level)
  waiting for transfers between devices: 9.39 us -> 5.85 us
    all_to_all x1, waiting for transfers between devices: 6.46 us -> 0.98 us  [to_all(): return lax.all_to_all(copies, axes, 0, 0, tiled=True)]
    ppermute x1, waiting for transfers between devices: 0.95 us -> 2.89 us  [shards(): lax.ppermute(own, SPACE, [(i, i + 1) for i in range(1, count - 1, 2)] + [...]
    reshape x2 -> x1, local copies, waits for them, and re-layouts: 2.05 us -> 0.34 us  [shards(): first_weight.transpose(1, 3, 2, 0).reshape(CH, PG * TAPS)]
    reshape x2, local copies, waits for them, and re-layouts: 0.47 us -> 2.05 us  [shards(): blocks[::-1, ::-1].transpose(0, 2, 3, 1, 4).reshape(3 * CH, 9 * PG)]
    transpose x2, local copies, waits for them, and re-layouts: 1.39 us -> 2.95 us  [shards(): blocks[::-1, ::-1].transpose(0, 2, 3, 1, 4).reshape(3 * CH, 9 * PG)]
    unnamed x11 -> x7, local copies, waits for them, and re-layouts: 3.37 us -> 2.27 us
  transfers between devices with their start and end apart: 5 -> 5, of which waited for: 3 -> 3; matrix products, arithmetic and copies ran while one was open for 7% -> 9% of each run, Pallas kernels for 5% -> 7%
where the time goes in v6:
time: 104 us; the launch traced here: 103 us
  starting transfers between devices  33.1 us (32%)
  blocking collectives  30.9 us (30%)
  Pallas kernels  17.3 us (17%)
  local copies, waits for them, and re-layouts  13.8 us (13%)
  waiting for transfers between devices  5.85 us (6%)
  between operations  1.51 us (1%)
  other arithmetic  1.06 us (1%)
    all_to_all x1, blocking collectives, shards(): lax.all_to_all(chip.reshape(PIECES, PIECE, LANES), NEAR, 0, 0, tiled=True)  17.1 us
    all_to_all x1, starting transfers between devices, to_all(): return lax.all_to_all(copies, axes, 0, 0, tiled=True)  14 us
    all_to_all x1, blocking collectives, to_all(): return lax.all_to_all(copies, axes, 0, 0, tiled=True)  13.8 us
    ppermute x1, starting transfers between devices, shards(): twin = lax.ppermute(own, 'core', swap)  8.79 us
    pallas_call x1, Pallas kernels, main_call(): pl.pallas_call(main_kernel, out_shape=(jax.ShapeDtypeStruct((ROWS, LANES)...  7.9 us
    ppermute x1, starting transfers between devices, shards(): other_half = lax.ppermute(own_half, 'core', swap)  6.47 us
    pallas_call x2, Pallas kernels, finish_call(): pl.pallas_call(functools.partial(finish_kernel, factor), out_shape=(jax.S...  3.92 us
    pallas_call x1, Pallas kernels, tail_call(): pl.pallas_call(tail_kernel, out_shape=(jax.ShapeDtypeStruct((192, LANES),...  3.25 us
  transfers between devices with their start and end apart: 5, of which 3 were waited for; matrix products, arithmetic and copies ran while one was open for 9% of the time, Pallas kernels for 7%

profile of v6, /device:TPU:1, one launch (start us, length us, event | category | flops | bytes accessed | tf_op | source)
XLA Modules:
  0.0 103.5 jit_solution(12777871224916048691)
XLA Ops:
  0.6 0.9 copy.34
  1.6 1.0 copy.22
  2.6 8.8 %collective-permute-start.1 = (bf16[5,96,256]{2,1,0:T(8,128)(2,1)S(1)}, bf16[5,96,256]{2,1,0:T(8,128)(2,1)S(1)}, u32[]{:S(2)}, u32[]{:S(2)}) collective-permute-start(bf16[5,96,256]{2,1,0:T(8,128)(2,1)S(1)} %pad_maximum_fusion.own_hbm), channel_id=1, source_target_pairs={{0,1},{1,0},{2,3},{3,2},{4,5},{5,4},{6,7},{7,6},{8,9},{9,8},{10,11... | collective-permute-start | bytes 737288 | tf_op jit(solution)/shard_map/ppermute | solution.py:515
  11.4 1.9 %collective-permute-start = (bf16[5,96,256]{2,1,0:T(8,128)(2,1)S(1)}, bf16[5,96,256]{2,1,0:T(8,128)(2,1)S(1)}, u32[]{:S(2)}, u32[]{:S(2)}) collective-permute-start(bf16[5,96,256]{2,1,0:T(8,128)(2,1)S(1)} %pad_maximum_fusion.own_hbm), channel_id=1, source_target_pairs={{1,2},{3,4},{5,6},{7,8},{9,10},{11,12},{13,14},{2,1},{4,3},{6,5},{... | collective-permute-start | bytes 737288 | tf_op jit(solution)/shard_map/ppermute | solution.py:516
  13.3 1.1 %copy.24 = bf16[4,24,24,27]{3,2,1,0:T(8,128)(2,1)S(1)} copy(bf16[4,24,24,27]{3,1,2,0:T(8,128)(2,1)} %bitcast.40) | data formatting | bytes 248832 | tf_op jit(solution)/shard_map/transpose | solution.py:524
  14.8 1.2 %prepare.1.w1_hbm = bf16[288,864]{1,0:T(8,128)(2,1)S(1)} custom-call(bf16[96,648]{1,0:T(8,128)(2,1)S(1)} %reshape.61.fw_ref), custom_call_target="tpu_custom_call" | custom-call | tf_op jit(solution)/shard_map/prepare/pallas_call | solution.py:380
  16.0 2.9 %collective-permute-done.far_hbm = bf16[5,96,256]{2,1,0:T(8,128)(2,1)S(1)} collective-permute-done((bf16[5,96,256]{2,1,0:T(8,128)(2,1)S(1)}, bf16[5,96,256]{2,1,0:T(8,128)(2,1)S(1)}, u32[]{:S(2)}, u32[]{:S(2)}) %collective-permute-start) | collective-permute-done | bytes 245792 | tf_op jit(solution)/shard_map/ppermute | solution.py:516
  18.9 7.9 %main.1 = (bf16[2304,128]{1,0:T(8,128)(2,1)S(1)}, bf16[2304,128]{1,0:T(8,128)(2,1)S(1)}, bf16[2592,128]{1,0:T(8,128)(2,1)S(1)}, bf16[4,96,1024]{2,1,0:T(8,128)(2,1)S(1)}) custom-call(f32[1]{0:T(128)} %bitcast.inner_ref, s32[1]{0:T(128)} %bitcast.1.core_ref.half_ref, bf16[5,96,256]{2,1,0:T(8,128)(2,1)S(1)} %collective-permute-done.far_hbm, ...), custom_call_target="tpu_custom_call" | custom-call | tf_op jit(solution)/shard_map/main/pallas_call | solution.py:392
  26.9 1.9 %collective-permute-start.2 = (bf16[2304,128]{1,0:T(8,128)(2,1)S(1)}, bf16[2304,128]{1,0:T(8,128)(2,1)S(1)}, u32[]{:S(2)}, u32[]{:S(2)}) collective-permute-start(bf16[2304,128]{1,0:T(8,128)(2,1)S(1)} %get-tuple-element.15), channel_id=1, source_target_pairs={{0,1},{1,0},{2,3},{3,2},{4,5},{5,4},{6,7},{7,6},{8,9},{9,8},{10,11... | collective-permute-start | bytes 1769480 | tf_op jit(solution)/shard_map/ppermute | solution.py:528
  28.8 2.0 %collective-permute-done.2.got_hbm = bf16[2304,128]{1,0:T(8,128)(2,1)S(1)} collective-permute-done((bf16[2304,128]{1,0:T(8,128)(2,1)S(1)}, bf16[2304,128]{1,0:T(8,128)(2,1)S(1)}, u32[]{:S(2)}, u32[]{:S(2)}) %collective-permute-start.2) | collective-permute-done | bytes 589856 | tf_op jit(solution)/shard_map/ppermute | solution.py:528
  31.3 17.1 %all_to_all.15 = bf16[32,72,128]{2,1,0:T(8,128)(2,1)S(1)} all-to-all(bf16[32,72,128]{2,1,0:T(8,128)(2,1)S(1)} %bitcast.32), channel_id=1, replica_groups=mesh['xh'=2,'zh'=8,'zl'=2,'xl'=2,'y'=4,'core'=2] {'xh','xl','y','zl'}, dimensions={0} | all-to-all | bytes 1179648 | tf_op jit(solution)/shard_map/all_to_all | solution.py:529
  49.1 14.0 %all-to-all-start.1 = ((bf16[8,72,128]{2,1,0:T(8,128)(2,1)}), bf16[8,72,128]{2,1,0:T(8,128)(2,1)}, u32[]{:S(2)}, u32[]{:S(2)}) async-start(bf16[8,72,128]{2,1,0:T(8,128)(2,1)} %broadcast_in_dim.7), calls=%async_computation.1 | async-start | bytes 294912 | tf_op jit(solution)/shard_map/all_to_all | solution.py:506
  63.2 2.3 %copy.25 = bf16[27,4,24,24]{3,2,1,0:T(8,128)(2,1)S(1)} copy(bf16[27,4,24,24]{0,3,2,1:T(8,128)(2,1)} %param.5) | data formatting | bytes 248832 | tf_op args[1]
  66.3 2.0 %copy.26 = bf16[3,4,24,9,24]{2,1,0,4,3:T(4,128)(2,1)S(1)} copy(bf16[3,4,24,9,24]{4,2,1,3,0:T(8,128)(2,1)} %reverse_bitcast_fusion) | data formatting | bytes 248832 | tf_op jit(solution)/shard_map/transpose | solution.py:525
  68.4 1.0 reshape.65
  69.4 1.0 copy.27.fw_ref
  70.5 3.2 %tail.1 = (bf16[192,128]{1,0:T(8,128)(2,1)}, bf16[2,96,512]{2,1,0:T(8,128)(2,1)S(1)}) custom-call(bf16[72,128]{1,0:T(8,128)(2,1)S(1)} %reduce_sum.12.after_hbm, bf16[4,96,1024]{2,1,0:T(8,128)(2,1)S(1)} %get-tuple-element.16.g_hbm, bf16[2592,128]{1,0:T(8,128)(2,1)S(1)} %copy-done.2, bf16[2592,192]{1,0:T(8,128)(2,1)S(1)} %bitcast.36, ...), custom_call_target="tpu_custom_call" | custom-call | flops 1000000000 | bytes 4000000 | tf_op jit(solution)/shard_map/tail/pallas_call | solution.py:425
  75.8 1.0 all-to-all-done.1
  76.7 0.9 reduce.17
  77.8 13.8 %all_to_all.16 = bf16[32,72,128]{2,1,0:T(8,128)(2,1)S(1)} all-to-all(bf16[32,72,128]{2,1,0:T(8,128)(2,1)S(1)} %broadcast_in_dim.8), channel_id=1, replica_groups=mesh['xh'=2,'zh'=8,'zl'=2,'xl'=2,'y'=4,'core'=2] {'xh','xl','y','zl'}, dimensions={0} | all-to-all | bytes 1179648 | tf_op jit(solution)/shard_map/all_to_all | solution.py:506
  91.6 6.5 %collective-permute-start.3 = (bf16[2304,128]{1,0:T(8,128)(2,1)S(1)}, bf16[2304,128]{1,0:T(8,128)(2,1)S(1)}, u32[]{:S(2)}, u32[]{:S(2)}) collective-permute-start(bf16[2304,128]{1,0:T(8,128)(2,1)S(1)} %bitcast.33), channel_id=1, source_target_pairs={{0,1},{1,0},{2,3},{3,2},{4,5},{5,4},{6,7},{7,6},{8,9},{9,8},{10,11... | collective-permute-start | bytes 1769480 | tf_op jit(solution)/shard_map/ppermute | solution.py:537
  98.1 2.0 %finish.2 = (f32[2592,192]{1,0:T(8,128)}, f32[96,768]{1,0:T(8,128)S(1)}) custom-call(s32[1]{0:T(128)} %bitcast.1.core_ref.half_ref, bf16[2304,128]{1,0:T(8,128)(2,1)S(1)} %bitcast.34), custom_call_target="tpu_custom_call" | custom-call | tf_op jit(solution)/shard_map/finish/pallas_call | solution.py:465
  100.0 2.0 %finish.3 = (f32[2592,192]{1,0:T(8,128)}, f32[96,768]{1,0:T(8,128)S(1)}) custom-call(s32[1]{0:T(128)S(6)} %sub.3.half_ref, bf16[2304,128]{1,0:T(8,128)(2,1)S(1)} %collective-permute-done.3.rows_hbm, f32[2592,192]{1,0:T(8,128)} %get-tuple-element.20.refs_0_, f32[96,768]{1,0:T(8,128)S(1)} %get-tuple-element.21.refs_1_), custom_call_target="tpu_custom_call", output_to_operand_aliasing={{0}: (2, {}), {1}: (3, {})} | custom-call | tf_op jit(solution)/shard_map/finish/pallas_call | solution.py:465
  102.0 1.5 %reshape.69 = f32[4,24,24,27]{3,2,1,0:T(8,128)} reshape(f32[96,648]{1,0:T(8,128)S(1)} %bitcast.37) | data formatting | bytes 497664 | tf_op jit(solution)/shard_map/reshape | solution.py:541
  (19 shorter events, 4.1 us)
Async XLA Ops:
  0.6 18.3 %copy-start = (bf16[27,96,192]{2,1,0:T(8,128)(2,1)S(1)}, bf16[27,96,192]{2,1,0:T(8,128)(2,1)}, u32[]{:S(2)}) copy-start(bf16[27,96,192]{2,1,0:T(8,128)(2,1)} %param.6) | copy-start | bytes 2985988
  2.6 13.4 %collective-permute-start.1 = (bf16[5,96,256]{2,1,0:T(8,128)(2,1)S(1)}, bf16[5,96,256]{2,1,0:T(8,128)(2,1)S(1)}, u32[]{:S(2)}, u32[]{:S(2)}) collective-permute-start(bf16[5,96,256]{2,1,0:T(8,128)(2,1)S(1)} %pad_maximum_fusion.own_hbm), channel_id=1, source_target_pairs={{0,1},{1,0},{2,3},{3,2},{4,5},{5,4},{6,7},{7,6},{8,9},{9,8},{10,11... | collective-permute-start | bytes 737288 | tf_op jit(solution)/shard_map/ppermute | solution.py:515
  11.4 7.5 %collective-permute-start = (bf16[5,96,256]{2,1,0:T(8,128)(2,1)S(1)}, bf16[5,96,256]{2,1,0:T(8,128)(2,1)S(1)}, u32[]{:S(2)}, u32[]{:S(2)}) collective-permute-start(bf16[5,96,256]{2,1,0:T(8,128)(2,1)S(1)} %pad_maximum_fusion.own_hbm), channel_id=1, source_target_pairs={{1,2},{3,4},{5,6},{7,8},{9,10},{11,12},{13,14},{2,1},{4,3},{6,5},{... | collective-permute-start | bytes 737288 | tf_op jit(solution)/shard_map/ppermute | solution.py:516
  26.8 4.4 %copy-start.1 = (bf16[2592,128]{1,0:T(8,128)(2,1)}, bf16[2592,128]{1,0:T(8,128)(2,1)S(1)}, u32[]{:S(2)}) copy-start(bf16[2592,128]{1,0:T(8,128)(2,1)S(1)} %get-tuple-element.17.wn_hbm) | copy-start | bytes 1990660
  26.9 3.9 %collective-permute-start.2 = (bf16[2304,128]{1,0:T(8,128)(2,1)S(1)}, bf16[2304,128]{1,0:T(8,128)(2,1)S(1)}, u32[]{:S(2)}, u32[]{:S(2)}) collective-permute-start(bf16[2304,128]{1,0:T(8,128)(2,1)S(1)} %get-tuple-element.15), channel_id=1, source_target_pairs={{0,1},{1,0},{2,3},{3,2},{4,5},{5,4},{6,7},{7,6},{8,9},{9,8},{10,11... | collective-permute-start | bytes 1769480 | tf_op jit(solution)/shard_map/ppermute | solution.py:528
  49.1 21.3 %copy-start.2 = (bf16[2592,128]{1,0:T(8,128)(2,1)S(1)}, bf16[2592,128]{1,0:T(8,128)(2,1)}, u32[]{:S(2)}) copy-start(bf16[2592,128]{1,0:T(8,128)(2,1)} %copy-done.1) | copy-start | bytes 1990660
  49.1 27.6 %all-to-all-start.1 = ((bf16[8,72,128]{2,1,0:T(8,128)(2,1)}), bf16[8,72,128]{2,1,0:T(8,128)(2,1)}, u32[]{:S(2)}, u32[]{:S(2)}) async-start(bf16[8,72,128]{2,1,0:T(8,128)(2,1)} %broadcast_in_dim.7), calls=%async_computation.1 | async-start | bytes 294912 | tf_op jit(solution)/shard_map/all_to_all | solution.py:506
  91.6 8.4 %collective-permute-start.3 = (bf16[2304,128]{1,0:T(8,128)(2,1)S(1)}, bf16[2304,128]{1,0:T(8,128)(2,1)S(1)}, u32[]{:S(2)}, u32[]{:S(2)}) collective-permute-start(bf16[2304,128]{1,0:T(8,128)(2,1)S(1)} %bitcast.33), channel_id=1, source_target_pairs={{0,1},{1,0},{2,3},{3,2},{4,5},{5,4},{6,7},{7,6},{8,9},{9,8},{10,11... | collective-permute-start | bytes 1769480 | tf_op jit(solution)/shard_map/ppermute | solution.py:537

commit v7 on v6

--- a/solution.py
+++ b/solution.py
@@ -116,20 +116,29 @@
     return jnp.where(mask, dot(narrow, fold), 0.0).astype(BF16)
 
 
-def prepare_kernel(fw_ref, w1_hbm, w1, sem):
+def fill_weights(w1, fw, flip):
     row = lax.broadcasted_iota(jnp.int32, (3 * 256, PG * TAPS), 0)
     column = lax.broadcasted_iota(jnp.int32, (1, PG * TAPS), 1)
     channel = quotient(column, TAPS, 16)
     tap = column - TAPS * channel
+    if flip:
+        tap = TAPS - 1 - tap
     plane = quotient(tap, 9, 16)
     order = ones_where(row == plane * 256 + (tap - 9 * plane) * PG + channel)
-    narrow = dot_nt(fw_ref[...], order).astype(BF16)
+    narrow = dot_nt(fw, order).astype(BF16)
     mask = group_mask()
     fold = fold_matrix(256)
     for a in range(3):
         w1[pl.ds(a * CH, CH), :] = expand(narrow[:, a * 256 : (a + 1) * 256], fold, mask)
-    send = pltpu.make_async_copy(w1, w1_hbm, sem)
+
+
+def prepare_kernel(own_hbm, fw_ref, w1_hbm, again_hbm, w1, sems):
+    copy = pltpu.make_async_copy(own_hbm, again_hbm, sems.at[0])
+    copy.start()
+    fill_weights(w1, fw_ref[...], False)
+    send = pltpu.make_async_copy(w1, w1_hbm, sems.at[1])
     send.start()
+    copy.wait()
     send.wait()
 
 
@@ -290,10 +299,7 @@
     ]
     for fetch in fetches:
         fetch.start()
-    mask = group_mask()
-    fold = fold_matrix(9 * PG)
-    for a in range(3):
-        w1[pl.ds(a * CH, CH), :] = expand(fw_ref[pl.ds(a * CH, CH), :], fold, mask)
+    fill_weights(w1, fw_ref[...], True)
     fetches[0].wait()
     for j in range(4):
         tiles = [
@@ -376,16 +382,19 @@
 MIB = 1024 * 1024
 
 
-def prepare_call(weight):
+def prepare_call(own, weight):
     return pl.pallas_call(
         prepare_kernel,
-        out_shape=jax.ShapeDtypeStruct((3 * CH, WIN), BF16),
-        in_specs=[VMEM],
-        out_specs=ANY,
-        scratch_shapes=[pltpu.VMEM((3 * CH, WIN), BF16), pltpu.SemaphoreType.DMA],
+        out_shape=(
+            jax.ShapeDtypeStruct((3 * CH, WIN), BF16),
+            jax.ShapeDtypeStruct(own.shape, BF16),
+        ),
+        in_specs=[ANY, VMEM],
+        out_specs=(ANY, ANY),
+        scratch_shapes=[pltpu.VMEM((3 * CH, WIN), BF16), pltpu.SemaphoreType.DMA((2,))],
         compiler_params=pltpu.CompilerParams(vmem_limit_bytes=16 * MIB),
         name="prepare",
-    )(weight)
+    )(own, weight)
 
 
 def main_call(inner, core, far, own, twin, weight, w2):
@@ -512,7 +521,6 @@
     cotangent = out_cotangent.reshape(2, CH, LANES).transpose(1, 0, 2).reshape(1, CH, 256)
     own = jnp.concatenate([planes, cotangent], axis=0)
     swap = [(0, 1), (1, 0)]
-    twin = lax.ppermute(own, "core", swap)
     far = lax.ppermute(
         own,
         SPACE,
@@ -520,9 +528,10 @@
     )
     core = lax.axis_index("core").astype(jnp.int32).reshape(1)
     inner = jnp.where(lax.axis_index(SPACE) > 0, 1.0, 0.0).astype(F32).reshape(1)
-    blocks = first_weight.reshape(3, 9, 4, PG, PG)
-    forward_weight = prepare_call(first_weight.transpose(1, 3, 2, 0).reshape(CH, PG * TAPS))
-    backward_weight = blocks[::-1, ::-1].transpose(0, 2, 3, 1, 4).reshape(3 * CH, 9 * PG)
+    forward_weight = first_weight.transpose(1, 3, 2, 0).reshape(CH, PG * TAPS)
+    forward_weight, again = prepare_call(own, forward_weight)
+    twin = lax.ppermute(again, "core", swap)
+    backward_weight = first_weight.transpose(1, 2, 3, 0).reshape(CH, PG * TAPS)
     w2 = second_weight.reshape(TAPS * CH, 192)
     mine, other, windows, grads = main_call(inner, core, far, own, twin, forward_weight, w2)
     chip = add_call(mine, lax.ppermute(other, "core", swap))

time: 104 us -> 101 us (0.971)
  local copies, waits for them, and re-layouts: 13.8 us -> 7.97 us
  waiting for transfers between devices: 5.85 us -> 9.12 us
    all_to_all x1, waiting for transfers between devices: 0.98 us -> 6.41 us  [to_all(): return lax.all_to_all(copies, axes, 0, 0, tiled=True)]
    ppermute x1, starting transfers between devices: 8.79 us -> 4.87 us  [shards(): twin = lax.ppermute(again, 'core', swap)]
    transpose x3 -> x1, local copies, waits for them, and re-layouts: 4.1 us -> 1.14 us  [shards(): forward_weight = first_weight.transpose(1, 3, 2, 0).reshape(CH, PG * TAPS)]
    ppermute x1, waiting for transfers between devices: 2.89 us -> 0.01 us  [shards(): lax.ppermute(own, SPACE, [(i, i + 1) for i in range(1, count - 1, 2)] + [...]
    ppermute x1, starting transfers between devices: 1.92 us -> 4.59 us  [shards(): lax.ppermute(own, SPACE, [(i, i + 1) for i in range(1, count - 1, 2)] + [...]
    reshape x3 -> x2, local copies, waits for them, and re-layouts: 2.39 us -> 0.68 us  [the longest x1 0.34 us: shards(): forward_weight = first_weight.transpose(1, 3, 2, 0).reshape(CH, PG * TAPS)]
    unnamed x7 -> x8, local copies, waits for them, and re-layouts: 2.27 us -> 1.1 us
    ppermute x1, waiting for transfers between devices: 0.01 us -> 1.09 us  [shards(): twin = lax.ppermute(again, 'core', swap)]
  transfers between devices with their start and end apart: 5 -> 5, of which waited for: 3 -> 3; matrix products, arithmetic and copies ran while one was open for 9% -> 3% of each run, Pallas kernels for 7% -> 7%
where the time goes in v7:
time: 101 us; the launch traced here: 100 us
  starting transfers between devices  32.3 us (32%)
  blocking collectives  31.4 us (31%)
  Pallas kernels  17.9 us (18%)
  waiting for transfers between devices  9.12 us (9%)
  local copies, waits for them, and re-layouts  7.97 us (8%)
  between operations  1.5 us (1%)
    all_to_all x1, blocking collectives, shards(): lax.all_to_all(chip.reshape(PIECES, PIECE, LANES), NEAR, 0, 0, tiled=True)  17.6 us
    all_to_all x1, starting transfers between devices, to_all(): return lax.all_to_all(copies, axes, 0, 0, tiled=True)  13.9 us
    all_to_all x1, blocking collectives, to_all(): return lax.all_to_all(copies, axes, 0, 0, tiled=True)  13.8 us
    pallas_call x1, Pallas kernels, main_call(): pl.pallas_call(main_kernel, out_shape=(jax.ShapeDtypeStruct((ROWS, LANES)...  7.9 us
    ppermute x1, starting transfers between devices, shards(): other_half = lax.ppermute(own_half, 'core', swap)  6.47 us
    all_to_all x1, waiting for transfers between devices, to_all(): return lax.all_to_all(copies, axes, 0, 0, tiled=True)  6.41 us
    ppermute x1, starting transfers between devices, shards(): twin = lax.ppermute(again, 'core', swap)  4.87 us
    ppermute x1, starting transfers between devices, shards(): lax.ppermute(own, SPACE, [(i, i + 1) for i in range(1, count - 1, 2)] + [...  4.59 us
  transfers between devices with their start and end apart: 5, of which 3 were waited for; matrix products, arithmetic and copies ran while one was open for 3% of the time, Pallas kernels for 7%

profile of v7, /device:TPU:1, one launch (start us, length us, event | category | flops | bytes accessed | tf_op | source)
XLA Modules:
  0.0 100.3 jit_solution(14497707760651777528)
XLA Ops:
  0.6 0.9 copy.23
  1.6 1.0 copy.14
  2.6 4.6 %collective-permute-start = (bf16[5,96,256]{2,1,0:T(8,128)(2,1)S(1)}, bf16[5,96,256]{2,1,0:T(8,128)(2,1)S(1)}, u32[]{:S(2)}, u32[]{:S(2)}) collective-permute-start(bf16[5,96,256]{2,1,0:T(8,128)(2,1)S(1)} %pad_maximum_fusion.own_hbm), channel_id=1, source_target_pairs={{1,2},{3,4},{5,6},{7,8},{9,10},{11,12},{13,14},{2,1},{4,3},{6,5},{... | collective-permute-start | bytes 737288 | tf_op jit(solution)/shard_map/ppermute | solution.py:524
  7.2 1.1 %copy.16 = bf16[4,24,24,27]{3,2,1,0:T(8,128)(2,1)S(1)} copy(bf16[4,24,24,27]{3,1,2,0:T(8,128)(2,1)} %bitcast.37) | data formatting | bytes 248832 | tf_op jit(solution)/shard_map/transpose | solution.py:531
  8.7 1.5 %prepare.1 = (bf16[288,864]{1,0:T(8,128)(2,1)S(1)}, bf16[5,96,256]{2,1,0:T(8,128)(2,1)S(1)}) custom-call(bf16[5,96,256]{2,1,0:T(8,128)(2,1)S(1)} %pad_maximum_fusion.own_hbm, bf16[96,648]{1,0:T(8,128)(2,1)S(1)} %reshape.58.fw_ref), custom_call_target="tpu_custom_call" | custom-call | tf_op jit(solution)/shard_map/prepare/pallas_call | solution.py:386
  10.2 4.9 %collective-permute-start.1 = (bf16[5,96,256]{2,1,0:T(8,128)(2,1)S(1)}, bf16[5,96,256]{2,1,0:T(8,128)(2,1)S(1)}, u32[]{:S(2)}, u32[]{:S(2)}) collective-permute-start(bf16[5,96,256]{2,1,0:T(8,128)(2,1)S(1)} %get-tuple-element.16), channel_id=1, source_target_pairs={{0,1},{1,0},{2,3},{3,2},{4,5},{5,4},{6,7},{7,6},{8,9},{9,8},{10,11... | collective-permute-start | bytes 737288 | tf_op jit(solution)/shard_map/ppermute | solution.py:533
  15.1 1.1 %collective-permute-done.1.twin_hbm = bf16[5,96,256]{2,1,0:T(8,128)(2,1)S(1)} collective-permute-done((bf16[5,96,256]{2,1,0:T(8,128)(2,1)S(1)}, bf16[5,96,256]{2,1,0:T(8,128)(2,1)S(1)}, u32[]{:S(2)}, u32[]{:S(2)}) %collective-permute-start.1) | collective-permute-done | bytes 245792 | tf_op jit(solution)/shard_map/ppermute | solution.py:533
  16.2 7.9 %main.1 = (bf16[2304,128]{1,0:T(8,128)(2,1)S(1)}, bf16[2304,128]{1,0:T(8,128)(2,1)S(1)}, bf16[2592,128]{1,0:T(8,128)(2,1)S(1)}, bf16[4,96,1024]{2,1,0:T(8,128)(2,1)S(1)}) custom-call(f32[1]{0:T(128)} %bitcast.inner_ref, s32[1]{0:T(128)} %bitcast.1.core_ref.half_ref, bf16[5,96,256]{2,1,0:T(8,128)(2,1)S(1)} %collective-permute-done.far_hbm, ...), custom_call_target="tpu_custom_call" | custom-call | tf_op jit(solution)/shard_map/main/pallas_call | solution.py:401
  24.1 2.4 %collective-permute-start.2 = (bf16[2304,128]{1,0:T(8,128)(2,1)S(1)}, bf16[2304,128]{1,0:T(8,128)(2,1)S(1)}, u32[]{:S(2)}, u32[]{:S(2)}) collective-permute-start(bf16[2304,128]{1,0:T(8,128)(2,1)S(1)} %get-tuple-element.19), channel_id=1, source_target_pairs={{0,1},{1,0},{2,3},{3,2},{4,5},{5,4},{6,7},{7,6},{8,9},{9,8},{10,11... | collective-permute-start | bytes 1769480 | tf_op jit(solution)/shard_map/ppermute | solution.py:537
  26.6 1.6 %collective-permute-done.2.got_hbm = bf16[2304,128]{1,0:T(8,128)(2,1)S(1)} collective-permute-done((bf16[2304,128]{1,0:T(8,128)(2,1)S(1)}, bf16[2304,128]{1,0:T(8,128)(2,1)S(1)}, u32[]{:S(2)}, u32[]{:S(2)}) %collective-permute-start.2) | collective-permute-done | bytes 589856 | tf_op jit(solution)/shard_map/ppermute | solution.py:537
  28.2 0.5 add.12
  28.7 17.6 %all_to_all.15 = bf16[32,72,128]{2,1,0:T(8,128)(2,1)S(1)} all-to-all(bf16[32,72,128]{2,1,0:T(8,128)(2,1)S(1)} %bitcast.30), channel_id=1, replica_groups=mesh['xh'=2,'zh'=8,'zl'=2,'xl'=2,'y'=4,'core'=2] {'xh','xl','y','zl'}, dimensions={0} | all-to-all | bytes 1179648 | tf_op jit(solution)/shard_map/all_to_all | solution.py:538
  46.4 0.7 broadcast_in_dim.7
  47.1 13.9 %all-to-all-start.1 = ((bf16[8,72,128]{2,1,0:T(8,128)(2,1)}), bf16[8,72,128]{2,1,0:T(8,128)(2,1)S(1)}, u32[]{:S(2)}, u32[]{:S(2)}) async-start(bf16[8,72,128]{2,1,0:T(8,128)(2,1)} %broadcast_in_dim.7), calls=%async_computation.1 | async-start | bytes 294912 | tf_op jit(solution)/shard_map/all_to_all | solution.py:515
  61.4 1.1 %copy-done.2 = bf16[2592,128]{1,0:T(8,128)(2,1)S(1)} copy-done((bf16[2592,128]{1,0:T(8,128)(2,1)S(1)}, bf16[2592,128]{1,0:T(8,128)(2,1)}, u32[]{:S(2)}) %copy-start.2) | copy-done | bytes 663576
  62.4 3.6 %tail.1 = (bf16[192,128]{1,0:T(8,128)(2,1)}, bf16[2,96,512]{2,1,0:T(8,128)(2,1)S(1)}) custom-call(bf16[72,128]{1,0:T(8,128)(2,1)S(1)} %reduce_sum.12.after_hbm, bf16[4,96,1024]{2,1,0:T(8,128)(2,1)S(1)} %get-tuple-element.20.g_hbm, bf16[2592,128]{1,0:T(8,128)(2,1)S(1)} %copy-done.2, bf16[2592,192]{1,0:T(8,128)(2,1)S(1)} %bitcast.34, ...), custom_call_target="tpu_custom_call" | custom-call | flops 1000000000 | bytes 4000000 | tf_op jit(solution)/shard_map/tail/pallas_call | solution.py:434
  66.1 0.8 copy.22
  66.9 0.5 zero.1
  68.1 6.4 %all-to-all-done.1 = bf16[8,72,128]{2,1,0:T(8,128)(2,1)S(1)} async-done(((bf16[8,72,128]{2,1,0:T(8,128)(2,1)}), bf16[8,72,128]{2,1,0:T(8,128)(2,1)S(1)}, u32[]{:S(2)}, u32[]{:S(2)}) %all-to-all-start.1) | async-done | bytes 147488 | tf_op jit(solution)/shard_map/all_to_all | solution.py:515
  74.6 13.8 %all_to_all.16 = bf16[32,72,128]{2,1,0:T(8,128)(2,1)S(1)} all-to-all(bf16[32,72,128]{2,1,0:T(8,128)(2,1)S(1)} %broadcast_in_dim.8), channel_id=1, replica_groups=mesh['xh'=2,'zh'=8,'zl'=2,'xl'=2,'y'=4,'core'=2] {'xh','xl','y','zl'}, dimensions={0} | all-to-all | bytes 1179648 | tf_op jit(solution)/shard_map/all_to_all | solution.py:515
  88.4 6.5 %collective-permute-start.3 = (bf16[2304,128]{1,0:T(8,128)(2,1)S(1)}, bf16[2304,128]{1,0:T(8,128)(2,1)S(1)}, u32[]{:S(2)}, u32[]{:S(2)}) collective-permute-start(bf16[2304,128]{1,0:T(8,128)(2,1)S(1)} %bitcast.31), channel_id=1, source_target_pairs={{0,1},{1,0},{2,3},{3,2},{4,5},{5,4},{6,7},{7,6},{8,9},{9,8},{10,11... | collective-permute-start | bytes 1769480 | tf_op jit(solution)/shard_map/ppermute | solution.py:546
  94.9 2.0 %finish.2 = (f32[2592,192]{1,0:T(8,128)}, f32[96,768]{1,0:T(8,128)S(1)}) custom-call(s32[1]{0:T(128)} %bitcast.1.core_ref.half_ref, bf16[2304,128]{1,0:T(8,128)(2,1)S(1)} %bitcast.32), custom_call_target="tpu_custom_call" | custom-call | tf_op jit(solution)/shard_map/finish/pallas_call | solution.py:474
  96.9 2.0 %finish.3 = (f32[2592,192]{1,0:T(8,128)}, f32[96,768]{1,0:T(8,128)S(1)}) custom-call(s32[1]{0:T(128)S(6)} %sub.3.half_ref, bf16[2304,128]{1,0:T(8,128)(2,1)S(1)} %collective-permute-done.3.rows_hbm, f32[2592,192]{1,0:T(8,128)} %get-tuple-element.24.refs_0_, f32[96,768]{1,0:T(8,128)S(1)} %get-tuple-element.25.refs_1_), custom_call_target="tpu_custom_call", output_to_operand_aliasing={{0}: (2, {}), {1}: (3, {})} | custom-call | tf_op jit(solution)/shard_map/finish/pallas_call | solution.py:474
  98.8 1.5 %reshape.65 = f32[4,24,24,27]{3,2,1,0:T(8,128)} reshape(f32[96,648]{1,0:T(8,128)S(1)} %bitcast.35) | data formatting | bytes 497664 | tf_op jit(solution)/shard_map/reshape | solution.py:550
  (17 shorter events, 1.0 us)
Async XLA Ops:
  0.6 15.6 %copy-start = (bf16[27,96,192]{2,1,0:T(8,128)(2,1)S(1)}, bf16[27,96,192]{2,1,0:T(8,128)(2,1)}, u32[]{:S(2)}) copy-start(bf16[27,96,192]{2,1,0:T(8,128)(2,1)} %param.6) | copy-start | bytes 2985988
  2.6 12.5 %collective-permute-start = (bf16[5,96,256]{2,1,0:T(8,128)(2,1)S(1)}, bf16[5,96,256]{2,1,0:T(8,128)(2,1)S(1)}, u32[]{:S(2)}, u32[]{:S(2)}) collective-permute-start(bf16[5,96,256]{2,1,0:T(8,128)(2,1)S(1)} %pad_maximum_fusion.own_hbm), channel_id=1, source_target_pairs={{1,2},{3,4},{5,6},{7,8},{9,10},{11,12},{13,14},{2,1},{4,3},{6,5},{... | collective-permute-start | bytes 737288 | tf_op jit(solution)/shard_map/ppermute | solution.py:524
  10.2 6.0 %collective-permute-start.1 = (bf16[5,96,256]{2,1,0:T(8,128)(2,1)S(1)}, bf16[5,96,256]{2,1,0:T(8,128)(2,1)S(1)}, u32[]{:S(2)}, u32[]{:S(2)}) collective-permute-start(bf16[5,96,256]{2,1,0:T(8,128)(2,1)S(1)} %get-tuple-element.16), channel_id=1, source_target_pairs={{0,1},{1,0},{2,3},{3,2},{4,5},{5,4},{6,7},{7,6},{8,9},{9,8},{10,11... | collective-permute-start | bytes 737288 | tf_op jit(solution)/shard_map/ppermute | solution.py:533
  24.1 4.6 %copy-start.1 = (bf16[2592,128]{1,0:T(8,128)(2,1)}, bf16[2592,128]{1,0:T(8,128)(2,1)S(1)}, u32[]{:S(2)}) copy-start(bf16[2592,128]{1,0:T(8,128)(2,1)S(1)} %get-tuple-element.21.wn_hbm) | copy-start | bytes 1990660
  24.1 36.9 %copy-start.3 = (bf16[27,4,24,24]{0,3,2,1:T(8,128)(2,1)S(1)}, bf16[27,4,24,24]{0,3,2,1:T(8,128)(2,1)}, u32[]{:S(2)}) copy-start(bf16[27,4,24,24]{0,3,2,1:T(8,128)(2,1)} %param.5) | copy-start | bytes 373252
  24.1 4.0 %collective-permute-start.2 = (bf16[2304,128]{1,0:T(8,128)(2,1)S(1)}, bf16[2304,128]{1,0:T(8,128)(2,1)S(1)}, u32[]{:S(2)}, u32[]{:S(2)}) collective-permute-start(bf16[2304,128]{1,0:T(8,128)(2,1)S(1)} %get-tuple-element.19), channel_id=1, source_target_pairs={{0,1},{1,0},{2,3},{3,2},{4,5},{5,4},{6,7},{7,6},{8,9},{9,8},{10,11... | collective-permute-start | bytes 1769480 | tf_op jit(solution)/shard_map/ppermute | solution.py:537
  47.1 27.4 %all-to-all-start.1 = ((bf16[8,72,128]{2,1,0:T(8,128)(2,1)}), bf16[8,72,128]{2,1,0:T(8,128)(2,1)S(1)}, u32[]{:S(2)}, u32[]{:S(2)}) async-start(bf16[8,72,128]{2,1,0:T(8,128)(2,1)} %broadcast_in_dim.7), calls=%async_computation.1 | async-start | bytes 294912 | tf_op jit(solution)/shard_map/all_to_all | solution.py:515
  61.4 1.1 %copy-start.2 = (bf16[2592,128]{1,0:T(8,128)(2,1)S(1)}, bf16[2592,128]{1,0:T(8,128)(2,1)}, u32[]{:S(2)}) copy-start(bf16[2592,128]{1,0:T(8,128)(2,1)} %copy-done.1) | copy-start | bytes 1990660
  88.4 8.4 %collective-permute-start.3 = (bf16[2304,128]{1,0:T(8,128)(2,1)S(1)}, bf16[2304,128]{1,0:T(8,128)(2,1)S(1)}, u32[]{:S(2)}, u32[]{:S(2)}) collective-permute-start(bf16[2304,128]{1,0:T(8,128)(2,1)S(1)} %bitcast.31), channel_id=1, source_target_pairs={{0,1},{1,0},{2,3},{3,2},{4,5},{5,4},{6,7},{7,6},{8,9},{9,8},{10,11... | collective-permute-start | bytes 1769480 | tf_op jit(solution)/shard_map/ppermute | solution.py:546

commit v8 on v6

--- a/solution.py
+++ b/solution.py
@@ -116,18 +116,30 @@
     return jnp.where(mask, dot(narrow, fold), 0.0).astype(BF16)
 
 
-def prepare_kernel(fw_ref, w1_hbm, w1, sem):
+def fill_weights(w1, fw, flip):
     row = lax.broadcasted_iota(jnp.int32, (3 * 256, PG * TAPS), 0)
     column = lax.broadcasted_iota(jnp.int32, (1, PG * TAPS), 1)
     channel = quotient(column, TAPS, 16)
     tap = column - TAPS * channel
+    if flip:
+        tap = TAPS - 1 - tap
     plane = quotient(tap, 9, 16)
     order = ones_where(row == plane * 256 + (tap - 9 * plane) * PG + channel)
-    narrow = dot_nt(fw_ref[...], order).astype(BF16)
+    narrow = dot_nt(fw, order).astype(BF16)
     mask = group_mask()
     fold = fold_matrix(256)
     for a in range(3):
         w1[pl.ds(a * CH, CH), :] = expand(narrow[:, a * 256 : (a + 1) * 256], fold, mask)
+
+
+def again_kernel(own_hbm, after_hbm, again_hbm, sem):
+    copy = pltpu.make_async_copy(own_hbm, again_hbm, sem)
+    copy.start()
+    copy.wait()
+
+
+def prepare_kernel(fw_ref, w1_hbm, w1, sem):
+    fill_weights(w1, fw_ref[...], False)
     send = pltpu.make_async_copy(w1, w1_hbm, sem)
     send.start()
     send.wait()
@@ -290,10 +302,7 @@
     ]
     for fetch in fetches:
         fetch.start()
-    mask = group_mask()
-    fold = fold_matrix(9 * PG)
-    for a in range(3):
-        w1[pl.ds(a * CH, CH), :] = expand(fw_ref[pl.ds(a * CH, CH), :], fold, mask)
+    fill_weights(w1, fw_ref[...], True)
     fetches[0].wait()
     for j in range(4):
         tiles = [
@@ -376,6 +385,18 @@
 MIB = 1024 * 1024
 
 
+def again_call(own, after):
+    return pl.pallas_call(
+        again_kernel,
+        out_shape=jax.ShapeDtypeStruct(own.shape, BF16),
+        in_specs=[ANY, ANY],
+        out_specs=ANY,
+        scratch_shapes=[pltpu.SemaphoreType.DMA],
+        compiler_params=pltpu.CompilerParams(vmem_limit_bytes=MIB),
+        name="again",
+    )(own, after)
+
+
 def prepare_call(weight):
     return pl.pallas_call(
         prepare_kernel,
@@ -383,7 +404,7 @@
         in_specs=[VMEM],
         out_specs=ANY,
         scratch_shapes=[pltpu.VMEM((3 * CH, WIN), BF16), pltpu.SemaphoreType.DMA],
-        compiler_params=pltpu.CompilerParams(vmem_limit_bytes=16 * MIB),
+        compiler_params=pltpu.CompilerParams(vmem_limit_bytes=6 * MIB),
         name="prepare",
     )(weight)
 
@@ -416,7 +437,7 @@
             pltpu.VMEM((CH, 6 * LANES), BF16),
             pltpu.SemaphoreType.DMA((5,)),
         ],
-        compiler_params=pltpu.CompilerParams(vmem_limit_bytes=40 * MIB),
+        compiler_params=pltpu.CompilerParams(vmem_limit_bytes=24 * MIB),
         name="main",
     )(inner, core, far, own, twin, weight, w2)
 
@@ -439,7 +460,7 @@
             pltpu.VMEM((2, CH, 512), F32),
             pltpu.SemaphoreType.DMA((3,)),
         ],
-        compiler_params=pltpu.CompilerParams(vmem_limit_bytes=40 * MIB),
+        compiler_params=pltpu.CompilerParams(vmem_limit_bytes=12 * MIB),
         cost_estimate=pl.CostEstimate(flops=10**9, bytes_accessed=4 * 10**6, transcendentals=0),
         name="tail",
     )(after, grads, windows, w2, weight)
@@ -456,7 +477,7 @@
             pltpu.VMEM((ROWS, LANES), BF16),
             pltpu.SemaphoreType.DMA((2,)),
         ],
-        compiler_params=pltpu.CompilerParams(vmem_limit_bytes=16 * MIB),
+        compiler_params=pltpu.CompilerParams(vmem_limit_bytes=4 * MIB),
         name="add",
     )(mine, got)
 
@@ -478,7 +499,7 @@
             pltpu.SemaphoreType.DMA((4,)),
         ],
         input_output_aliases={2 + i: i for i in range(len(before))},
-        compiler_params=pltpu.CompilerParams(vmem_limit_bytes=16 * MIB),
+        compiler_params=pltpu.CompilerParams(vmem_limit_bytes=6 * MIB),
         name="finish",
     )(half, rows, *before)
 
@@ -493,6 +514,7 @@
         out_shape=jax.ShapeDtypeStruct((1,), F32),
         in_specs=[ANY],
         out_specs=SMEM,
+        compiler_params=pltpu.CompilerParams(vmem_limit_bytes=MIB),
         name="zero",
     )(after)
 
@@ -512,7 +534,6 @@
     cotangent = out_cotangent.reshape(2, CH, LANES).transpose(1, 0, 2).reshape(1, CH, 256)
     own = jnp.concatenate([planes, cotangent], axis=0)
     swap = [(0, 1), (1, 0)]
-    twin = lax.ppermute(own, "core", swap)
     far = lax.ppermute(
         own,
         SPACE,
@@ -520,19 +541,19 @@
     )
     core = lax.axis_index("core").astype(jnp.int32).reshape(1)
     inner = jnp.where(lax.axis_index(SPACE) > 0, 1.0, 0.0).astype(F32).reshape(1)
-    blocks = first_weight.reshape(3, 9, 4, PG, PG)
-    forward_weight = prepare_call(first_weight.transpose(1, 3, 2, 0).reshape(CH, PG * TAPS))
-    backward_weight = blocks[::-1, ::-1].transpose(0, 2, 3, 1, 4).reshape(3 * CH, 9 * PG)
+    forward_weight = first_weight.transpose(1, 3, 2, 0).reshape(CH, PG * TAPS)
+    twin = lax.ppermute(again_call(own, forward_weight), "core", swap)
+    forward_weight = prepare_call(forward_weight)
+    backward_weight = first_weight.transpose(1, 2, 3, 0).reshape(CH, PG * TAPS)
     w2 = second_weight.reshape(TAPS * CH, 192)
     mine, other, windows, grads = main_call(inner, core, far, own, twin, forward_weight, w2)
     chip = add_call(mine, lax.ppermute(other, "core", swap))
     parts = lax.all_to_all(chip.reshape(PIECES, PIECE, LANES), NEAR, 0, 0, tiled=True)
-    piece = sum_pieces(parts)
-    feat, vgrad = tail_call(piece, grads, windows, w2, backward_weight)
+    feat, vgrad = tail_call(chip, grads, windows, w2, backward_weight)
     features = feat.reshape(out_cotangent.shape)
     volume_grad = vgrad.reshape(2, CH, 2, 256).transpose(1, 0, 2, 3)
-    parts = to_all(piece, "zh", lax.axis_size("zh"))
     piece = lax.reduce(parts.astype(F32), zero_call(volume_grad)[0], lax.add, (0,)).astype(BF16)
+    piece = sum_pieces(to_all(piece, "zh", lax.axis_size("zh")))
     own_half = to_all(piece, NEAR, PIECES).reshape(ROWS, LANES)
     other_half = lax.ppermute(own_half, "core", swap)
     factor = 1.0 / math.sqrt(lax.axis_size(DP) * lax.axis_size(SPACE) * LANES)

time: 104 us -> 102 us (0.981)
  blocking collectives: 30.9 us -> 41 us
  starting transfers between devices: 33.1 us -> 24.5 us
  local copies, waits for them, and re-layouts: 13.8 us -> 6.64 us
  waiting for transfers between devices: 5.85 us -> 7.63 us
  Pallas kernels: 17.3 us -> 18.6 us
    all_to_all x1 -> x2, blocking collectives: 13.8 us -> 41 us  [to_all(): return lax.all_to_all(copies, axes, 0, 0, tiled=True)]
    all_to_all x1 -> x0, blocking collectives: 17.1 us -> none  [shards(): lax.all_to_all(chip.reshape(PIECES, PIECE, LANES), NEAR, 0, 0, tiled=True)]
    all_to_all x1, starting transfers between devices: 14 us -> 6.26 us  [shards(): lax.all_to_all(chip.reshape(PIECES, PIECE, LANES), NEAR, 0, 0, tiled=True)]
    all_to_all x1, waiting for transfers between devices: 0.98 us -> 5.89 us  [shards(): lax.all_to_all(chip.reshape(PIECES, PIECE, LANES), NEAR, 0, 0, tiled=True)]
    ppermute x1, starting transfers between devices: 8.79 us -> 4.87 us  [shards(): twin = lax.ppermute(again_call(own, forward_weight), 'core', swap)]
    transpose x3 -> x1, local copies, waits for them, and re-layouts: 4.1 us -> 1.14 us  [shards(): forward_weight = first_weight.transpose(1, 3, 2, 0).reshape(CH, PG * TAPS)]
    ppermute x1, waiting for transfers between devices: 2.89 us -> 0.01 us  [shards(): lax.ppermute(own, SPACE, [(i, i + 1) for i in range(1, count - 1, 2)] + [...]
    ppermute x1, starting transfers between devices: 1.92 us -> 4.59 us  [shards(): lax.ppermute(own, SPACE, [(i, i + 1) for i in range(1, count - 1, 2)] + [...]
  transfers between devices with their start and end apart: 5 -> 5, of which waited for: 3 -> 2; matrix products, arithmetic and copies ran while one was open for 9% -> 2% of each run, Pallas kernels for 7% -> 7%
where the time goes in v8:
time: 102 us; the launch traced here: 101 us
  blocking collectives  41 us (40%)
  starting transfers between devices  24.5 us (24%)
  Pallas kernels  18.6 us (18%)
  waiting for transfers between devices  7.63 us (7%)
  local copies, waits for them, and re-layouts  6.64 us (7%)
  between operations  1.57 us (2%)
  other arithmetic  1.21 us (1%)
    all_to_all x2, blocking collectives, to_all(): return lax.all_to_all(copies, axes, 0, 0, tiled=True)  41 us
    pallas_call x1, Pallas kernels, main_call(): pl.pallas_call(main_kernel, out_shape=(jax.ShapeDtypeStruct((ROWS, LANES)...  7.93 us
    ppermute x1, starting transfers between devices, shards(): other_half = lax.ppermute(own_half, 'core', swap)  6.47 us
    all_to_all x1, starting transfers between devices, shards(): lax.all_to_all(chip.reshape(PIECES, PIECE, LANES), NEAR, 0, 0, tiled=True)  6.26 us
    all_to_all x1, waiting for transfers between devices, shards(): lax.all_to_all(chip.reshape(PIECES, PIECE, LANES), NEAR, 0, 0, tiled=True)  5.89 us
    ppermute x1, starting transfers between devices, shards(): twin = lax.ppermute(again_call(own, forward_weight), 'core', swap)  4.87 us
    ppermute x1, starting transfers between devices, shards(): lax.ppermute(own, SPACE, [(i, i + 1) for i in range(1, count - 1, 2)] + [...  4.59 us
    pallas_call x2, Pallas kernels, finish_call(): pl.pallas_call(functools.partial(finish_kernel, factor), out_shape=(jax.S...  3.92 us
  transfers between devices with their start and end apart: 5, of which 2 were waited for; matrix products, arithmetic and copies ran while one was open for 2% of the time, Pallas kernels for 7%

profile of v8, /device:TPU:1, one launch (start us, length us, event | category | flops | bytes accessed | tf_op | source)
XLA Modules:
  0.0 101.1 jit_solution(5816406099620671339)
XLA Ops:
  0.6 0.9 copy.23
  1.6 1.0 copy.14
  2.6 4.6 %collective-permute-start = (bf16[5,96,256]{2,1,0:T(8,128)(2,1)S(1)}, bf16[5,96,256]{2,1,0:T(8,128)(2,1)S(1)}, u32[]{:S(2)}, u32[]{:S(2)}) collective-permute-start(bf16[5,96,256]{2,1,0:T(8,128)(2,1)S(1)} %pad_maximum_fusion.own_hbm), channel_id=1, source_target_pairs={{1,2},{3,4},{5,6},{7,8},{9,10},{11,12},{13,14},{2,1},{4,3},{6,5},{... | collective-permute-start | bytes 737288 | tf_op jit(solution)/shard_map/ppermute | solution.py:537
  7.2 1.1 %copy.16 = bf16[4,24,24,27]{3,2,1,0:T(8,128)(2,1)S(1)} copy(bf16[4,24,24,27]{3,1,2,0:T(8,128)(2,1)} %bitcast.38) | data formatting | bytes 248832 | tf_op jit(solution)/shard_map/transpose | solution.py:544
  8.4 0.3 reshape.58.after_hbm.fw_ref
  9.1 4.9 %collective-permute-start.1 = (bf16[5,96,256]{2,1,0:T(8,128)(2,1)S(1)}, bf16[5,96,256]{2,1,0:T(8,128)(2,1)S(1)}, u32[]{:S(2)}, u32[]{:S(2)}) collective-permute-start(bf16[5,96,256]{2,1,0:T(8,128)(2,1)S(1)} %again.1), channel_id=1, source_target_pairs={{0,1},{1,0},{2,3},{3,2},{4,5},{5,4},{6,7},{7,6},{8,9},{9,8},{10,11... | collective-permute-start | bytes 737288 | tf_op jit(solution)/shard_map/ppermute | solution.py:545
  13.9 1.2 %prepare.1.w1_hbm = bf16[288,864]{1,0:T(8,128)(2,1)S(1)} custom-call(bf16[96,648]{1,0:T(8,128)(2,1)S(1)} %reshape.58.after_hbm.fw_ref), custom_call_target="tpu_custom_call" | custom-call | tf_op jit(solution)/shard_map/prepare/pallas_call | solution.py:401
  15.1 7.9 %main.1 = (bf16[2304,128]{1,0:T(8,128)(2,1)S(1)}, bf16[2304,128]{1,0:T(8,128)(2,1)S(1)}, bf16[2592,128]{1,0:T(8,128)(2,1)S(1)}, bf16[4,96,1024]{2,1,0:T(8,128)(2,1)S(1)}) custom-call(f32[1]{0:T(128)} %bitcast.inner_ref, s32[1]{0:T(128)} %bitcast.1.core_ref.half_ref, bf16[5,96,256]{2,1,0:T(8,128)(2,1)S(1)} %collective-permute-done.far_hbm, ...), custom_call_target="tpu_custom_call" | custom-call | tf_op jit(solution)/shard_map/main/pallas_call | solution.py:413
  23.1 2.3 %collective-permute-start.2 = (bf16[2304,128]{1,0:T(8,128)(2,1)S(1)}, bf16[2304,128]{1,0:T(8,128)(2,1)S(1)}, u32[]{:S(2)}, u32[]{:S(2)}) collective-permute-start(bf16[2304,128]{1,0:T(8,128)(2,1)S(1)} %get-tuple-element.15), channel_id=1, source_target_pairs={{0,1},{1,0},{2,3},{3,2},{4,5},{5,4},{6,7},{7,6},{8,9},{9,8},{10,11... | collective-permute-start | bytes 1769480 | tf_op jit(solution)/shard_map/ppermute | solution.py:550
  25.4 1.7 %collective-permute-done.2.got_hbm = bf16[2304,128]{1,0:T(8,128)(2,1)S(1)} collective-permute-done((bf16[2304,128]{1,0:T(8,128)(2,1)S(1)}, bf16[2304,128]{1,0:T(8,128)(2,1)S(1)}, u32[]{:S(2)}, u32[]{:S(2)}) %collective-permute-start.2) | collective-permute-done | bytes 589856 | tf_op jit(solution)/shard_map/ppermute | solution.py:550
  27.1 1.2 %add.12.after_hbm = bf16[2304,128]{1,0:T(8,128)(2,1)} custom-call(bf16[2304,128]{1,0:T(8,128)(2,1)S(1)} %get-tuple-element.14.mine_hbm, bf16[2304,128]{1,0:T(8,128)(2,1)S(1)} %collective-permute-done.2.got_hbm), custom_call_target="tpu_custom_call" | custom-call | tf_op jit(solution)/shard_map/add/pallas_call | solution.py:470
  28.4 6.3 %all-to-all-start = ((bf16[32,72,128]{2,1,0:T(8,128)(2,1)}), bf16[32,72,128]{2,1,0:T(8,128)(2,1)}, u32[]{:S(2)}, u32[]{:S(2)}) async-start(bf16[32,72,128]{2,1,0:T(8,128)(2,1)} %bitcast.13), calls=%async_computation | async-start | bytes 1179648 | tf_op jit(solution)/shard_map/all_to_all | solution.py:551
  34.6 0.3 reshape.60.fw_ref
  35.0 1.1 %copy-done.3 = bf16[2592,128]{1,0:T(8,128)(2,1)S(1)} copy-done((bf16[2592,128]{1,0:T(8,128)(2,1)S(1)}, bf16[2592,128]{1,0:T(8,128)(2,1)}, u32[]{:S(2)}) %copy-start.3) | copy-done | bytes 663576
  36.1 3.6 %tail.1 = (bf16[192,128]{1,0:T(8,128)(2,1)}, bf16[2,96,512]{2,1,0:T(8,128)(2,1)S(1)}) custom-call(bf16[2304,128]{1,0:T(8,128)(2,1)} %add.12.after_hbm, bf16[4,96,1024]{2,1,0:T(8,128)(2,1)S(1)} %get-tuple-element.16.g_hbm, bf16[2592,128]{1,0:T(8,128)(2,1)S(1)} %copy-done.3, bf16[2592,192]{1,0:T(8,128)(2,1)S(1)} %bitcast.33, bf16[96,648]{1,0:T(8,128)(2,1)S(1)} %reshape.60.fw_ref), custom_call_target="tpu_custom_call" | custom-call | flops 1000000000 | bytes 4000000 | tf_op jit(solution)/shard_map/tail/pallas_call | solution.py:446
  39.9 0.5 zero.1
  41.0 5.9 %all-to-all-done = bf16[32,72,128]{2,1,0:T(8,128)(2,1)} async-done(((bf16[32,72,128]{2,1,0:T(8,128)(2,1)}), bf16[32,72,128]{2,1,0:T(8,128)(2,1)}, u32[]{:S(2)}, u32[]{:S(2)}) %all-to-all-start) | async-done | bytes 589856 | tf_op jit(solution)/shard_map/all_to_all | solution.py:551
  46.9 1.2 %reduce.17 = bf16[72,128]{1,0:T(8,128)(2,1)S(1)} reduce(bf16[32,72,128]{2,1,0:T(8,128)(2,1)} %all-to-all-done, bf16[]{:T(256)} %bitcast.14), dimensions={0}, to_apply=%region_0.1 | reduce | flops 285696 | bytes 608258 | tf_op jit(solution)/shard_map/reduce | solution.py:555
  48.1 27.2 %all_to_all.15 = bf16[8,72,128]{2,1,0:T(8,128)(2,1)S(1)} all-to-all(bf16[8,72,128]{2,1,0:T(8,128)(2,1)S(1)} %broadcast_in_dim.7), channel_id=1, replica_groups=mesh['xh'=2,'zh'=8,'zl'=2,'xl'=2,'y'=4,'core'=2] {'zh'}, dimensions={0} | all-to-all | bytes 294912 | tf_op jit(solution)/shard_map/all_to_all | solution.py:528
  75.4 13.8 %all_to_all.16 = bf16[32,72,128]{2,1,0:T(8,128)(2,1)S(1)} all-to-all(bf16[32,72,128]{2,1,0:T(8,128)(2,1)S(1)} %broadcast_in_dim.8), channel_id=1, replica_groups=mesh['xh'=2,'zh'=8,'zl'=2,'xl'=2,'y'=4,'core'=2] {'xh','xl','y','zl'}, dimensions={0} | all-to-all | bytes 1179648 | tf_op jit(solution)/shard_map/all_to_all | solution.py:528
  89.2 6.5 %collective-permute-start.3 = (bf16[2304,128]{1,0:T(8,128)(2,1)S(1)}, bf16[2304,128]{1,0:T(8,128)(2,1)S(1)}, u32[]{:S(2)}, u32[]{:S(2)}) collective-permute-start(bf16[2304,128]{1,0:T(8,128)(2,1)S(1)} %bitcast.30), channel_id=1, source_target_pairs={{0,1},{1,0},{2,3},{3,2},{4,5},{5,4},{6,7},{7,6},{8,9},{9,8},{10,11... | collective-permute-start | bytes 1769480 | tf_op jit(solution)/shard_map/ppermute | solution.py:558
  95.7 2.0 %finish.2 = (f32[2592,192]{1,0:T(8,128)}, f32[96,768]{1,0:T(8,128)S(1)}) custom-call(s32[1]{0:T(128)} %bitcast.1.core_ref.half_ref, bf16[2304,128]{1,0:T(8,128)(2,1)S(1)} %bitcast.31), custom_call_target="tpu_custom_call" | custom-call | tf_op jit(solution)/shard_map/finish/pallas_call | solution.py:486
  97.7 2.0 %finish.3 = (f32[2592,192]{1,0:T(8,128)}, f32[96,768]{1,0:T(8,128)S(1)}) custom-call(s32[1]{0:T(128)S(6)} %sub.3.half_ref, bf16[2304,128]{1,0:T(8,128)(2,1)S(1)} %collective-permute-done.3.rows_hbm, f32[2592,192]{1,0:T(8,128)} %get-tuple-element.20.refs_0_, f32[96,768]{1,0:T(8,128)S(1)} %get-tuple-element.21.refs_1_), custom_call_target="tpu_custom_call", output_to_operand_aliasing={{0}: (2, {}), {1}: (3, {})} | custom-call | tf_op jit(solution)/shard_map/finish/pallas_call | solution.py:486
  99.7 1.5 %reshape.65 = f32[4,24,24,27]{3,2,1,0:T(8,128)} reshape(f32[96,648]{1,0:T(8,128)S(1)} %bitcast.34) | data formatting | bytes 497664 | tf_op jit(solution)/shard_map/reshape | solution.py:562
  (20 shorter events, 0.7 us)
Async XLA Ops:
  0.6 14.5 %copy-start = (bf16[27,96,192]{2,1,0:T(8,128)(2,1)S(1)}, bf16[27,96,192]{2,1,0:T(8,128)(2,1)}, u32[]{:S(2)}) copy-start(bf16[27,96,192]{2,1,0:T(8,128)(2,1)} %param.6) | copy-start | bytes 2985988
  2.6 12.5 %collective-permute-start = (bf16[5,96,256]{2,1,0:T(8,128)(2,1)S(1)}, bf16[5,96,256]{2,1,0:T(8,128)(2,1)S(1)}, u32[]{:S(2)}, u32[]{:S(2)}) collective-permute-start(bf16[5,96,256]{2,1,0:T(8,128)(2,1)S(1)} %pad_maximum_fusion.own_hbm), channel_id=1, source_target_pairs={{1,2},{3,4},{5,6},{7,8},{9,10},{11,12},{13,14},{2,1},{4,3},{6,5},{... | collective-permute-start | bytes 737288 | tf_op jit(solution)/shard_map/ppermute | solution.py:537
  9.1 6.1 %collective-permute-start.1 = (bf16[5,96,256]{2,1,0:T(8,128)(2,1)S(1)}, bf16[5,96,256]{2,1,0:T(8,128)(2,1)S(1)}, u32[]{:S(2)}, u32[]{:S(2)}) collective-permute-start(bf16[5,96,256]{2,1,0:T(8,128)(2,1)S(1)} %again.1), channel_id=1, source_target_pairs={{0,1},{1,0},{2,3},{3,2},{4,5},{5,4},{6,7},{7,6},{8,9},{9,8},{10,11... | collective-permute-start | bytes 737288 | tf_op jit(solution)/shard_map/ppermute | solution.py:545
  23.1 5.3 %copy-start.2 = (bf16[2592,128]{1,0:T(8,128)(2,1)}, bf16[2592,128]{1,0:T(8,128)(2,1)S(1)}, u32[]{:S(2)}) copy-start(bf16[2592,128]{1,0:T(8,128)(2,1)S(1)} %get-tuple-element.17.wn_hbm) | copy-start | bytes 1990660
  23.1 11.5 %copy-start.4 = (bf16[27,4,24,24]{0,3,2,1:T(8,128)(2,1)S(1)}, bf16[27,4,24,24]{0,3,2,1:T(8,128)(2,1)}, u32[]{:S(2)}) copy-start(bf16[27,4,24,24]{0,3,2,1:T(8,128)(2,1)} %param.5) | copy-start | bytes 373252
  23.1 4.0 %collective-permute-start.2 = (bf16[2304,128]{1,0:T(8,128)(2,1)S(1)}, bf16[2304,128]{1,0:T(8,128)(2,1)S(1)}, u32[]{:S(2)}, u32[]{:S(2)}) collective-permute-start(bf16[2304,128]{1,0:T(8,128)(2,1)S(1)} %get-tuple-element.15), channel_id=1, source_target_pairs={{0,1},{1,0},{2,3},{3,2},{4,5},{5,4},{6,7},{7,6},{8,9},{9,8},{10,11... | collective-permute-start | bytes 1769480 | tf_op jit(solution)/shard_map/ppermute | solution.py:550
  28.4 18.6 %all-to-all-start = ((bf16[32,72,128]{2,1,0:T(8,128)(2,1)}), bf16[32,72,128]{2,1,0:T(8,128)(2,1)}, u32[]{:S(2)}, u32[]{:S(2)}) async-start(bf16[32,72,128]{2,1,0:T(8,128)(2,1)} %bitcast.13), calls=%async_computation | async-start | bytes 1179648 | tf_op jit(solution)/shard_map/all_to_all | solution.py:551
  35.0 1.1 %copy-start.3 = (bf16[2592,128]{1,0:T(8,128)(2,1)S(1)}, bf16[2592,128]{1,0:T(8,128)(2,1)}, u32[]{:S(2)}) copy-start(bf16[2592,128]{1,0:T(8,128)(2,1)} %copy-done.2) | copy-start | bytes 1990660
  39.8 59.8 %copy-start.1 = (bf16[2,96,2,256]{3,2,0,1:T(2,128)(2,1)}, bf16[2,96,2,256]{3,2,0,1:T(2,128)(2,1)S(1)}, u32[]{:S(2)}) copy-start(bf16[2,96,2,256]{3,2,0,1:T(2,128)(2,1)S(1)} %copy.22) | copy-start | bytes 589828
  89.2 8.4 %collective-permute-start.3 = (bf16[2304,128]{1,0:T(8,128)(2,1)S(1)}, bf16[2304,128]{1,0:T(8,128)(2,1)S(1)}, u32[]{:S(2)}, u32[]{:S(2)}) collective-permute-start(bf16[2304,128]{1,0:T(8,128)(2,1)S(1)} %bitcast.30), channel_id=1, source_target_pairs={{0,1},{1,0},{2,3},{3,2},{4,5},{5,4},{6,7},{7,6},{8,9},{9,8},{10,11... | collective-permute-start | bytes 1769480 | tf_op jit(solution)/shard_map/ppermute | solution.py:558

commit v9 on v8

--- a/solution.py
+++ b/solution.py
@@ -138,31 +138,24 @@
     copy.wait()
 
 
-def prepare_kernel(fw_ref, w1_hbm, w1, sem):
-    fill_weights(w1, fw_ref[...], False)
-    send = pltpu.make_async_copy(w1, w1_hbm, sem)
-    send.start()
-    send.wait()
-
-
 def cotangent_of(slab):
     return jnp.concatenate([slab[4, :, :LANES], slab[4, :, LANES:]], axis=0)
 
 
 def main_kernel(
-    inner_ref, core_ref, far_hbm, own_hbm, twin_hbm, w1_hbm, w2_hbm,
+    inner_ref, core_ref, far_hbm, own_hbm, twin_hbm, fw_hbm, w2_hbm,
     mine_hbm, other_hbm, wn_hbm, g_hbm,
-    beside, own_ref, w2_ref, mine_ref, other_ref, wn_ref, g_ref,
+    beside, own_ref, fw_ref, w2_ref, mine_ref, other_ref, wn_ref, g_ref,
     xs, w1, pre_ref, xc_ref, gs, order_ref, fg, sems,
 ):
     inner = inner_ref[0]
     core = core_ref[0]
     low_ref, high_ref = beside.at[0], beside.at[1]
     fetches = [
+        pltpu.make_async_copy(fw_hbm, fw_ref, sems.at[3]),
         pltpu.make_async_copy(own_hbm, own_ref, sems.at[0]),
         pltpu.make_async_copy(far_hbm, beside.at[core], sems.at[1]),
         pltpu.make_async_copy(twin_hbm, beside.at[1 - core], sems.at[2]),
-        pltpu.make_async_copy(w1_hbm, w1, sems.at[3]),
         pltpu.make_async_copy(w2_hbm, w2_ref, sems.at[4]),
     ]
     for fetch in fetches:
@@ -170,11 +163,13 @@
     split = split_matrix()
     mask = group_mask()
     fetches[0].wait()
+    fill_weights(w1, fw_ref[...], False)
+    fetches[1].wait()
     for e in (2, 3, 0, 1, 4, 5):
         slab = (low_ref, own_ref, high_ref)[e // 2]
         if e == 0:
-            fetches[1].wait()
             fetches[2].wait()
+            fetches[3].wait()
         tiles = []
         for y in range(2):
             parts = dot(slab[2 * (e % 2) + y], split).astype(BF16)
@@ -182,7 +177,6 @@
             if 1 <= e <= 4:
                 xc_ref[e - 1, :, pl.ds(y * 256, 256)] = parts[:, :256]
         fill_windows(xs.at[e], tiles)
-    fetches[3].wait()
     for e in range(6):
         first, last = max(0, e - 3), min(2, e)
         terms = dot(w1[pl.ds(first * CH, (last - first + 1) * CH), :], xs[e])
@@ -397,18 +391,6 @@
     )(own, after)
 
 
-def prepare_call(weight):
-    return pl.pallas_call(
-        prepare_kernel,
-        out_shape=jax.ShapeDtypeStruct((3 * CH, WIN), BF16),
-        in_specs=[VMEM],
-        out_specs=ANY,
-        scratch_shapes=[pltpu.VMEM((3 * CH, WIN), BF16), pltpu.SemaphoreType.DMA],
-        compiler_params=pltpu.CompilerParams(vmem_limit_bytes=6 * MIB),
-        name="prepare",
-    )(weight)
-
-
 def main_call(inner, core, far, own, twin, weight, w2):
     return pl.pallas_call(
         main_kernel,
@@ -423,6 +405,7 @@
         scratch_shapes=[
             pltpu.VMEM((2, 5, CH, 256), BF16),
             pltpu.VMEM((5, CH, 256), BF16),
+            pltpu.VMEM((CH, PG * TAPS), BF16),
             pltpu.VMEM((TAPS * CH, 192), BF16),
             pltpu.VMEM((ROWS, LANES), BF16),
             pltpu.VMEM((ROWS, LANES), BF16),
@@ -543,17 +526,17 @@
     inner = jnp.where(lax.axis_index(SPACE) > 0, 1.0, 0.0).astype(F32).reshape(1)
     forward_weight = first_weight.transpose(1, 3, 2, 0).reshape(CH, PG * TAPS)
     twin = lax.ppermute(again_call(own, forward_weight), "core", swap)
-    forward_weight = prepare_call(forward_weight)
     backward_weight = first_weight.transpose(1, 2, 3, 0).reshape(CH, PG * TAPS)
     w2 = second_weight.reshape(TAPS * CH, 192)
     mine, other, windows, grads = main_call(inner, core, far, own, twin, forward_weight, w2)
     chip = add_call(mine, lax.ppermute(other, "core", swap))
     parts = lax.all_to_all(chip.reshape(PIECES, PIECE, LANES), NEAR, 0, 0, tiled=True)
-    feat, vgrad = tail_call(chip, grads, windows, w2, backward_weight)
+    piece = sum_pieces(parts)
+    feat, vgrad = tail_call(piece, grads, windows, w2, backward_weight)
     features = feat.reshape(out_cotangent.shape)
     volume_grad = vgrad.reshape(2, CH, 2, 256).transpose(1, 0, 2, 3)
+    parts = to_all(piece, "zh", lax.axis_size("zh"))
     piece = lax.reduce(parts.astype(F32), zero_call(volume_grad)[0], lax.add, (0,)).astype(BF16)
-    piece = sum_pieces(to_all(piece, "zh", lax.axis_size("zh")))
     own_half = to_all(piece, NEAR, PIECES).reshape(ROWS, LANES)
     other_half = lax.ppermute(own_half, "core", swap)
     factor = 1.0 / math.sqrt(lax.axis_size(DP) * lax.axis_size(SPACE) * LANES)

time: 102 us -> 102 us (level)
  blocking collectives: 41 us -> 32.3 us
  starting transfers between devices: 24.5 us -> 32.3 us
  waiting for transfers between devices: 7.63 us -> 9.77 us
  Pallas kernels: 18.6 us -> 17.3 us
    all_to_all x2 -> x1, blocking collectives: 41 us -> 13.8 us  [to_all(): return lax.all_to_all(copies, axes, 0, 0, tiled=True)]
    all_to_all x0 -> x1, blocking collectives: none -> 18.5 us  [shards(): lax.all_to_all(chip.reshape(PIECES, PIECE, LANES), NEAR, 0, 0, tiled=True)]
    all_to_all x1, starting transfers between devices: 6.26 us -> 13.9 us  [to_all(): return lax.all_to_all(copies, axes, 0, 0, tiled=True)]
    all_to_all x1, waiting for transfers between devices: 5.89 us -> 7.06 us  [to_all(): return lax.all_to_all(copies, axes, 0, 0, tiled=True)]
    pallas_call x1 -> x0, Pallas kernels: 1.15 us -> none  [prepare_call(): pl.pallas_call(prepare_kernel, out_shape=jax.ShapeDtypeStruct((3 * CH, WI...]
    reduce_sum x1, other arithmetic: 0.03 us -> 1.16 us  [sum_pieces(): return jnp.sum(parts.astype(F32), axis=0).astype(BF16)]
    another operation x1, other arithmetic: 1.16 us -> 0.03 us  [shards(): lax.reduce(parts.astype(F32), zero_call(volume_grad)[0], lax.add, (0,))]
    ppermute x1, waiting for transfers between devices: 0.01 us -> 1.09 us  [shards(): twin = lax.ppermute(again_call(own, forward_weight), 'core', swap)]
  transfers between devices with their start and end apart: 5 -> 5, of which waited for: 2 -> 3; matrix products, arithmetic and copies ran while one was open for 2% -> 2% of each run, Pallas kernels for 7% -> 6%
where the time goes in v9:
time: 102 us
  starting transfers between devices  32.3 us (32%)
  blocking collectives  32.3 us (32%)
  Pallas kernels  17.3 us (17%)
  waiting for transfers between devices  9.77 us (10%)
  local copies, waits for them, and re-layouts  7.3 us (7%)
  between operations  1.52 us (1%)
  other arithmetic  1.21 us (1%)
    all_to_all x1, blocking collectives, shards(): lax.all_to_all(chip.reshape(PIECES, PIECE, LANES), NEAR, 0, 0, tiled=True)  18.5 us
    all_to_all x1, starting transfers between devices, to_all(): return lax.all_to_all(copies, axes, 0, 0, tiled=True)  13.9 us
    all_to_all x1, blocking collectives, to_all(): return lax.all_to_all(copies, axes, 0, 0, tiled=True)  13.8 us
    pallas_call x1, Pallas kernels, main_call(): pl.pallas_call(main_kernel, out_shape=(jax.ShapeDtypeStruct((ROWS, LANES)...  8.42 us
    all_to_all x1, waiting for transfers between devices, to_all(): return lax.all_to_all(copies, axes, 0, 0, tiled=True)  7.06 us
    ppermute x1, starting transfers between devices, shards(): other_half = lax.ppermute(own_half, 'core', swap)  6.47 us
    ppermute x1, starting transfers between devices, shards(): twin = lax.ppermute(again_call(own, forward_weight), 'core', swap)  4.87 us
    ppermute x1, starting transfers between devices, shards(): lax.ppermute(own, SPACE, [(i, i + 1) for i in range(1, count - 1, 2)] + [...  4.59 us
  transfers between devices with their start and end apart: 5, of which 3 were waited for; matrix products, arithmetic and copies ran while one was open for 2% of the time, Pallas kernels for 6%

profile of v9, /device:TPU:1, one launch (start us, length us, event | category | flops | bytes accessed | tf_op | source)
XLA Modules:
  0.0 101.6 jit_solution(15546155457783005280)
XLA Ops:
  0.6 0.9 copy.23
  1.6 1.0 copy.14
  2.6 4.6 %collective-permute-start = (bf16[5,96,256]{2,1,0:T(8,128)(2,1)S(1)}, bf16[5,96,256]{2,1,0:T(8,128)(2,1)S(1)}, u32[]{:S(2)}, u32[]{:S(2)}) collective-permute-start(bf16[5,96,256]{2,1,0:T(8,128)(2,1)S(1)} %pad_maximum_fusion.own_hbm), channel_id=1, source_target_pairs={{1,2},{3,4},{5,6},{7,8},{9,10},{11,12},{13,14},{2,1},{4,3},{6,5},{... | collective-permute-start | bytes 737288 | tf_op jit(solution)/shard_map/ppermute | solution.py:520
  7.2 1.1 %copy.16 = bf16[4,24,24,27]{3,2,1,0:T(8,128)(2,1)S(1)} copy(bf16[4,24,24,27]{3,1,2,0:T(8,128)(2,1)} %bitcast.39) | data formatting | bytes 248832 | tf_op jit(solution)/shard_map/transpose | solution.py:527
  8.4 0.3 reshape.58.after_hbm.fw_hbm
  9.1 4.9 %collective-permute-start.1 = (bf16[5,96,256]{2,1,0:T(8,128)(2,1)S(1)}, bf16[5,96,256]{2,1,0:T(8,128)(2,1)S(1)}, u32[]{:S(2)}, u32[]{:S(2)}) collective-permute-start(bf16[5,96,256]{2,1,0:T(8,128)(2,1)S(1)} %again.1), channel_id=1, source_target_pairs={{0,1},{1,0},{2,3},{3,2},{4,5},{5,4},{6,7},{7,6},{8,9},{9,8},{10,11... | collective-permute-start | bytes 737288 | tf_op jit(solution)/shard_map/ppermute | solution.py:528
  14.0 1.1 %collective-permute-done.1.twin_hbm = bf16[5,96,256]{2,1,0:T(8,128)(2,1)S(1)} collective-permute-done((bf16[5,96,256]{2,1,0:T(8,128)(2,1)S(1)}, bf16[5,96,256]{2,1,0:T(8,128)(2,1)S(1)}, u32[]{:S(2)}, u32[]{:S(2)}) %collective-permute-start.1) | collective-permute-done | bytes 245792 | tf_op jit(solution)/shard_map/ppermute | solution.py:528
  15.0 8.4 %main.1 = (bf16[2304,128]{1,0:T(8,128)(2,1)S(1)}, bf16[2304,128]{1,0:T(8,128)(2,1)S(1)}, bf16[2592,128]{1,0:T(8,128)(2,1)S(1)}, bf16[4,96,1024]{2,1,0:T(8,128)(2,1)S(1)}) custom-call(f32[1]{0:T(128)} %bitcast.inner_ref, s32[1]{0:T(128)} %bitcast.1.core_ref.half_ref, bf16[5,96,256]{2,1,0:T(8,128)(2,1)S(1)} %collective-permute-done.far_hbm, ...), custom_call_target="tpu_custom_call" | custom-call | tf_op jit(solution)/shard_map/main/pallas_call | solution.py:395
  23.5 2.4 %collective-permute-start.2 = (bf16[2304,128]{1,0:T(8,128)(2,1)S(1)}, bf16[2304,128]{1,0:T(8,128)(2,1)S(1)}, u32[]{:S(2)}, u32[]{:S(2)}) collective-permute-start(bf16[2304,128]{1,0:T(8,128)(2,1)S(1)} %get-tuple-element.15), channel_id=1, source_target_pairs={{0,1},{1,0},{2,3},{3,2},{4,5},{5,4},{6,7},{7,6},{8,9},{9,8},{10,11... | collective-permute-start | bytes 1769480 | tf_op jit(solution)/shard_map/ppermute | solution.py:532
  25.9 1.6 %collective-permute-done.2.got_hbm = bf16[2304,128]{1,0:T(8,128)(2,1)S(1)} collective-permute-done((bf16[2304,128]{1,0:T(8,128)(2,1)S(1)}, bf16[2304,128]{1,0:T(8,128)(2,1)S(1)}, u32[]{:S(2)}, u32[]{:S(2)}) %collective-permute-start.2) | collective-permute-done | bytes 589856 | tf_op jit(solution)/shard_map/ppermute | solution.py:532
  27.5 0.5 add.12
  28.1 18.5 %all_to_all.15 = bf16[32,72,128]{2,1,0:T(8,128)(2,1)} all-to-all(bf16[32,72,128]{2,1,0:T(8,128)(2,1)S(1)} %bitcast.30), channel_id=1, replica_groups=mesh['xh'=2,'zh'=8,'zl'=2,'xl'=2,'y'=4,'core'=2] {'xh','xl','y','zl'}, dimensions={0} | all-to-all | bytes 1179648 | tf_op jit(solution)/shard_map/all_to_all | solution.py:533
  46.5 1.2 %reduce_sum.12.after_hbm = bf16[72,128]{1,0:T(8,128)(2,1)S(1)} reduce(bf16[32,72,128]{2,1,0:T(8,128)(2,1)} %all_to_all.15, bf16[]{:T(256)} %constant.23.clone.1), dimensions={0}, to_apply=%region_0.1 | reduce | flops 285696 | bytes 608258 | tf_op jit(solution)/shard_map/reduce_sum | solution.py:506
  47.7 0.7 broadcast_in_dim.7
  48.4 13.9 %all-to-all-start.1 = ((bf16[8,72,128]{2,1,0:T(8,128)(2,1)}), bf16[8,72,128]{2,1,0:T(8,128)(2,1)S(1)}, u32[]{:S(2)}, u32[]{:S(2)}) async-start(bf16[8,72,128]{2,1,0:T(8,128)(2,1)} %broadcast_in_dim.7), calls=%async_computation.1 | async-start | bytes 294912 | tf_op jit(solution)/shard_map/all_to_all | solution.py:511
  62.7 1.1 %copy-done.3 = bf16[2592,128]{1,0:T(8,128)(2,1)S(1)} copy-done((bf16[2592,128]{1,0:T(8,128)(2,1)S(1)}, bf16[2592,128]{1,0:T(8,128)(2,1)}, u32[]{:S(2)}) %copy-start.3) | copy-done | bytes 663576
  63.7 3.6 %tail.1 = (bf16[192,128]{1,0:T(8,128)(2,1)}, bf16[2,96,512]{2,1,0:T(8,128)(2,1)S(1)}) custom-call(bf16[72,128]{1,0:T(8,128)(2,1)S(1)} %reduce_sum.12.after_hbm, bf16[4,96,1024]{2,1,0:T(8,128)(2,1)S(1)} %get-tuple-element.16.g_hbm, bf16[2592,128]{1,0:T(8,128)(2,1)S(1)} %copy-done.3, bf16[2592,192]{1,0:T(8,128)(2,1)S(1)} %bitcast.34, ...), custom_call_target="tpu_custom_call" | custom-call | flops 1000000000 | bytes 4000000 | tf_op jit(solution)/shard_map/tail/pallas_call | solution.py:429
  67.5 0.5 zero.1
  68.7 7.1 %all-to-all-done.1 = bf16[8,72,128]{2,1,0:T(8,128)(2,1)S(1)} async-done(((bf16[8,72,128]{2,1,0:T(8,128)(2,1)}), bf16[8,72,128]{2,1,0:T(8,128)(2,1)S(1)}, u32[]{:S(2)}, u32[]{:S(2)}) %all-to-all-start.1) | async-done | bytes 147488 | tf_op jit(solution)/shard_map/all_to_all | solution.py:511
  75.9 13.8 %all_to_all.16 = bf16[32,72,128]{2,1,0:T(8,128)(2,1)S(1)} all-to-all(bf16[32,72,128]{2,1,0:T(8,128)(2,1)S(1)} %broadcast_in_dim.8), channel_id=1, replica_groups=mesh['xh'=2,'zh'=8,'zl'=2,'xl'=2,'y'=4,'core'=2] {'xh','xl','y','zl'}, dimensions={0} | all-to-all | bytes 1179648 | tf_op jit(solution)/shard_map/all_to_all | solution.py:511
  89.7 6.5 %collective-permute-start.3 = (bf16[2304,128]{1,0:T(8,128)(2,1)S(1)}, bf16[2304,128]{1,0:T(8,128)(2,1)S(1)}, u32[]{:S(2)}, u32[]{:S(2)}) collective-permute-start(bf16[2304,128]{1,0:T(8,128)(2,1)S(1)} %bitcast.31), channel_id=1, source_target_pairs={{0,1},{1,0},{2,3},{3,2},{4,5},{5,4},{6,7},{7,6},{8,9},{9,8},{10,11... | collective-permute-start | bytes 1769480 | tf_op jit(solution)/shard_map/ppermute | solution.py:541
  96.2 2.0 %finish.2 = (f32[2592,192]{1,0:T(8,128)}, f32[96,768]{1,0:T(8,128)S(1)}) custom-call(s32[1]{0:T(128)} %bitcast.1.core_ref.half_ref, bf16[2304,128]{1,0:T(8,128)(2,1)S(1)} %bitcast.32), custom_call_target="tpu_custom_call" | custom-call | tf_op jit(solution)/shard_map/finish/pallas_call | solution.py:469
  98.2 2.0 %finish.3 = (f32[2592,192]{1,0:T(8,128)}, f32[96,768]{1,0:T(8,128)S(1)}) custom-call(s32[1]{0:T(128)S(6)} %sub.3.half_ref, bf16[2304,128]{1,0:T(8,128)(2,1)S(1)} %collective-permute-done.3.rows_hbm, f32[2592,192]{1,0:T(8,128)} %get-tuple-element.20.refs_0_, f32[96,768]{1,0:T(8,128)S(1)} %get-tuple-element.21.refs_1_), custom_call_target="tpu_custom_call", output_to_operand_aliasing={{0}: (2, {}), {1}: (3, {})} | custom-call | tf_op jit(solution)/shard_map/finish/pallas_call | solution.py:469
  100.1 1.5 %reshape.65 = f32[4,24,24,27]{3,2,1,0:T(8,128)} reshape(f32[96,648]{1,0:T(8,128)S(1)} %bitcast.35) | data formatting | bytes 497664 | tf_op jit(solution)/shard_map/reshape | solution.py:545
  (19 shorter events, 1.1 us)
Async XLA Ops:
  0.6 14.4 %copy-start = (bf16[27,96,192]{2,1,0:T(8,128)(2,1)S(1)}, bf16[27,96,192]{2,1,0:T(8,128)(2,1)}, u32[]{:S(2)}) copy-start(bf16[27,96,192]{2,1,0:T(8,128)(2,1)} %param.6) | copy-start | bytes 2985988
  2.6 11.3 %collective-permute-start = (bf16[5,96,256]{2,1,0:T(8,128)(2,1)S(1)}, bf16[5,96,256]{2,1,0:T(8,128)(2,1)S(1)}, u32[]{:S(2)}, u32[]{:S(2)}) collective-permute-start(bf16[5,96,256]{2,1,0:T(8,128)(2,1)S(1)} %pad_maximum_fusion.own_hbm), channel_id=1, source_target_pairs={{1,2},{3,4},{5,6},{7,8},{9,10},{11,12},{13,14},{2,1},{4,3},{6,5},{... | collective-permute-start | bytes 737288 | tf_op jit(solution)/shard_map/ppermute | solution.py:520
  9.1 6.0 %collective-permute-start.1 = (bf16[5,96,256]{2,1,0:T(8,128)(2,1)S(1)}, bf16[5,96,256]{2,1,0:T(8,128)(2,1)S(1)}, u32[]{:S(2)}, u32[]{:S(2)}) collective-permute-start(bf16[5,96,256]{2,1,0:T(8,128)(2,1)S(1)} %again.1), channel_id=1, source_target_pairs={{0,1},{1,0},{2,3},{3,2},{4,5},{5,4},{6,7},{7,6},{8,9},{9,8},{10,11... | collective-permute-start | bytes 737288 | tf_op jit(solution)/shard_map/ppermute | solution.py:528
  23.5 4.6 %copy-start.2 = (bf16[2592,128]{1,0:T(8,128)(2,1)}, bf16[2592,128]{1,0:T(8,128)(2,1)S(1)}, u32[]{:S(2)}) copy-start(bf16[2592,128]{1,0:T(8,128)(2,1)S(1)} %get-tuple-element.17.wn_hbm) | copy-start | bytes 1990660
  23.5 38.8 %copy-start.4 = (bf16[27,4,24,24]{0,3,2,1:T(8,128)(2,1)S(1)}, bf16[27,4,24,24]{0,3,2,1:T(8,128)(2,1)}, u32[]{:S(2)}) copy-start(bf16[27,4,24,24]{0,3,2,1:T(8,128)(2,1)} %param.5) | copy-start | bytes 373252
  23.5 4.0 %collective-permute-start.2 = (bf16[2304,128]{1,0:T(8,128)(2,1)S(1)}, bf16[2304,128]{1,0:T(8,128)(2,1)S(1)}, u32[]{:S(2)}, u32[]{:S(2)}) collective-permute-start(bf16[2304,128]{1,0:T(8,128)(2,1)S(1)} %get-tuple-element.15), channel_id=1, source_target_pairs={{0,1},{1,0},{2,3},{3,2},{4,5},{5,4},{6,7},{7,6},{8,9},{9,8},{10,11... | collective-permute-start | bytes 1769480 | tf_op jit(solution)/shard_map/ppermute | solution.py:532
  48.4 27.4 %all-to-all-start.1 = ((bf16[8,72,128]{2,1,0:T(8,128)(2,1)}), bf16[8,72,128]{2,1,0:T(8,128)(2,1)S(1)}, u32[]{:S(2)}, u32[]{:S(2)}) async-start(bf16[8,72,128]{2,1,0:T(8,128)(2,1)} %broadcast_in_dim.7), calls=%async_computation.1 | async-start | bytes 294912 | tf_op jit(solution)/shard_map/all_to_all | solution.py:511
  62.6 1.1 %copy-start.3 = (bf16[2592,128]{1,0:T(8,128)(2,1)S(1)}, bf16[2592,128]{1,0:T(8,128)(2,1)}, u32[]{:S(2)}) copy-start(bf16[2592,128]{1,0:T(8,128)(2,1)} %copy-done.2) | copy-start | bytes 1990660
  67.5 32.6 %copy-start.1 = (bf16[2,96,2,256]{3,2,0,1:T(2,128)(2,1)}, bf16[2,96,2,256]{3,2,0,1:T(2,128)(2,1)S(1)}, u32[]{:S(2)}) copy-start(bf16[2,96,2,256]{3,2,0,1:T(2,128)(2,1)S(1)} %copy.22) | copy-start | bytes 589828
  89.7 8.4 %collective-permute-start.3 = (bf16[2304,128]{1,0:T(8,128)(2,1)S(1)}, bf16[2304,128]{1,0:T(8,128)(2,1)S(1)}, u32[]{:S(2)}, u32[]{:S(2)}) collective-permute-start(bf16[2304,128]{1,0:T(8,128)(2,1)S(1)} %bitcast.31), channel_id=1, source_target_pairs={{0,1},{1,0},{2,3},{3,2},{4,5},{5,4},{6,7},{7,6},{8,9},{9,8},{10,11... | collective-permute-start | bytes 1769480 | tf_op jit(solution)/shard_map/ppermute | solution.py:541

commit v10 on v8

--- a/solution.py
+++ b/solution.py
@@ -460,7 +460,7 @@
             pltpu.VMEM((2, CH, 512), F32),
             pltpu.SemaphoreType.DMA((3,)),
         ],
-        compiler_params=pltpu.CompilerParams(vmem_limit_bytes=12 * MIB),
+        compiler_params=pltpu.CompilerParams(vmem_limit_bytes=52 * MIB),
         cost_estimate=pl.CostEstimate(flops=10**9, bytes_accessed=4 * 10**6, transcendentals=0),
         name="tail",
     )(after, grads, windows, w2, weight)
@@ -549,11 +549,12 @@
     mine, other, windows, grads = main_call(inner, core, far, own, twin, forward_weight, w2)
     chip = add_call(mine, lax.ppermute(other, "core", swap))
     parts = lax.all_to_all(chip.reshape(PIECES, PIECE, LANES), NEAR, 0, 0, tiled=True)
-    feat, vgrad = tail_call(chip, grads, windows, w2, backward_weight)
+    piece = sum_pieces(parts)
+    feat, vgrad = tail_call(piece, grads, windows, w2, backward_weight)
     features = feat.reshape(out_cotangent.shape)
     volume_grad = vgrad.reshape(2, CH, 2, 256).transpose(1, 0, 2, 3)
+    parts = to_all(piece, "zh", lax.axis_size("zh"))
     piece = lax.reduce(parts.astype(F32), zero_call(volume_grad)[0], lax.add, (0,)).astype(BF16)
-    piece = sum_pieces(to_all(piece, "zh", lax.axis_size("zh")))
     own_half = to_all(piece, NEAR, PIECES).reshape(ROWS, LANES)
     other_half = lax.ppermute(own_half, "core", swap)
     factor = 1.0 / math.sqrt(lax.axis_size(DP) * lax.axis_size(SPACE) * LANES)

time: 102 us -> 100 us (0.980)
  blocking collectives: 41 us -> 32.1 us
  starting transfers between devices: 24.5 us -> 32.1 us
  waiting for transfers between devices: 7.63 us -> 8.9 us
  other arithmetic: 1.21 us -> 0.15 us
    all_to_all x2 -> x1, blocking collectives: 41 us -> 13.8 us  [to_all(): return lax.all_to_all(copies, axes, 0, 0, tiled=True)]
    all_to_all x0 -> x1, blocking collectives: none -> 18.3 us  [shards(): lax.all_to_all(chip.reshape(PIECES, PIECE, LANES), NEAR, 0, 0, tiled=True)]
    all_to_all x1, starting transfers between devices: 6.26 us -> 13.9 us  [to_all(): return lax.all_to_all(copies, axes, 0, 0, tiled=True)]
    all_to_all x1, waiting for transfers between devices: 5.89 us -> 7.18 us  [to_all(): return lax.all_to_all(copies, axes, 0, 0, tiled=True)]
    another operation x1, other arithmetic: 1.16 us -> 0.03 us  [shards(): lax.reduce(parts.astype(F32), zero_call(volume_grad)[0], lax.add, (0,))]
where the time goes in v10:
time: 100 us; the launch traced here: 99.9 us
  starting transfers between devices  32.1 us (32%)
  blocking collectives  32.1 us (32%)
  Pallas kernels  17.8 us (18%)
  waiting for transfers between devices  8.9 us (9%)
  local copies, waits for them, and re-layouts  7.3 us (7%)
  between operations  1.55 us (2%)
    all_to_all x1, blocking collectives, shards(): lax.all_to_all(chip.reshape(PIECES, PIECE, LANES), NEAR, 0, 0, tiled=True)  18.3 us
    all_to_all x1, starting transfers between devices, to_all(): return lax.all_to_all(copies, axes, 0, 0, tiled=True)  13.9 us
    all_to_all x1, blocking collectives, to_all(): return lax.all_to_all(copies, axes, 0, 0, tiled=True)  13.8 us
    pallas_call x1, Pallas kernels, main_call(): pl.pallas_call(main_kernel, out_shape=(jax.ShapeDtypeStruct((ROWS, LANES)...  7.92 us
    all_to_all x1, waiting for transfers between devices, to_all(): return lax.all_to_all(copies, axes, 0, 0, tiled=True)  7.18 us
    ppermute x1, starting transfers between devices, shards(): other_half = lax.ppermute(own_half, 'core', swap)  6.47 us
    ppermute x1, starting transfers between devices, shards(): twin = lax.ppermute(again_call(own, forward_weight), 'core', swap)  4.87 us
    ppermute x1, starting transfers between devices, shards(): lax.ppermute(own, SPACE, [(i, i + 1) for i in range(1, count - 1, 2)] + [...  4.59 us
  transfers between devices with their start and end apart: 5, of which 2 were waited for; matrix products, arithmetic and copies ran while one was open for 2% of the time, Pallas kernels for 7%

profile of v10, /device:TPU:1, one launch (start us, length us, event | category | flops | bytes accessed | tf_op | source)
XLA Modules:
  0.0 99.9 jit_solution(10992362476893758535)
XLA Ops:
  0.6 0.9 copy.23
  1.6 1.0 copy.14
  2.6 4.6 %collective-permute-start = (bf16[5,96,256]{2,1,0:T(8,128)(2,1)S(1)}, bf16[5,96,256]{2,1,0:T(8,128)(2,1)S(1)}, u32[]{:S(2)}, u32[]{:S(2)}) collective-permute-start(bf16[5,96,256]{2,1,0:T(8,128)(2,1)S(1)} %pad_maximum_fusion.own_hbm), channel_id=1, source_target_pairs={{1,2},{3,4},{5,6},{7,8},{9,10},{11,12},{13,14},{2,1},{4,3},{6,5},{... | collective-permute-start | bytes 737288 | tf_op jit(solution)/shard_map/ppermute | solution.py:537
  7.2 1.1 %copy.16 = bf16[4,24,24,27]{3,2,1,0:T(8,128)(2,1)S(1)} copy(bf16[4,24,24,27]{3,1,2,0:T(8,128)(2,1)} %bitcast.39) | data formatting | bytes 248832 | tf_op jit(solution)/shard_map/transpose | solution.py:544
  8.4 0.3 reshape.58.after_hbm.fw_ref
  9.1 4.9 %collective-permute-start.1 = (bf16[5,96,256]{2,1,0:T(8,128)(2,1)S(1)}, bf16[5,96,256]{2,1,0:T(8,128)(2,1)S(1)}, u32[]{:S(2)}, u32[]{:S(2)}) collective-permute-start(bf16[5,96,256]{2,1,0:T(8,128)(2,1)S(1)} %again.1), channel_id=1, source_target_pairs={{0,1},{1,0},{2,3},{3,2},{4,5},{5,4},{6,7},{7,6},{8,9},{9,8},{10,11... | collective-permute-start | bytes 737288 | tf_op jit(solution)/shard_map/ppermute | solution.py:545
  13.9 1.2 %prepare.1.w1_hbm = bf16[288,864]{1,0:T(8,128)(2,1)S(1)} custom-call(bf16[96,648]{1,0:T(8,128)(2,1)S(1)} %reshape.58.after_hbm.fw_ref), custom_call_target="tpu_custom_call" | custom-call | tf_op jit(solution)/shard_map/prepare/pallas_call | solution.py:401
  15.1 7.9 %main.1 = (bf16[2304,128]{1,0:T(8,128)(2,1)S(1)}, bf16[2304,128]{1,0:T(8,128)(2,1)S(1)}, bf16[2592,128]{1,0:T(8,128)(2,1)S(1)}, bf16[4,96,1024]{2,1,0:T(8,128)(2,1)S(1)}) custom-call(f32[1]{0:T(128)} %bitcast.inner_ref, s32[1]{0:T(128)} %bitcast.1.core_ref.half_ref, bf16[5,96,256]{2,1,0:T(8,128)(2,1)S(1)} %collective-permute-done.far_hbm, ...), custom_call_target="tpu_custom_call" | custom-call | tf_op jit(solution)/shard_map/main/pallas_call | solution.py:413
  23.1 2.3 %collective-permute-start.2 = (bf16[2304,128]{1,0:T(8,128)(2,1)S(1)}, bf16[2304,128]{1,0:T(8,128)(2,1)S(1)}, u32[]{:S(2)}, u32[]{:S(2)}) collective-permute-start(bf16[2304,128]{1,0:T(8,128)(2,1)S(1)} %get-tuple-element.15), channel_id=1, source_target_pairs={{0,1},{1,0},{2,3},{3,2},{4,5},{5,4},{6,7},{7,6},{8,9},{9,8},{10,11... | collective-permute-start | bytes 1769480 | tf_op jit(solution)/shard_map/ppermute | solution.py:550
  25.4 1.7 %collective-permute-done.2.got_hbm = bf16[2304,128]{1,0:T(8,128)(2,1)S(1)} collective-permute-done((bf16[2304,128]{1,0:T(8,128)(2,1)S(1)}, bf16[2304,128]{1,0:T(8,128)(2,1)S(1)}, u32[]{:S(2)}, u32[]{:S(2)}) %collective-permute-start.2) | collective-permute-done | bytes 589856 | tf_op jit(solution)/shard_map/ppermute | solution.py:550
  27.1 0.5 add.12
  27.7 18.3 %all_to_all.15 = bf16[32,72,128]{2,1,0:T(8,128)(2,1)S(1)} all-to-all(bf16[32,72,128]{2,1,0:T(8,128)(2,1)S(1)} %bitcast.30), channel_id=1, replica_groups=mesh['xh'=2,'zh'=8,'zl'=2,'xl'=2,'y'=4,'core'=2] {'xh','xl','y','zl'}, dimensions={0} | all-to-all | bytes 1179648 | tf_op jit(solution)/shard_map/all_to_all | solution.py:551
  46.0 0.7 broadcast_in_dim.7
  46.7 13.9 %all-to-all-start.1 = ((bf16[8,72,128]{2,1,0:T(8,128)(2,1)}), bf16[8,72,128]{2,1,0:T(8,128)(2,1)S(1)}, u32[]{:S(2)}, u32[]{:S(2)}) async-start(bf16[8,72,128]{2,1,0:T(8,128)(2,1)} %broadcast_in_dim.7), calls=%async_computation.1 | async-start | bytes 294912 | tf_op jit(solution)/shard_map/all_to_all | solution.py:528
  60.6 0.3 reshape.61.fw_ref
  61.0 1.1 %copy-done.3 = bf16[2592,128]{1,0:T(8,128)(2,1)S(1)} copy-done((bf16[2592,128]{1,0:T(8,128)(2,1)S(1)}, bf16[2592,128]{1,0:T(8,128)(2,1)}, u32[]{:S(2)}) %copy-start.3) | copy-done | bytes 663576
  62.1 3.4 %tail.1 = (bf16[192,128]{1,0:T(8,128)(2,1)}, bf16[2,96,512]{2,1,0:T(8,128)(2,1)S(1)}) custom-call(bf16[72,128]{1,0:T(8,128)(2,1)S(1)} %reduce_sum.12.after_hbm, bf16[4,96,1024]{2,1,0:T(8,128)(2,1)S(1)} %get-tuple-element.16.g_hbm, bf16[2592,128]{1,0:T(8,128)(2,1)S(1)} %copy-done.3, bf16[2592,192]{1,0:T(8,128)(2,1)} %bitcast.33, ...), custom_call_target="tpu_custom_call" | custom-call | flops 1000000000 | bytes 4000000 | tf_op jit(solution)/shard_map/tail/pallas_call | solution.py:446
  65.7 0.5 zero.1
  66.9 7.2 %all-to-all-done.1 = bf16[8,72,128]{2,1,0:T(8,128)(2,1)S(1)} async-done(((bf16[8,72,128]{2,1,0:T(8,128)(2,1)}), bf16[8,72,128]{2,1,0:T(8,128)(2,1)S(1)}, u32[]{:S(2)}, u32[]{:S(2)}) %all-to-all-start.1) | async-done | bytes 147488 | tf_op jit(solution)/shard_map/all_to_all | solution.py:528
  74.2 13.8 %all_to_all.16 = bf16[32,72,128]{2,1,0:T(8,128)(2,1)S(1)} all-to-all(bf16[32,72,128]{2,1,0:T(8,128)(2,1)S(1)} %broadcast_in_dim.8), channel_id=1, replica_groups=mesh['xh'=2,'zh'=8,'zl'=2,'xl'=2,'y'=4,'core'=2] {'xh','xl','y','zl'}, dimensions={0} | all-to-all | bytes 1179648 | tf_op jit(solution)/shard_map/all_to_all | solution.py:528
  88.0 6.5 %collective-permute-start.3 = (bf16[2304,128]{1,0:T(8,128)(2,1)S(1)}, bf16[2304,128]{1,0:T(8,128)(2,1)S(1)}, u32[]{:S(2)}, u32[]{:S(2)}) collective-permute-start(bf16[2304,128]{1,0:T(8,128)(2,1)S(1)} %bitcast.31), channel_id=1, source_target_pairs={{0,1},{1,0},{2,3},{3,2},{4,5},{5,4},{6,7},{7,6},{8,9},{9,8},{10,11... | collective-permute-start | bytes 1769480 | tf_op jit(solution)/shard_map/ppermute | solution.py:559
  94.5 2.0 %finish.2 = (f32[2592,192]{1,0:T(8,128)}, f32[96,768]{1,0:T(8,128)S(1)}) custom-call(s32[1]{0:T(128)} %bitcast.1.core_ref.half_ref, bf16[2304,128]{1,0:T(8,128)(2,1)S(1)} %bitcast.32), custom_call_target="tpu_custom_call" | custom-call | tf_op jit(solution)/shard_map/finish/pallas_call | solution.py:486
  96.5 2.0 %finish.3 = (f32[2592,192]{1,0:T(8,128)}, f32[96,768]{1,0:T(8,128)S(1)}) custom-call(s32[1]{0:T(128)S(6)} %sub.3.half_ref, bf16[2304,128]{1,0:T(8,128)(2,1)S(1)} %collective-permute-done.3.rows_hbm, f32[2592,192]{1,0:T(8,128)} %get-tuple-element.20.refs_0_, f32[96,768]{1,0:T(8,128)S(1)} %get-tuple-element.21.refs_1_), custom_call_target="tpu_custom_call", output_to_operand_aliasing={{0}: (2, {}), {1}: (3, {})} | custom-call | tf_op jit(solution)/shard_map/finish/pallas_call | solution.py:486
  98.4 1.5 %reshape.65 = f32[4,24,24,27]{3,2,1,0:T(8,128)} reshape(f32[96,648]{1,0:T(8,128)S(1)} %bitcast.35) | data formatting | bytes 497664 | tf_op jit(solution)/shard_map/reshape | solution.py:563
  (20 shorter events, 0.8 us)
Async XLA Ops:
  0.6 14.5 %copy-start = (bf16[27,96,192]{2,1,0:T(8,128)(2,1)S(1)}, bf16[27,96,192]{2,1,0:T(8,128)(2,1)}, u32[]{:S(2)}) copy-start(bf16[27,96,192]{2,1,0:T(8,128)(2,1)} %param.6) | copy-start | bytes 2985988
  2.6 12.5 %collective-permute-start = (bf16[5,96,256]{2,1,0:T(8,128)(2,1)S(1)}, bf16[5,96,256]{2,1,0:T(8,128)(2,1)S(1)}, u32[]{:S(2)}, u32[]{:S(2)}) collective-permute-start(bf16[5,96,256]{2,1,0:T(8,128)(2,1)S(1)} %pad_maximum_fusion.own_hbm), channel_id=1, source_target_pairs={{1,2},{3,4},{5,6},{7,8},{9,10},{11,12},{13,14},{2,1},{4,3},{6,5},{... | collective-permute-start | bytes 737288 | tf_op jit(solution)/shard_map/ppermute | solution.py:537
  9.1 6.1 %collective-permute-start.1 = (bf16[5,96,256]{2,1,0:T(8,128)(2,1)S(1)}, bf16[5,96,256]{2,1,0:T(8,128)(2,1)S(1)}, u32[]{:S(2)}, u32[]{:S(2)}) collective-permute-start(bf16[5,96,256]{2,1,0:T(8,128)(2,1)S(1)} %again.1), channel_id=1, source_target_pairs={{0,1},{1,0},{2,3},{3,2},{4,5},{5,4},{6,7},{7,6},{8,9},{9,8},{10,11... | collective-permute-start | bytes 737288 | tf_op jit(solution)/shard_map/ppermute | solution.py:545
  23.1 4.6 %copy-start.2 = (bf16[2592,128]{1,0:T(8,128)(2,1)}, bf16[2592,128]{1,0:T(8,128)(2,1)S(1)}, u32[]{:S(2)}) copy-start(bf16[2592,128]{1,0:T(8,128)(2,1)S(1)} %get-tuple-element.17.wn_hbm) | copy-start | bytes 1990660
  23.1 37.5 %copy-start.4 = (bf16[27,4,24,24]{0,3,2,1:T(8,128)(2,1)S(1)}, bf16[27,4,24,24]{0,3,2,1:T(8,128)(2,1)}, u32[]{:S(2)}) copy-start(bf16[27,4,24,24]{0,3,2,1:T(8,128)(2,1)} %param.5) | copy-start | bytes 373252
  23.1 4.0 %collective-permute-start.2 = (bf16[2304,128]{1,0:T(8,128)(2,1)S(1)}, bf16[2304,128]{1,0:T(8,128)(2,1)S(1)}, u32[]{:S(2)}, u32[]{:S(2)}) collective-permute-start(bf16[2304,128]{1,0:T(8,128)(2,1)S(1)} %get-tuple-element.15), channel_id=1, source_target_pairs={{0,1},{1,0},{2,3},{3,2},{4,5},{5,4},{6,7},{7,6},{8,9},{9,8},{10,11... | collective-permute-start | bytes 1769480 | tf_op jit(solution)/shard_map/ppermute | solution.py:550
  46.7 27.4 %all-to-all-start.1 = ((bf16[8,72,128]{2,1,0:T(8,128)(2,1)}), bf16[8,72,128]{2,1,0:T(8,128)(2,1)S(1)}, u32[]{:S(2)}, u32[]{:S(2)}) async-start(bf16[8,72,128]{2,1,0:T(8,128)(2,1)} %broadcast_in_dim.7), calls=%async_computation.1 | async-start | bytes 294912 | tf_op jit(solution)/shard_map/all_to_all | solution.py:528
  61.0 1.1 %copy-start.3 = (bf16[2592,128]{1,0:T(8,128)(2,1)S(1)}, bf16[2592,128]{1,0:T(8,128)(2,1)}, u32[]{:S(2)}) copy-start(bf16[2592,128]{1,0:T(8,128)(2,1)} %copy-done.2) | copy-start | bytes 1990660
  65.7 32.7 %copy-start.1 = (bf16[2,96,2,256]{3,2,0,1:T(2,128)(2,1)}, bf16[2,96,2,256]{3,2,0,1:T(2,128)(2,1)S(1)}, u32[]{:S(2)}) copy-start(bf16[2,96,2,256]{3,2,0,1:T(2,128)(2,1)S(1)} %copy.22) | copy-start | bytes 589828
  88.0 8.4 %collective-permute-start.3 = (bf16[2304,128]{1,0:T(8,128)(2,1)S(1)}, bf16[2304,128]{1,0:T(8,128)(2,1)S(1)}, u32[]{:S(2)}, u32[]{:S(2)}) collective-permute-start(bf16[2304,128]{1,0:T(8,128)(2,1)S(1)} %bitcast.31), channel_id=1, source_target_pairs={{0,1},{1,0},{2,3},{3,2},{4,5},{5,4},{6,7},{7,6},{8,9},{9,8},{10,11... | collective-permute-start | bytes 1769480 | tf_op jit(solution)/shard_map/ppermute | solution.py:559

commit v11 on v10

--- a/solution.py
+++ b/solution.py
@@ -19,6 +19,8 @@
 PG = 24
 TAPS = 27
 WIN = 9 * CH
+PAIR = CH // 2
+WIN2 = 9 * PAIR
 LANES = 128
 HALF = TAPS * CH // 2
 PART = HALF // 3
@@ -56,7 +58,6 @@
     zero = jnp.zeros((CH, LANES), BF16)
     for b in range(3):
         for c in range(3):
-            rows = pl.ds((b * 3 + c) * CH, CH)
             for y in range(2):
                 source = y + b - 1
                 if source in (0, 1):
@@ -64,8 +65,12 @@
                     pair = ((odd_later, even), (even, odd), (odd, even_earlier))[c]
                 else:
                     pair = (zero, zero)
-                for parity in range(2):
-                    ref[rows, pl.ds((2 * y + parity) * LANES, LANES)] = pair[parity]
+                for h in range(2):
+                    rows = pl.ds(h * WIN2 + (b * 3 + c) * PAIR, PAIR)
+                    for parity in range(2):
+                        ref[rows, pl.ds((2 * y + parity) * LANES, LANES)] = pair[parity][
+                            h * PAIR : (h + 1) * PAIR
+                        ]
 
 
 def ones_where(condition):
@@ -88,17 +93,17 @@
     return (value * (2**bits // divisor + 1)) >> bits
 
 
-def fold_matrix(rows):
-    row = lax.broadcasted_iota(jnp.int32, (rows, WIN), 0)
-    column = lax.broadcasted_iota(jnp.int32, (1, WIN), 1)
-    target = quotient(column, CH, 16) * PG + column - PG * quotient(column, PG, 16)
+def fold_matrix():
+    row = lax.broadcasted_iota(jnp.int32, (256, WIN2), 0)
+    column = lax.broadcasted_iota(jnp.int32, (1, WIN2), 1)
+    target = quotient(column, PAIR, 16) * PG + column - PG * quotient(column, PG, 16)
     return ones_where(row == target)
 
 
 def group_mask():
-    row = lax.broadcasted_iota(jnp.int32, (CH, WIN), 0)
-    column = lax.broadcasted_iota(jnp.int32, (1, WIN), 1)
-    offset = row - PG * quotient(column - CH * quotient(column, CH, 16), PG, 16)
+    row = lax.broadcasted_iota(jnp.int32, (PAIR, WIN2), 0)
+    column = lax.broadcasted_iota(jnp.int32, (1, WIN2), 1)
+    offset = row - PG * quotient(column - PAIR * quotient(column, PAIR, 16), PG, 16)
     return (offset >= 0) & (offset < PG)
 
 
@@ -110,10 +115,6 @@
     plane = quotient(tap, 9, 16)
     target = plane * 256 + (8 - tap + 9 * plane) * PG + channel
     return ones_where((row == target) & (column < PG * TAPS))
-
-
-def expand(narrow, fold, mask):
-    return jnp.where(mask, dot(narrow, fold), 0.0).astype(BF16)
 
 
 def fill_weights(w1, fw, flip):
@@ -127,9 +128,11 @@
     order = ones_where(row == plane * 256 + (tap - 9 * plane) * PG + channel)
     narrow = dot_nt(fw, order).astype(BF16)
     mask = group_mask()
-    fold = fold_matrix(256)
-    for a in range(3):
-        w1[pl.ds(a * CH, CH), :] = expand(narrow[:, a * 256 : (a + 1) * 256], fold, mask)
+    fold = fold_matrix()
+    for h in range(2):
+        for a in range(3):
+            block = dot(narrow[h * PAIR : (h + 1) * PAIR, a * 256 : (a + 1) * 256], fold)
+            w1[h, pl.ds(a * PAIR, PAIR), :] = jnp.where(mask, block, 0.0).astype(BF16)
 
 
 def again_kernel(own_hbm, after_hbm, again_hbm, sem):
@@ -185,14 +188,19 @@
     fetches[3].wait()
     for e in range(6):
         first, last = max(0, e - 3), min(2, e)
-        terms = dot(w1[pl.ds(first * CH, (last - first + 1) * CH), :], xs[e])
-        for a in range(first, last + 1):
-            term = terms[(a - first) * CH : (a - first + 1) * CH]
-            j = e - a
-            if a == 0:
-                pre_ref[j] = term
-            else:
-                pre_ref[j] += term
+        for h in range(2):
+            here = pl.ds(h * PAIR, PAIR)
+            terms = dot(
+                w1[h, pl.ds(first * PAIR, (last - first + 1) * PAIR), :],
+                xs[e, pl.ds(h * WIN2, WIN2), :],
+            )
+            for a in range(first, last + 1):
+                term = terms[(a - first) * PAIR : (a - first + 1) * PAIR]
+                j = e - a
+                if a == 0:
+                    pre_ref[j, here, :] = term
+                else:
+                    pre_ref[j, here, :] += term
     zero = jnp.zeros((CH, LANES), BF16)
     for a in range(3):
         for c in range(3):
@@ -262,16 +270,28 @@
             fill_windows(gs.at[j - 1], tiles)
     send_g = pltpu.make_async_copy(g_ref, g_hbm, sems.at[1])
     send_g.start()
-    taps = None
-    for j in (1, 2):
-        planes = jnp.concatenate([xc_ref[j - 1], xc_ref[j], xc_ref[j + 1]], axis=0)
-        term = dot_nt(planes, gs[j - 1])
-        taps = term if taps is None else taps + term
-    fold = fold_matrix(256)
-    kept = [jnp.where(mask, taps[a * CH : (a + 1) * CH], 0.0).astype(BF16) for a in range(3)]
-    narrow = dot_nt(jnp.concatenate(kept, axis=0), fold).astype(BF16)
+    fold = fold_matrix()
+    narrow = []
+    for h in range(2):
+        here = pl.ds(h * PAIR, PAIR)
+        taps = None
+        for j in (1, 2):
+            planes = jnp.concatenate([xc_ref[j + a, here, :] for a in (-1, 0, 1)], axis=0)
+            term = dot_nt(planes, gs[j - 1, pl.ds(h * WIN2, WIN2), :])
+            taps = term if taps is None else taps + term
+        kept = [
+            jnp.where(mask, taps[a * PAIR : (a + 1) * PAIR], 0.0).astype(BF16) for a in range(3)
+        ]
+        narrow.append(dot_nt(jnp.concatenate(kept, axis=0), fold).astype(BF16))
     ordered = dot(
-        jnp.concatenate([narrow[a * CH : (a + 1) * CH] for a in range(3)], axis=1), order_ref[...]
+        jnp.concatenate(
+            [
+                jnp.concatenate([part[a * PAIR : (a + 1) * PAIR] for part in narrow], axis=0)
+                for a in range(3)
+            ],
+            axis=1,
+        ),
+        order_ref[...],
     )
     fg[...] = ordered.astype(BF16)
     for out_ref, half in ((other_ref, 1 - core), (mine_ref, core)):
@@ -311,14 +331,19 @@
         fill_windows(gs.at[j], tiles)
     for j in range(4):
         first, last = max(0, j - 1), min(2, j)
-        terms = dot(w1[pl.ds(first * CH, (last - first + 1) * CH), :], gs[j])
-        for a in range(first, last + 1):
-            term = terms[(a - first) * CH : (a - first + 1) * CH]
-            out = j - a
-            if a == 0:
-                acc[out] = term
-            else:
-                acc[out] += term
+        for h in range(2):
+            here = pl.ds(h * PAIR, PAIR)
+            terms = dot(
+                w1[h, pl.ds(first * PAIR, (last - first + 1) * PAIR), :],
+                gs[j, pl.ds(h * WIN2, WIN2), :],
+            )
+            for a in range(first, last + 1):
+                term = terms[(a - first) * PAIR : (a - first + 1) * PAIR]
+                out = j - a
+                if a == 0:
+                    acc[out, here, :] = term
+                else:
+                    acc[out, here, :] += term
     merge = merge_matrix()
     for out in range(2):
         for y in range(2):
@@ -345,19 +370,13 @@
 
 
 def finish_kernel(factor, half_ref, rows_hbm, *refs):
-    strided_hbm, grouped_hbm, rows_ref, strided_ref, grouped_ref, fetch_sems, send_sems = refs[-7:]
+    strided_hbm, grouped_hbm, rows_ref, strided_ref, grouped_ref, fetch_sem, send_sems = refs[-7:]
     half = half_ref[0]
-    fetches = [
-        pltpu.make_async_copy(
-            rows_hbm.at[pl.ds(k * CHUNK, CHUNK)], rows_ref.at[pl.ds(k * CHUNK, CHUNK)], fetch_sems.at[k]
-        )
-        for k in range(3)
-    ]
-    for fetch in fetches:
-        fetch.start()
+    fetch = pltpu.make_async_copy(rows_hbm, rows_ref, fetch_sem)
+    fetch.start()
+    fetch.wait()
     sends = []
     for k in range(3):
-        fetches[k].wait()
         at = k * CHUNK
         here = pl.ds(k * PART, PART)
         strided_ref[here, pl.ds(0, LANES)] = rows_ref[pl.ds(at, PART), :].astype(F32) * factor
@@ -400,10 +419,10 @@
 def prepare_call(weight):
     return pl.pallas_call(
         prepare_kernel,
-        out_shape=jax.ShapeDtypeStruct((3 * CH, WIN), BF16),
+        out_shape=jax.ShapeDtypeStruct((2, 3 * PAIR, WIN2), BF16),
         in_specs=[VMEM],
         out_specs=ANY,
-        scratch_shapes=[pltpu.VMEM((3 * CH, WIN), BF16), pltpu.SemaphoreType.DMA],
+        scratch_shapes=[pltpu.VMEM((2, 3 * PAIR, WIN2), BF16), pltpu.SemaphoreType.DMA],
         compiler_params=pltpu.CompilerParams(vmem_limit_bytes=6 * MIB),
         name="prepare",
     )(weight)
@@ -429,7 +448,7 @@
             pltpu.VMEM((TAPS * CH, LANES), BF16),
             pltpu.VMEM((4, CH, 8 * LANES), BF16),
             pltpu.VMEM((6, WIN, 512), BF16),
-            pltpu.VMEM((3 * CH, WIN), BF16),
+            pltpu.VMEM((2, 3 * PAIR, WIN2), BF16),
             pltpu.VMEM((4, CH, 512), F32),
             pltpu.VMEM((4, CH, 512), BF16),
             pltpu.VMEM((2, WIN, 512), BF16),
@@ -456,7 +475,7 @@
             pltpu.VMEM((TAPS * CH, LANES), BF16),
             pltpu.VMEM((TAPS * CH, 192), BF16),
             pltpu.VMEM((4, WIN, 512), BF16),
-            pltpu.VMEM((3 * CH, WIN), BF16),
+            pltpu.VMEM((2, 3 * PAIR, WIN2), BF16),
             pltpu.VMEM((2, CH, 512), F32),
             pltpu.SemaphoreType.DMA((3,)),
         ],
@@ -495,7 +514,7 @@
             pltpu.VMEM((ROWS, LANES), BF16),
             pltpu.VMEM((HALF, 192), F32),
             pltpu.VMEM((F_PART, 6 * LANES), F32),
-            pltpu.SemaphoreType.DMA((3,)),
+            pltpu.SemaphoreType.DMA,
             pltpu.SemaphoreType.DMA((4,)),
         ],
         input_output_aliases={2 + i: i for i in range(len(before))},

time: 100 us -> 98.8 us (0.988)
  Pallas kernels: 17.8 us -> 15.6 us
    pallas_call x2, Pallas kernels: 3.92 us -> 2.65 us  [finish_call(): pl.pallas_call(functools.partial(finish_kernel, factor), out_shape=(jax.S...]
  transfers between devices with their start and end apart: 5 -> 5, of which waited for: 2 -> 4; matrix products, arithmetic and copies ran while one was open for 2% -> 2% of each run, Pallas kernels for 7% -> 7%
where the time goes in v11:
time: 98.8 us; the launch traced here: 98.3 us
  starting transfers between devices  32.3 us (33%)
  blocking collectives  32.2 us (33%)
  Pallas kernels  15.6 us (16%)
  waiting for transfers between devices  9.27 us (9%)
  local copies, waits for them, and re-layouts  7.3 us (7%)
  between operations  1.53 us (2%)
    all_to_all x1, blocking collectives, shards(): lax.all_to_all(chip.reshape(PIECES, PIECE, LANES), NEAR, 0, 0, tiled=True)  18.4 us
    all_to_all x1, starting transfers between devices, to_all(): return lax.all_to_all(copies, axes, 0, 0, tiled=True)  13.9 us
    all_to_all x1, blocking collectives, to_all(): return lax.all_to_all(copies, axes, 0, 0, tiled=True)  13.8 us
    pallas_call x1, Pallas kernels, main_call(): pl.pallas_call(main_kernel, out_shape=(jax.ShapeDtypeStruct((ROWS, LANES)...  7.29 us
    all_to_all x1, waiting for transfers between devices, to_all(): return lax.all_to_all(copies, axes, 0, 0, tiled=True)  7.23 us
    ppermute x1, starting transfers between devices, shards(): other_half = lax.ppermute(own_half, 'core', swap)  6.47 us
    ppermute x1, starting transfers between devices, shards(): twin = lax.ppermute(again_call(own, forward_weight), 'core', swap)  4.87 us
    ppermute x1, starting transfers between devices, shards(): lax.ppermute(own, SPACE, [(i, i + 1) for i in range(1, count - 1, 2)] + [...  4.59 us
  transfers between devices with their start and end apart: 5, of which 4 were waited for; matrix products, arithmetic and copies ran while one was open for 2% of the time, Pallas kernels for 7%

profile of v11, /device:TPU:1, one launch (start us, length us, event | category | flops | bytes accessed | tf_op | source)
XLA Modules:
  0.0 98.3 jit_solution(11051374932182329902)
XLA Ops:
  0.6 0.9 copy.23
  1.6 1.0 copy.14
  2.6 4.6 %collective-permute-start = (bf16[5,96,256]{2,1,0:T(8,128)(2,1)S(1)}, bf16[5,96,256]{2,1,0:T(8,128)(2,1)S(1)}, u32[]{:S(2)}, u32[]{:S(2)}) collective-permute-start(bf16[5,96,256]{2,1,0:T(8,128)(2,1)S(1)} %pad_maximum_fusion.own_hbm), channel_id=1, source_target_pairs={{1,2},{3,4},{5,6},{7,8},{9,10},{11,12},{13,14},{2,1},{4,3},{6,5},{... | collective-permute-start | bytes 737288 | tf_op jit(solution)/shard_map/ppermute | solution.py:556
  7.2 1.1 %copy.16 = bf16[4,24,24,27]{3,2,1,0:T(8,128)(2,1)S(1)} copy(bf16[4,24,24,27]{3,1,2,0:T(8,128)(2,1)} %bitcast.39) | data formatting | bytes 248832 | tf_op jit(solution)/shard_map/transpose | solution.py:563
  8.4 0.3 reshape.58.after_hbm.fw_ref
  9.1 4.9 %collective-permute-start.1 = (bf16[5,96,256]{2,1,0:T(8,128)(2,1)S(1)}, bf16[5,96,256]{2,1,0:T(8,128)(2,1)S(1)}, u32[]{:S(2)}, u32[]{:S(2)}) collective-permute-start(bf16[5,96,256]{2,1,0:T(8,128)(2,1)S(1)} %again.1), channel_id=1, source_target_pairs={{0,1},{1,0},{2,3},{3,2},{4,5},{5,4},{6,7},{7,6},{8,9},{9,8},{10,11... | collective-permute-start | bytes 737288 | tf_op jit(solution)/shard_map/ppermute | solution.py:564
  13.9 0.9 prepare.1.w1_hbm
  15.0 7.3 %main.1 = (bf16[2304,128]{1,0:T(8,128)(2,1)S(1)}, bf16[2304,128]{1,0:T(8,128)(2,1)S(1)}, bf16[2592,128]{1,0:T(8,128)(2,1)S(1)}, bf16[4,96,1024]{2,1,0:T(8,128)(2,1)S(1)}) custom-call(f32[1]{0:T(128)} %bitcast.inner_ref, s32[1]{0:T(128)} %bitcast.1.core_ref.half_ref, bf16[5,96,256]{2,1,0:T(8,128)(2,1)S(1)} %collective-permute-done.far_hbm, ...), custom_call_target="tpu_custom_call" | custom-call | tf_op jit(solution)/shard_map/main/pallas_call | solution.py:432
  22.4 2.4 %collective-permute-start.2 = (bf16[2304,128]{1,0:T(8,128)(2,1)S(1)}, bf16[2304,128]{1,0:T(8,128)(2,1)S(1)}, u32[]{:S(2)}, u32[]{:S(2)}) collective-permute-start(bf16[2304,128]{1,0:T(8,128)(2,1)S(1)} %get-tuple-element.15), channel_id=1, source_target_pairs={{0,1},{1,0},{2,3},{3,2},{4,5},{5,4},{6,7},{7,6},{8,9},{9,8},{10,11... | collective-permute-start | bytes 1769480 | tf_op jit(solution)/shard_map/ppermute | solution.py:569
  24.8 1.6 %collective-permute-done.2.got_hbm = bf16[2304,128]{1,0:T(8,128)(2,1)S(1)} collective-permute-done((bf16[2304,128]{1,0:T(8,128)(2,1)S(1)}, bf16[2304,128]{1,0:T(8,128)(2,1)S(1)}, u32[]{:S(2)}, u32[]{:S(2)}) %collective-permute-start.2) | collective-permute-done | bytes 589856 | tf_op jit(solution)/shard_map/ppermute | solution.py:569
  26.4 0.5 add.12
  26.9 18.4 %all_to_all.15 = bf16[32,72,128]{2,1,0:T(8,128)(2,1)S(1)} all-to-all(bf16[32,72,128]{2,1,0:T(8,128)(2,1)S(1)} %bitcast.30), channel_id=1, replica_groups=mesh['xh'=2,'zh'=8,'zl'=2,'xl'=2,'y'=4,'core'=2] {'xh','xl','y','zl'}, dimensions={0} | all-to-all | bytes 1179648 | tf_op jit(solution)/shard_map/all_to_all | solution.py:570
  45.4 0.7 broadcast_in_dim.7
  46.1 13.9 %all-to-all-start.1 = ((bf16[8,72,128]{2,1,0:T(8,128)(2,1)}), bf16[8,72,128]{2,1,0:T(8,128)(2,1)S(1)}, u32[]{:S(2)}, u32[]{:S(2)}) async-start(bf16[8,72,128]{2,1,0:T(8,128)(2,1)} %broadcast_in_dim.7), calls=%async_computation.1 | async-start | bytes 294912 | tf_op jit(solution)/shard_map/all_to_all | solution.py:547
  60.0 0.3 reshape.61.fw_ref
  60.4 1.1 %copy-done.3 = bf16[2592,128]{1,0:T(8,128)(2,1)S(1)} copy-done((bf16[2592,128]{1,0:T(8,128)(2,1)S(1)}, bf16[2592,128]{1,0:T(8,128)(2,1)}, u32[]{:S(2)}) %copy-start.3) | copy-done | bytes 663576
  61.4 3.4 %tail.1 = (bf16[192,128]{1,0:T(8,128)(2,1)}, bf16[2,96,512]{2,1,0:T(8,128)(2,1)S(1)}) custom-call(bf16[72,128]{1,0:T(8,128)(2,1)S(1)} %reduce_sum.12.after_hbm, bf16[4,96,1024]{2,1,0:T(8,128)(2,1)S(1)} %get-tuple-element.16.g_hbm, bf16[2592,128]{1,0:T(8,128)(2,1)S(1)} %copy-done.3, bf16[2592,192]{1,0:T(8,128)(2,1)} %bitcast.33, ...), custom_call_target="tpu_custom_call" | custom-call | flops 1000000000 | bytes 4000000 | tf_op jit(solution)/shard_map/tail/pallas_call | solution.py:465
  65.1 0.5 zero.1
  66.2 7.2 %all-to-all-done.1 = bf16[8,72,128]{2,1,0:T(8,128)(2,1)S(1)} async-done(((bf16[8,72,128]{2,1,0:T(8,128)(2,1)}), bf16[8,72,128]{2,1,0:T(8,128)(2,1)S(1)}, u32[]{:S(2)}, u32[]{:S(2)}) %all-to-all-start.1) | async-done | bytes 147488 | tf_op jit(solution)/shard_map/all_to_all | solution.py:547
  73.6 13.8 %all_to_all.16 = bf16[32,72,128]{2,1,0:T(8,128)(2,1)S(1)} all-to-all(bf16[32,72,128]{2,1,0:T(8,128)(2,1)S(1)} %broadcast_in_dim.8), channel_id=1, replica_groups=mesh['xh'=2,'zh'=8,'zl'=2,'xl'=2,'y'=4,'core'=2] {'xh','xl','y','zl'}, dimensions={0} | all-to-all | bytes 1179648 | tf_op jit(solution)/shard_map/all_to_all | solution.py:547
  87.4 6.5 %collective-permute-start.3 = (bf16[2304,128]{1,0:T(8,128)(2,1)S(1)}, bf16[2304,128]{1,0:T(8,128)(2,1)S(1)}, u32[]{:S(2)}, u32[]{:S(2)}) collective-permute-start(bf16[2304,128]{1,0:T(8,128)(2,1)S(1)} %bitcast.31), channel_id=1, source_target_pairs={{0,1},{1,0},{2,3},{3,2},{4,5},{5,4},{6,7},{7,6},{8,9},{9,8},{10,11... | collective-permute-start | bytes 1769480 | tf_op jit(solution)/shard_map/ppermute | solution.py:578
  93.9 1.3 %finish.2 = (f32[2592,192]{1,0:T(8,128)}, f32[96,768]{1,0:T(8,128)S(1)}) custom-call(s32[1]{0:T(128)} %bitcast.1.core_ref.half_ref, bf16[2304,128]{1,0:T(8,128)(2,1)S(1)} %bitcast.32), custom_call_target="tpu_custom_call" | custom-call | tf_op jit(solution)/shard_map/finish/pallas_call | solution.py:505
  95.5 1.3 %finish.3 = (f32[2592,192]{1,0:T(8,128)}, f32[96,768]{1,0:T(8,128)S(1)}) custom-call(s32[1]{0:T(128)S(6)} %sub.3.half_ref, bf16[2304,128]{1,0:T(8,128)(2,1)S(1)} %collective-permute-done.3.rows_hbm, f32[2592,192]{1,0:T(8,128)} %get-tuple-element.20.refs_0_, f32[96,768]{1,0:T(8,128)S(1)} %get-tuple-element.21.refs_1_), custom_call_target="tpu_custom_call", output_to_operand_aliasing={{0}: (2, {}), {1}: (3, {})} | custom-call | tf_op jit(solution)/shard_map/finish/pallas_call | solution.py:505
  96.8 1.5 %reshape.65 = f32[4,24,24,27]{3,2,1,0:T(8,128)} reshape(f32[96,648]{1,0:T(8,128)S(1)} %bitcast.35) | data formatting | bytes 497664 | tf_op jit(solution)/shard_map/reshape | solution.py:582
  (20 shorter events, 1.2 us)
Async XLA Ops:
  0.6 14.4 %copy-start = (bf16[27,96,192]{2,1,0:T(8,128)(2,1)S(1)}, bf16[27,96,192]{2,1,0:T(8,128)(2,1)}, u32[]{:S(2)}) copy-start(bf16[27,96,192]{2,1,0:T(8,128)(2,1)} %param.6) | copy-start | bytes 2985988
  2.6 12.3 %collective-permute-start = (bf16[5,96,256]{2,1,0:T(8,128)(2,1)S(1)}, bf16[5,96,256]{2,1,0:T(8,128)(2,1)S(1)}, u32[]{:S(2)}, u32[]{:S(2)}) collective-permute-start(bf16[5,96,256]{2,1,0:T(8,128)(2,1)S(1)} %pad_maximum_fusion.own_hbm), channel_id=1, source_target_pairs={{1,2},{3,4},{5,6},{7,8},{9,10},{11,12},{13,14},{2,1},{4,3},{6,5},{... | collective-permute-start | bytes 737288 | tf_op jit(solution)/shard_map/ppermute | solution.py:556
  9.1 6.0 %collective-permute-start.1 = (bf16[5,96,256]{2,1,0:T(8,128)(2,1)S(1)}, bf16[5,96,256]{2,1,0:T(8,128)(2,1)S(1)}, u32[]{:S(2)}, u32[]{:S(2)}) collective-permute-start(bf16[5,96,256]{2,1,0:T(8,128)(2,1)S(1)} %again.1), channel_id=1, source_target_pairs={{0,1},{1,0},{2,3},{3,2},{4,5},{5,4},{6,7},{7,6},{8,9},{9,8},{10,11... | collective-permute-start | bytes 737288 | tf_op jit(solution)/shard_map/ppermute | solution.py:564
  22.3 4.6 %copy-start.2 = (bf16[2592,128]{1,0:T(8,128)(2,1)}, bf16[2592,128]{1,0:T(8,128)(2,1)S(1)}, u32[]{:S(2)}) copy-start(bf16[2592,128]{1,0:T(8,128)(2,1)S(1)} %get-tuple-element.17.wn_hbm) | copy-start | bytes 1990660
  22.4 37.6 %copy-start.4 = (bf16[27,4,24,24]{0,3,2,1:T(8,128)(2,1)S(1)}, bf16[27,4,24,24]{0,3,2,1:T(8,128)(2,1)}, u32[]{:S(2)}) copy-start(bf16[27,4,24,24]{0,3,2,1:T(8,128)(2,1)} %param.5) | copy-start | bytes 373252
  22.4 4.0 %collective-permute-start.2 = (bf16[2304,128]{1,0:T(8,128)(2,1)S(1)}, bf16[2304,128]{1,0:T(8,128)(2,1)S(1)}, u32[]{:S(2)}, u32[]{:S(2)}) collective-permute-start(bf16[2304,128]{1,0:T(8,128)(2,1)S(1)} %get-tuple-element.15), channel_id=1, source_target_pairs={{0,1},{1,0},{2,3},{3,2},{4,5},{5,4},{6,7},{7,6},{8,9},{9,8},{10,11... | collective-permute-start | bytes 1769480 | tf_op jit(solution)/shard_map/ppermute | solution.py:569
  46.1 27.4 %all-to-all-start.1 = ((bf16[8,72,128]{2,1,0:T(8,128)(2,1)}), bf16[8,72,128]{2,1,0:T(8,128)(2,1)S(1)}, u32[]{:S(2)}, u32[]{:S(2)}) async-start(bf16[8,72,128]{2,1,0:T(8,128)(2,1)} %broadcast_in_dim.7), calls=%async_computation.1 | async-start | bytes 294912 | tf_op jit(solution)/shard_map/all_to_all | solution.py:547
  60.3 1.1 %copy-start.3 = (bf16[2592,128]{1,0:T(8,128)(2,1)S(1)}, bf16[2592,128]{1,0:T(8,128)(2,1)}, u32[]{:S(2)}) copy-start(bf16[2592,128]{1,0:T(8,128)(2,1)} %copy-done.2) | copy-start | bytes 1990660
  65.0 31.8 %copy-start.1 = (bf16[2,96,2,256]{3,2,0,1:T(2,128)(2,1)}, bf16[2,96,2,256]{3,2,0,1:T(2,128)(2,1)S(1)}, u32[]{:S(2)}) copy-start(bf16[2,96,2,256]{3,2,0,1:T(2,128)(2,1)S(1)} %copy.22) | copy-start | bytes 589828
  87.4 8.1 %collective-permute-start.3 = (bf16[2304,128]{1,0:T(8,128)(2,1)S(1)}, bf16[2304,128]{1,0:T(8,128)(2,1)S(1)}, u32[]{:S(2)}, u32[]{:S(2)}) collective-permute-start(bf16[2304,128]{1,0:T(8,128)(2,1)S(1)} %bitcast.31), channel_id=1, source_target_pairs={{0,1},{1,0},{2,3},{3,2},{4,5},{5,4},{6,7},{7,6},{8,9},{9,8},{10,11... | collective-permute-start | bytes 1769480 | tf_op jit(solution)/shard_map/ppermute | solution.py:578

commit v12 on v11

--- a/solution.py
+++ b/solution.py
@@ -11,7 +11,7 @@
 
 SPACE = ("xl", "y", "core")
 DP = ("xh", "zh", "zl")
-NEAR = ("xh", "xl", "y", "zl")
+NEAR = ("zl", "y", "xh", "xl")
 F32 = jnp.float32
 BF16 = jnp.bfloat16
 

time: 98.8 us -> 98 us (level)
  blocking collectives: 32.2 us -> 30.8 us
    all_to_all x1, blocking collectives: 18.4 us -> 17.2 us  [shards(): lax.all_to_all(chip.reshape(PIECES, PIECE, LANES), NEAR, 0, 0, tiled=True)]
where the time goes in v12:
time: 98 us; the launch traced here: 97.5 us
  starting transfers between devices  32.5 us (33%)
  blocking collectives  30.8 us (31%)
  Pallas kernels  15.6 us (16%)
  waiting for transfers between devices  9.6 us (10%)
  local copies, waits for them, and re-layouts  7.3 us (7%)
  between operations  1.53 us (2%)
    all_to_all x1, blocking collectives, shards(): lax.all_to_all(chip.reshape(PIECES, PIECE, LANES), NEAR, 0, 0, tiled=True)  17.2 us
    all_to_all x1, starting transfers between devices, to_all(): return lax.all_to_all(copies, axes, 0, 0, tiled=True)  13.9 us
    all_to_all x1, blocking collectives, to_all(): return lax.all_to_all(copies, axes, 0, 0, tiled=True)  13.7 us
    all_to_all x1, waiting for transfers between devices, to_all(): return lax.all_to_all(copies, axes, 0, 0, tiled=True)  7.56 us
    pallas_call x1, Pallas kernels, main_call(): pl.pallas_call(main_kernel, out_shape=(jax.ShapeDtypeStruct((ROWS, LANES)...  7.29 us
    ppermute x1, starting transfers between devices, shards(): other_half = lax.ppermute(own_half, 'core', swap)  6.71 us
    ppermute x1, starting transfers between devices, shards(): twin = lax.ppermute(again_call(own, forward_weight), 'core', swap)  4.87 us
    ppermute x1, starting transfers between devices, shards(): lax.ppermute(own, SPACE, [(i, i + 1) for i in range(1, count - 1, 2)] + [...  4.59 us
  transfers between devices with their start and end apart: 5, of which 4 were waited for; matrix products, arithmetic and copies ran while one was open for 2% of the time, Pallas kernels for 7%

profile of v12, /device:TPU:1, one launch (start us, length us, event | category | flops | bytes accessed | tf_op | source)
XLA Modules:
  0.0 97.5 jit_solution(2802921091813512466)
XLA Ops:
  0.6 0.9 copy.23
  1.6 1.0 copy.14
  2.6 4.6 %collective-permute-start = (bf16[5,96,256]{2,1,0:T(8,128)(2,1)S(1)}, bf16[5,96,256]{2,1,0:T(8,128)(2,1)S(1)}, u32[]{:S(2)}, u32[]{:S(2)}) collective-permute-start(bf16[5,96,256]{2,1,0:T(8,128)(2,1)S(1)} %pad_maximum_fusion.own_hbm), channel_id=1, source_target_pairs={{1,2},{3,4},{5,6},{7,8},{9,10},{11,12},{13,14},{2,1},{4,3},{6,5},{... | collective-permute-start | bytes 737288 | tf_op jit(solution)/shard_map/ppermute | solution.py:556
  7.2 1.1 %copy.16 = bf16[4,24,24,27]{3,2,1,0:T(8,128)(2,1)S(1)} copy(bf16[4,24,24,27]{3,1,2,0:T(8,128)(2,1)} %bitcast.39) | data formatting | bytes 248832 | tf_op jit(solution)/shard_map/transpose | solution.py:563
  8.4 0.3 reshape.58.after_hbm.fw_ref
  9.1 4.9 %collective-permute-start.1 = (bf16[5,96,256]{2,1,0:T(8,128)(2,1)S(1)}, bf16[5,96,256]{2,1,0:T(8,128)(2,1)S(1)}, u32[]{:S(2)}, u32[]{:S(2)}) collective-permute-start(bf16[5,96,256]{2,1,0:T(8,128)(2,1)S(1)} %again.1), channel_id=1, source_target_pairs={{0,1},{1,0},{2,3},{3,2},{4,5},{5,4},{6,7},{7,6},{8,9},{9,8},{10,11... | collective-permute-start | bytes 737288 | tf_op jit(solution)/shard_map/ppermute | solution.py:564
  13.9 0.9 prepare.1.w1_hbm
  15.0 7.3 %main.1 = (bf16[2304,128]{1,0:T(8,128)(2,1)S(1)}, bf16[2304,128]{1,0:T(8,128)(2,1)S(1)}, bf16[2592,128]{1,0:T(8,128)(2,1)S(1)}, bf16[4,96,1024]{2,1,0:T(8,128)(2,1)S(1)}) custom-call(f32[1]{0:T(128)} %bitcast.inner_ref, s32[1]{0:T(128)} %bitcast.1.core_ref.half_ref, bf16[5,96,256]{2,1,0:T(8,128)(2,1)S(1)} %collective-permute-done.far_hbm, ...), custom_call_target="tpu_custom_call" | custom-call | tf_op jit(solution)/shard_map/main/pallas_call | solution.py:432
  22.4 2.4 %collective-permute-start.2 = (bf16[2304,128]{1,0:T(8,128)(2,1)S(1)}, bf16[2304,128]{1,0:T(8,128)(2,1)S(1)}, u32[]{:S(2)}, u32[]{:S(2)}) collective-permute-start(bf16[2304,128]{1,0:T(8,128)(2,1)S(1)} %get-tuple-element.15), channel_id=1, source_target_pairs={{0,1},{1,0},{2,3},{3,2},{4,5},{5,4},{6,7},{7,6},{8,9},{9,8},{10,11... | collective-permute-start | bytes 1769480 | tf_op jit(solution)/shard_map/ppermute | solution.py:569
  24.8 1.6 %collective-permute-done.2.got_hbm = bf16[2304,128]{1,0:T(8,128)(2,1)S(1)} collective-permute-done((bf16[2304,128]{1,0:T(8,128)(2,1)S(1)}, bf16[2304,128]{1,0:T(8,128)(2,1)S(1)}, u32[]{:S(2)}, u32[]{:S(2)}) %collective-permute-start.2) | collective-permute-done | bytes 589856 | tf_op jit(solution)/shard_map/ppermute | solution.py:569
  26.4 0.5 add.12
  26.9 17.2 %all_to_all.15 = bf16[32,72,128]{2,1,0:T(8,128)(2,1)S(1)} all-to-all(bf16[32,72,128]{2,1,0:T(8,128)(2,1)S(1)} %bitcast.30), channel_id=1, replica_groups=mesh['xh'=2,'zh'=8,'zl'=2,'xl'=2,'y'=4,'core'=2] {'zl','y','xh','xl'}, dimensions={0} | all-to-all | bytes 1179648 | tf_op jit(solution)/shard_map/all_to_all | solution.py:570
  44.2 0.7 broadcast_in_dim.7
  44.9 13.9 %all-to-all-start.1 = ((bf16[8,72,128]{2,1,0:T(8,128)(2,1)}), bf16[8,72,128]{2,1,0:T(8,128)(2,1)S(1)}, u32[]{:S(2)}, u32[]{:S(2)}) async-start(bf16[8,72,128]{2,1,0:T(8,128)(2,1)} %broadcast_in_dim.7), calls=%async_computation.1 | async-start | bytes 294912 | tf_op jit(solution)/shard_map/all_to_all | solution.py:547
  58.8 0.3 reshape.61.fw_ref
  59.2 1.1 %copy-done.3 = bf16[2592,128]{1,0:T(8,128)(2,1)S(1)} copy-done((bf16[2592,128]{1,0:T(8,128)(2,1)S(1)}, bf16[2592,128]{1,0:T(8,128)(2,1)}, u32[]{:S(2)}) %copy-start.3) | copy-done | bytes 663576
  60.3 3.4 %tail.1 = (bf16[192,128]{1,0:T(8,128)(2,1)}, bf16[2,96,512]{2,1,0:T(8,128)(2,1)S(1)}) custom-call(bf16[72,128]{1,0:T(8,128)(2,1)S(1)} %reduce_sum.12.after_hbm, bf16[4,96,1024]{2,1,0:T(8,128)(2,1)S(1)} %get-tuple-element.16.g_hbm, bf16[2592,128]{1,0:T(8,128)(2,1)S(1)} %copy-done.3, bf16[2592,192]{1,0:T(8,128)(2,1)} %bitcast.33, ...), custom_call_target="tpu_custom_call" | custom-call | flops 1000000000 | bytes 4000000 | tf_op jit(solution)/shard_map/tail/pallas_call | solution.py:465
  63.9 0.5 zero.1
  65.0 7.6 %all-to-all-done.1 = bf16[8,72,128]{2,1,0:T(8,128)(2,1)S(1)} async-done(((bf16[8,72,128]{2,1,0:T(8,128)(2,1)}), bf16[8,72,128]{2,1,0:T(8,128)(2,1)S(1)}, u32[]{:S(2)}, u32[]{:S(2)}) %all-to-all-start.1) | async-done | bytes 147488 | tf_op jit(solution)/shard_map/all_to_all | solution.py:547
  72.7 13.7 %all_to_all.16 = bf16[32,72,128]{2,1,0:T(8,128)(2,1)S(1)} all-to-all(bf16[32,72,128]{2,1,0:T(8,128)(2,1)S(1)} %broadcast_in_dim.8), channel_id=1, replica_groups=mesh['xh'=2,'zh'=8,'zl'=2,'xl'=2,'y'=4,'core'=2] {'zl','y','xh','xl'}, dimensions={0} | all-to-all | bytes 1179648 | tf_op jit(solution)/shard_map/all_to_all | solution.py:547
  86.4 6.7 %collective-permute-start.3 = (bf16[2304,128]{1,0:T(8,128)(2,1)S(1)}, bf16[2304,128]{1,0:T(8,128)(2,1)S(1)}, u32[]{:S(2)}, u32[]{:S(2)}) collective-permute-start(bf16[2304,128]{1,0:T(8,128)(2,1)S(1)} %bitcast.31), channel_id=1, source_target_pairs={{0,1},{1,0},{2,3},{3,2},{4,5},{5,4},{6,7},{7,6},{8,9},{9,8},{10,11... | collective-permute-start | bytes 1769480 | tf_op jit(solution)/shard_map/ppermute | solution.py:578
  93.1 1.3 %finish.2 = (f32[2592,192]{1,0:T(8,128)}, f32[96,768]{1,0:T(8,128)S(1)}) custom-call(s32[1]{0:T(128)} %bitcast.1.core_ref.half_ref, bf16[2304,128]{1,0:T(8,128)(2,1)S(1)} %bitcast.32), custom_call_target="tpu_custom_call" | custom-call | tf_op jit(solution)/shard_map/finish/pallas_call | solution.py:505
  94.7 1.3 %finish.3 = (f32[2592,192]{1,0:T(8,128)}, f32[96,768]{1,0:T(8,128)S(1)}) custom-call(s32[1]{0:T(128)S(6)} %sub.3.half_ref, bf16[2304,128]{1,0:T(8,128)(2,1)S(1)} %collective-permute-done.3.rows_hbm, f32[2592,192]{1,0:T(8,128)} %get-tuple-element.20.refs_0_, f32[96,768]{1,0:T(8,128)S(1)} %get-tuple-element.21.refs_1_), custom_call_target="tpu_custom_call", output_to_operand_aliasing={{0}: (2, {}), {1}: (3, {})} | custom-call | tf_op jit(solution)/shard_map/finish/pallas_call | solution.py:505
  96.0 1.5 %reshape.65 = f32[4,24,24,27]{3,2,1,0:T(8,128)} reshape(f32[96,648]{1,0:T(8,128)S(1)} %bitcast.35) | data formatting | bytes 497664 | tf_op jit(solution)/shard_map/reshape | solution.py:582
  (20 shorter events, 1.2 us)
Async XLA Ops:
  0.6 14.4 %copy-start = (bf16[27,96,192]{2,1,0:T(8,128)(2,1)S(1)}, bf16[27,96,192]{2,1,0:T(8,128)(2,1)}, u32[]{:S(2)}) copy-start(bf16[27,96,192]{2,1,0:T(8,128)(2,1)} %param.6) | copy-start | bytes 2985988
  2.6 12.3 %collective-permute-start = (bf16[5,96,256]{2,1,0:T(8,128)(2,1)S(1)}, bf16[5,96,256]{2,1,0:T(8,128)(2,1)S(1)}, u32[]{:S(2)}, u32[]{:S(2)}) collective-permute-start(bf16[5,96,256]{2,1,0:T(8,128)(2,1)S(1)} %pad_maximum_fusion.own_hbm), channel_id=1, source_target_pairs={{1,2},{3,4},{5,6},{7,8},{9,10},{11,12},{13,14},{2,1},{4,3},{6,5},{... | collective-permute-start | bytes 737288 | tf_op jit(solution)/shard_map/ppermute | solution.py:556
  9.1 6.0 %collective-permute-start.1 = (bf16[5,96,256]{2,1,0:T(8,128)(2,1)S(1)}, bf16[5,96,256]{2,1,0:T(8,128)(2,1)S(1)}, u32[]{:S(2)}, u32[]{:S(2)}) collective-permute-start(bf16[5,96,256]{2,1,0:T(8,128)(2,1)S(1)} %again.1), channel_id=1, source_target_pairs={{0,1},{1,0},{2,3},{3,2},{4,5},{5,4},{6,7},{7,6},{8,9},{9,8},{10,11... | collective-permute-start | bytes 737288 | tf_op jit(solution)/shard_map/ppermute | solution.py:564
  22.3 4.6 %copy-start.2 = (bf16[2592,128]{1,0:T(8,128)(2,1)}, bf16[2592,128]{1,0:T(8,128)(2,1)S(1)}, u32[]{:S(2)}) copy-start(bf16[2592,128]{1,0:T(8,128)(2,1)S(1)} %get-tuple-element.17.wn_hbm) | copy-start | bytes 1990660
  22.4 36.5 %copy-start.4 = (bf16[27,4,24,24]{0,3,2,1:T(8,128)(2,1)S(1)}, bf16[27,4,24,24]{0,3,2,1:T(8,128)(2,1)}, u32[]{:S(2)}) copy-start(bf16[27,4,24,24]{0,3,2,1:T(8,128)(2,1)} %param.5) | copy-start | bytes 373252
  22.4 4.0 %collective-permute-start.2 = (bf16[2304,128]{1,0:T(8,128)(2,1)S(1)}, bf16[2304,128]{1,0:T(8,128)(2,1)S(1)}, u32[]{:S(2)}, u32[]{:S(2)}) collective-permute-start(bf16[2304,128]{1,0:T(8,128)(2,1)S(1)} %get-tuple-element.15), channel_id=1, source_target_pairs={{0,1},{1,0},{2,3},{3,2},{4,5},{5,4},{6,7},{7,6},{8,9},{9,8},{10,11... | collective-permute-start | bytes 1769480 | tf_op jit(solution)/shard_map/ppermute | solution.py:569
  44.9 27.7 %all-to-all-start.1 = ((bf16[8,72,128]{2,1,0:T(8,128)(2,1)}), bf16[8,72,128]{2,1,0:T(8,128)(2,1)S(1)}, u32[]{:S(2)}, u32[]{:S(2)}) async-start(bf16[8,72,128]{2,1,0:T(8,128)(2,1)} %broadcast_in_dim.7), calls=%async_computation.1 | async-start | bytes 294912 | tf_op jit(solution)/shard_map/all_to_all | solution.py:547
  59.2 1.1 %copy-start.3 = (bf16[2592,128]{1,0:T(8,128)(2,1)S(1)}, bf16[2592,128]{1,0:T(8,128)(2,1)}, u32[]{:S(2)}) copy-start(bf16[2592,128]{1,0:T(8,128)(2,1)} %copy-done.2) | copy-start | bytes 1990660
  63.9 32.2 %copy-start.1 = (bf16[2,96,2,256]{3,2,0,1:T(2,128)(2,1)}, bf16[2,96,2,256]{3,2,0,1:T(2,128)(2,1)S(1)}, u32[]{:S(2)}) copy-start(bf16[2,96,2,256]{3,2,0,1:T(2,128)(2,1)S(1)} %copy.22) | copy-start | bytes 589828
  86.4 8.3 %collective-permute-start.3 = (bf16[2304,128]{1,0:T(8,128)(2,1)S(1)}, bf16[2304,128]{1,0:T(8,128)(2,1)S(1)}, u32[]{:S(2)}, u32[]{:S(2)}) collective-permute-start(bf16[2304,128]{1,0:T(8,128)(2,1)S(1)} %bitcast.31), channel_id=1, source_target_pairs={{0,1},{1,0},{2,3},{3,2},{4,5},{5,4},{6,7},{7,6},{8,9},{9,8},{10,11... | collective-permute-start | bytes 1769480 | tf_op jit(solution)/shard_map/ppermute | solution.py:578
